TPU v7x, 32 devices: a whole 2x2x4 slice. The times are simulated.
32 devices in a mesh: expert: 4 (over z), dp: 4 (over x, core), tensor: 2 (over y).
Axes of the slice: x: 2, y: 2, z: 4, core: 2. Of those that a mesh axis runs over, the one named last changes fastest.
Arguments:
- tokens: bfloat16 [2, 512, 7168], P(None, ('expert', 'dp')), may hold values from -6 to 6
- cotangent: bfloat16 [2, 512, 7168], P(None, ('expert', 'dp')), may hold values from -0.625 to 0.625
- route_gate: bfloat16 [2, 512, 2], P(None, ('expert', 'dp')), may hold values from 0.19921875 to 1
- routes: int32 [2, 512, 2], P(None, ('expert', 'dp')), may hold values from 0 to 3, all different within a row; in each aligned block of 32 rows (0 to 31, 32 to 63, ..., all dimensions but the last counted through in order) at most 24 rows name the same one
- gate_weight: bfloat16 [4, 7168, 1024], P('expert', 'dp', 'tensor'), may hold values from -0.0625 to 0.0625
- up_weight: bfloat16 [4, 7168, 1024], P('expert', 'dp', 'tensor'), may hold values from -0.0625 to 0.0625
- down_weight: bfloat16 [4, 1024, 7168], P('expert', 'tensor', 'dp'), may hold values from -0.1875 to 0.1875
- dropped: int32 [4, 3], P('expert'), may hold values from 0 to 7, as said below
Outputs:
- saliency: float32 [2, 4, 1024], P(None, 'expert', 'tensor')
- compact_down: bfloat16 [4, 640, 7168], P('expert', 'tensor', 'dp')
Inputs may be any that keep to these rules, and one draw needn't show every extreme that they name: `routes`: each token names 2 different experts. Among the 32 tokens of one set on one index of expert and dp, no expert is named more than 24 times, a bound that some block reaches. `dropped`: each row lists 3 different block numbers.
All inputs are finite; a program needn't handle non-finite values.
Results may differ from a plain program's by a relative error of at most 0.001.
Values may be sent and summed in bfloat16 or wider, within the bound.
No kernel may reach another device: no remote copies, remote signals or barrier semaphores. Data moves between devices by JAX's collectives and lax.ppermute only.
A program may use at most 128 MiB of HBM per device.

v0:
```python
import jax
import jax.numpy as jnp
from jax import lax
from jax.sharding import PartitionSpec as P

BLOCK = 128
NBLK = 8
KEEP = 5


def neuron_terms(x_recv, grad_recv, gate_recv, gate_full, up_full, down_full):
    gate_act = jnp.einsum("pscd,df->pscf", x_recv, gate_full, preferred_element_type=jnp.float32)
    up_act = jnp.einsum("pscd,df->pscf", x_recv, up_full, preferred_element_type=jnp.float32)
    hidden = jax.nn.silu(gate_act) * up_act
    product = jnp.einsum("pscd,fd->pscf", grad_recv, down_full, preferred_element_type=jnp.float32)
    hidden_grad = gate_recv.astype(jnp.float32)[..., None] * product
    return jnp.sum(hidden * hidden_grad, axis=(0, 2))


def body(tokens, cotangent, route_gate, routes, gate_weight, up_weight, down_weight, dropped):
    experts = lax.axis_size("expert")
    tensor_count = lax.axis_size("tensor")
    tensor_pos = lax.axis_index("tensor")
    tok_rows = tokens.shape[1]
    top_count = routes.shape[2]
    capacity = min(tok_rows, max(2, 3 * tok_rows * top_count // (2 * experts)))
    expert_ids = jnp.arange(experts, dtype=jnp.int32)
    matched = routes[:, :, :, None] == expert_ids
    chosen = jnp.any(matched, axis=2).astype(jnp.float32)
    weight_sum = jnp.sum(
        jnp.where(matched, route_gate.astype(jnp.float32)[:, :, :, None], 0.0), axis=2
    )
    earlier = jnp.cumsum(chosen, axis=1) - chosen
    placing = chosen[..., None] * (earlier[..., None] == jnp.arange(capacity, dtype=jnp.float32))
    slot_gate = jnp.einsum("stec,ste->esc", placing, weight_sum, precision=lax.Precision.HIGHEST)
    gate_slots = slot_gate.astype(jnp.bfloat16)
    placing_half = placing.astype(jnp.bfloat16)
    gate_rows, up_rows = (
        lax.all_gather(gate_weight, "dp", axis=1, tiled=True),
        lax.all_gather(up_weight, "dp", axis=1, tiled=True),
    )
    down_cols = lax.all_gather(down_weight, "dp", axis=2, tiled=True)
    gate_full = gate_rows[0]
    up_full = up_rows[0]
    down_full = down_cols[0]
    x_slots = jnp.einsum(
        "stec,std->escd", placing_half, tokens, preferred_element_type=jnp.float32
    ).astype(jnp.bfloat16)
    grad_slots = jnp.einsum(
        "stec,std->escd", placing_half, cotangent, preferred_element_type=jnp.float32
    ).astype(jnp.bfloat16)
    partial_terms = neuron_terms(
        lax.all_to_all(x_slots, "expert", split_axis=0, concat_axis=0, tiled=True),
        lax.all_to_all(grad_slots, "expert", split_axis=0, concat_axis=0, tiled=True),
        lax.all_to_all(gate_slots, "expert", split_axis=0, concat_axis=0, tiled=True),
        gate_full,
        up_full,
        down_full,
    )
    totals = lax.psum(partial_terms, "dp")
    saliency = jnp.abs(totals)[:, None, :]
    blocks = jnp.arange(NBLK, dtype=jnp.int32)
    kept_flag = jnp.all(dropped[0][:, None] != blocks[None, :], axis=0)
    ranking = jnp.cumsum(kept_flag.astype(jnp.int32)) - 1
    rows_out = KEEP * BLOCK // tensor_count
    whole_rows = lax.all_gather(down_weight, "tensor", axis=1, tiled=True)[0]
    target_rows = tensor_pos * rows_out + jnp.arange(rows_out, dtype=jnp.int32)
    wanted_rank = target_rows // BLOCK
    chosen_block = kept_flag[None, :] & (ranking[None, :] == wanted_rank[:, None])
    source_block = jnp.sum(jnp.where(chosen_block, blocks[None, :], 0), axis=1)
    source_rows = source_block * BLOCK + target_rows % BLOCK
    compact_down = jnp.take(whole_rows, source_rows, axis=0)[None]
    return (saliency, compact_down)


def solution(mesh):
    return jax.shard_map(
        body,
        mesh=mesh,
        in_specs=(
            P(None, ("expert", "dp"), None),
            P(None, ("expert", "dp"), None),
            P(None, ("expert", "dp"), None),
            P(None, ("expert", "dp"), None),
            P("expert", "dp", "tensor"),
            P("expert", "dp", "tensor"),
            P("expert", "tensor", "dp"),
            P("expert", None),
        ),
        out_specs=(P(None, "expert", "tensor"), P("expert", "tensor", "dp")),
        check_vma=False,
    )
```

profile of v0, /device:TPU:0, one launch (start us, length us, event | category | flops | bytes accessed | tf_op | source)
XLA Modules:
  0.0 244.3 jit_solution(8573489387039866933)
XLA Ops:
  7.2 0.7 all-gather.11.cloned.1.call-update
  8.0 0.7 all-gather.5.cloned.1.call-update
  8.7 0.0 all-gather.7.cloned.1.call-start
  8.7 0.7 all-gather.7.cloned.1.call-update
  9.5 0.5 all-gather.9.cloned.1.call-update
  10.0 0.1 copy.28
  10.1 0.1 copy.30
  10.2 0.1 reduce_window_sum.18
  10.3 0.1 copy.29
  10.4 0.3 fusion.22
  10.7 0.6 convert_element_type.59
  11.3 6.3 %all-to-all-start.1 = ((bf16[4,2,24]{2,1,0:T(2,128)(2,1)}), bf16[4,2,24]{2,1,0:T(2,128)(2,1)S(1)}, u32[]{:S(2)}, u32[]{:S(2)}) async-start(bf16[4,2,24]{2,1,0:T(2,128)(2,1)} %convert_element_type.59), calls=%async_computation.1 | async-start | bytes 4096 | tf_op jit(solution)/shard_map/all_to_all | solution.py:55
  17.6 0.9 fusion
  18.5 1.8 copy.32
  20.3 2.8 %all-to-all-done.1 = bf16[4,2,24]{2,1,0:T(2,128)(2,1)S(1)} async-done(((bf16[4,2,24]{2,1,0:T(2,128)(2,1)}), bf16[4,2,24]{2,1,0:T(2,128)(2,1)S(1)}, u32[]{:S(2)}, u32[]{:S(2)}) %all-to-all-start.1) | async-done | bytes 416 | tf_op jit(solution)/shard_map/all_to_all | solution.py:55
  23.1 4.6 %all-to-all-start = ((bf16[4,2,24,7168]{3,2,1,0:T(8,128)(2,1)}), bf16[4,2,24,7168]{3,2,1,0:T(8,128)(2,1)}, u32[]{:S(2)}, u32[]{:S(2)}) async-start(bf16[4,2,24,7168]{3,2,1,0:T(8,128)(2,1)} %copy.32), calls=%async_computation | async-start | bytes 5505024 | tf_op jit(solution)/shard_map/all_to_all | solution.py:53
  27.7 0.1 fusion.33
  27.8 2.4 fusion.1
  30.2 58.7 %all-to-all-done = bf16[4,2,24,7168]{3,2,1,0:T(8,128)(2,1)} async-done(((bf16[4,2,24,7168]{3,2,1,0:T(8,128)(2,1)}), bf16[4,2,24,7168]{3,2,1,0:T(8,128)(2,1)}, u32[]{:S(2)}, u32[]{:S(2)}) %all-to-all-start) | async-done | bytes 2752544 | tf_op jit(solution)/shard_map/all_to_all | solution.py:53
  88.9 4.6 %all-to-all-start.2 = ((bf16[4,2,24,7168]{3,2,1,0:T(8,128)(2,1)}), bf16[4,2,24,7168]{3,2,1,0:T(8,128)(2,1)}, u32[]{:S(2)}, u32[]{:S(2)}) async-start(bf16[4,2,24,7168]{3,2,1,0:T(8,128)(2,1)} %fusion.1), calls=%async_computation.2 | async-start | bytes 5505024 | tf_op jit(solution)/shard_map/all_to_all | solution.py:54
  93.5 0.2 reduce-window.8
  93.7 0.1 select_reduce_fusion
  93.9 6.5 %gather_fusion = bf16[320,1792]{1,0:T(8,128)(2,1)S(1)} fusion(bf16[1024,1792]{1,0:T(8,128)(2,1)} %bitcast.55, s32[1024]{0:T(1024)S(1)} %pad_clamp_fusion), kind=kCustom, calls=%fused_computation | custom fusion | bytes 2295040 | tf_op jit(solution)/shard_map/jit(_take)/gather | solution.py:72
  100.4 1.2 bitcast_select_fusion
  101.6 15.5 %all-gather.5.cloned.1.call-done = bf16[1,7168,512]{2,1,0:T(8,128)(2,1)} async-done(((bf16[1,1792,512]{2,1,0:T(8,128)(2,1)}), bf16[1,7168,512]{2,1,0:T(8,128)(2,1)}) %all-gather.5.cloned.1.call-update) | async-done | bytes 7340048 | tf_op jit(solution)/shard_map/all_gather | solution.py:39
  117.1 5.5 %fusion.6 = f32[4,2,24,512]{3,2,1,0:T(8,128)S(1)} fusion(bf16[4,2,24,7168]{3,2,1,0:T(8,128)(2,1)} %all-to-all-done, bf16[1,7168,512]{2,1,0:T(8,128)(2,1)} %all-gather.5.cloned.1.call-done), kind=kOutput, calls=%fused_computation.9 | convolution fusion | flops 1409286144 | bytes 10485760 | tf_op jit(solution)/shard_map/pscd,df->pscf/dot_general | solution.py:12
  122.6 48.4 %all-gather.7.cloned.1.call-done = bf16[1,7168,512]{2,1,0:T(8,128)(2,1)} async-done(((bf16[1,1792,512]{2,1,0:T(8,128)(2,1)}), bf16[1,7168,512]{2,1,0:T(8,128)(2,1)}) %all-gather.7.cloned.1.call-update) | async-done | bytes 7340048 | tf_op jit(solution)/shard_map/all_gather | solution.py:40
  171.0 5.5 %fusion.8 = f32[4,2,24,512]{3,2,1,0:T(8,128)S(1)} fusion(bf16[4,2,24,7168]{3,2,1,0:T(8,128)(2,1)} %all-to-all-done, bf16[1,7168,512]{2,1,0:T(8,128)(2,1)} %all-gather.7.cloned.1.call-done, f32[4,2,24,512]{3,2,1,0:T(8,128)S(1)} %fusion.6), kind=kOutput, calls=%fused_computation.11 | convolution fusion | flops 1409777664 | bytes 10878976 | tf_op jit(solution)/shard_map/pscd,df->pscf/dot_general | solution.py:13
  176.5 48.2 %all-gather.9.cloned.1.call-done = bf16[1,512,7168]{2,1,0:T(8,128)(2,1)} async-done(((bf16[1,512,1792]{2,1,0:T(8,128)(2,1)}), bf16[1,512,7168]{2,1,0:T(8,128)(2,1)}) %all-gather.9.cloned.1.call-update) | async-done | bytes 7340048 | tf_op jit(solution)/shard_map/all_gather | solution.py:42
  224.8 6.5 %fusion.17 = f32[2,512]{1,0:T(2,128)S(1)} fusion(f32[4,2,24,512]{3,2,1,0:T(8,128)S(1)} %fusion.8, bf16[4,2,24,7168]{3,2,1,0:T(8,128)(2,1)} %all-to-all-done.2, bf16[1,512,7168]{2,1,0:T(8,128)(2,1)} %all-gather.9.cloned.1.call-done, f32[4,2,24]{2,1,0:T(2,128)S(1)} %convert_element_type.60), kind=kOutput, calls=%fused_computation.14 | convolution fusion | flops 1409580032 | bytes 10490624 | tf_op jit(solution)/shard_map/pscd,fd->pscf/dot_general | solution.py:15
  231.3 5.9 %psum.7 = f32[2,512]{1,0:T(2,128)S(1)} all-reduce(f32[2,512]{1,0:T(2,128)S(1)} %fusion.17), channel_id=1, replica_groups=mesh['expert'=4,'dp'=4,'tensor'=2] {'dp'}, use_global_device_ids=true, to_apply=%region_4.5 | all-reduce | flops 1024 | bytes 8192 | tf_op jit(solution)/shard_map/psum | solution.py:60
  237.2 0.6 broadcast_in_dim.52
  (29 shorter events, 0.3 us)
Async XLA Ops:
  7.2 10.4 %copy-start = (bf16[2,32,7168]{2,1,0:T(8,128)(2,1)S(1)}, bf16[2,32,7168]{2,1,0:T(8,128)(2,1)}, u32[]{:S(2)}) copy-start(bf16[2,32,7168]{2,1,0:T(8,128)(2,1)} %param.8) | copy-start | bytes 2752516
  7.2 86.7 %all-gather.11.cloned.1.call-start = ((), (), s32[]{:S(2)}) async-start(), calls=%async_computation.6 | async-start | bytes 5505024 | tf_op jit(solution)/shard_map/all_gather | solution.py:66
  7.9 2.1 copy-start.2
  7.9 2.5 %copy-start.3 = (bf16[2,32,2]{1,2,0:T(2,128)(2,1)S(1)}, bf16[2,32,2]{1,2,0:T(2,128)(2,1)}, u32[]{:S(2)}) copy-start(bf16[2,32,2]{1,2,0:T(2,128)(2,1)} %param.10) | copy-start | bytes 772
  7.9 109.1 %all-gather.5.cloned.1.call-start = ((), (), s32[]{:S(2)}) async-start(), calls=%async_computation.3 | async-start | bytes 9175040 | tf_op jit(solution)/shard_map/all_gather | solution.py:39
  8.7 162.3 %all-gather.7.cloned.1.call-start = ((), (), s32[]{:S(2)}) async-start(), calls=%async_computation.4 | async-start | bytes 9175040 | tf_op jit(solution)/shard_map/all_gather | solution.py:40
  9.4 215.4 %all-gather.9.cloned.1.call-start = ((), (), s32[]{:S(2)}) async-start(), calls=%async_computation.5 | async-start | bytes 9175040 | tf_op jit(solution)/shard_map/all_gather | solution.py:42
  11.3 11.8 %all-to-all-start.1 = ((bf16[4,2,24]{2,1,0:T(2,128)(2,1)}), bf16[4,2,24]{2,1,0:T(2,128)(2,1)S(1)}, u32[]{:S(2)}, u32[]{:S(2)}) async-start(bf16[4,2,24]{2,1,0:T(2,128)(2,1)} %convert_element_type.59), calls=%async_computation.1 | async-start | bytes 4096 | tf_op jit(solution)/shard_map/all_to_all | solution.py:55
  20.3 7.4 %copy-start.4 = (s32[1,3]{1,0:T(1,128)S(1)}, s32[1,3]{1,0:T(1,128)}, u32[]{:S(2)}) copy-start(s32[1,3]{1,0:T(1,128)} %param.15) | copy-start | bytes 40
  20.3 7.5 %copy-start.1 = (bf16[2,32,7168]{2,1,0:T(8,128)(2,1)S(1)}, bf16[2,32,7168]{2,1,0:T(8,128)(2,1)}, u32[]{:S(2)}) copy-start(bf16[2,32,7168]{2,1,0:T(8,128)(2,1)} %param.9) | copy-start | bytes 2752516
  23.1 65.9 %all-to-all-start = ((bf16[4,2,24,7168]{3,2,1,0:T(8,128)(2,1)}), bf16[4,2,24,7168]{3,2,1,0:T(8,128)(2,1)}, u32[]{:S(2)}, u32[]{:S(2)}) async-start(bf16[4,2,24,7168]{3,2,1,0:T(8,128)(2,1)} %copy.32), calls=%async_computation | async-start | bytes 5505024 | tf_op jit(solution)/shard_map/all_to_all | solution.py:53
  88.9 87.6 %all-to-all-start.2 = ((bf16[4,2,24,7168]{3,2,1,0:T(8,128)(2,1)}), bf16[4,2,24,7168]{3,2,1,0:T(8,128)(2,1)}, u32[]{:S(2)}, u32[]{:S(2)}) async-start(bf16[4,2,24,7168]{3,2,1,0:T(8,128)(2,1)} %fusion.1), calls=%async_computation.2 | async-start | bytes 5505024 | tf_op jit(solution)/shard_map/all_to_all | solution.py:54
Sparse Core Ops, SparseCore 0:
  9.6 53.5 all-gather.10
  64.7 52.3 all-gather.4
  118.6 52.3 all-gather.6
  172.4 52.3 all-gather.8
where the time goes:
time: 245 us; the launch traced here: 244 us
  waiting for transfers between devices  176 us (72%)
  matrix products  21 us (9%)
  starting transfers between devices  15.7 us (6%)
  between operations  13.9 us (6%)
  local copies, waits for them, and re-layouts  9.24 us (4%)
  blocking collectives  5.92 us (2%)
    all_to_all x1, waiting for transfers between devices, body(): lax.all_to_all(x_slots, 'expert', split_axis=0, concat_axis=0, tiled=True)  58.7 us
    all_gather x1, waiting for transfers between devices, body(): lax.all_gather(up_weight, 'dp', axis=1, tiled=True)  48.4 us
    all_gather x1, waiting for transfers between devices, body(): down_cols = lax.all_gather(down_weight, 'dp', axis=2, tiled=True)  48.2 us
    all_gather x1, waiting for transfers between devices, body(): lax.all_gather(gate_weight, 'dp', axis=1, tiled=True)  15.5 us
    gather x1, local copies, waits for them, and re-layouts, body(): compact_down = jnp.take(whole_rows, source_rows, axis=0)[None]  6.49 us
    dot_general x1, matrix products, neuron_terms(): jnp.einsum('pscd,fd->pscf', grad_recv, down_full, preferred_element_type=...  6.46 us
    all_to_all x1, starting transfers between devices, body(): lax.all_to_all(gate_slots, 'expert', split_axis=0, concat_axis=0, tiled=T...  6.32 us
    psum x1, blocking collectives, body(): totals = lax.psum(partial_terms, 'dp')  5.92 us
  transfers between devices with their start and end apart: 7, of which 5 were waited for; matrix products, arithmetic and copies ran while one was open for 10% of the time, Pallas kernels for 0%

commit v1 on v0

--- a/solution.py
+++ b/solution.py
@@ -1,11 +1,22 @@
+import functools
+
 import jax
 import jax.numpy as jnp
 from jax import lax
+from jax.experimental import pallas as pl
+from jax.experimental.pallas import tpu as pltpu
 from jax.sharding import PartitionSpec as P
 
 BLOCK = 128
 NBLK = 8
 KEEP = 5
+LANES = 128
+HALF = 64
+MIB = 1 << 20
+
+
+def capacity_of(tok_rows, top_count, experts):
+    return min(tok_rows, max(2, 3 * tok_rows * top_count // (2 * experts)))
 
 
 def neuron_terms(x_recv, grad_recv, gate_recv, gate_full, up_full, down_full):
@@ -17,13 +28,21 @@
     return jnp.sum(hidden * hidden_grad, axis=(0, 2))
 
 
-def body(tokens, cotangent, route_gate, routes, gate_weight, up_weight, down_weight, dropped):
+def kept_blocks(dropped):
+    blocks = jnp.arange(NBLK, dtype=jnp.int32)
+    kept_flag = jnp.all(dropped[0][:, None] != blocks[None, :], axis=0)
+    ranking = jnp.cumsum(kept_flag.astype(jnp.int32)) - 1
+    ranks = jnp.arange(KEEP, dtype=jnp.int32)
+    chosen = kept_flag[None, :] & (ranking[None, :] == ranks[:, None])
+    return jnp.sum(jnp.where(chosen, blocks[None, :], 0), axis=1), kept_flag
+
+
+def general_body(tokens, cotangent, route_gate, routes, gate_weight, up_weight, down_weight, dropped):
     experts = lax.axis_size("expert")
     tensor_count = lax.axis_size("tensor")
     tensor_pos = lax.axis_index("tensor")
     tok_rows = tokens.shape[1]
-    top_count = routes.shape[2]
-    capacity = min(tok_rows, max(2, 3 * tok_rows * top_count // (2 * experts)))
+    capacity = capacity_of(tok_rows, routes.shape[2], experts)
     expert_ids = jnp.arange(experts, dtype=jnp.int32)
     matched = routes[:, :, :, None] == expert_ids
     chosen = jnp.any(matched, axis=2).astype(jnp.float32)
@@ -35,14 +54,9 @@
     slot_gate = jnp.einsum("stec,ste->esc", placing, weight_sum, precision=lax.Precision.HIGHEST)
     gate_slots = slot_gate.astype(jnp.bfloat16)
     placing_half = placing.astype(jnp.bfloat16)
-    gate_rows, up_rows = (
-        lax.all_gather(gate_weight, "dp", axis=1, tiled=True),
-        lax.all_gather(up_weight, "dp", axis=1, tiled=True),
-    )
-    down_cols = lax.all_gather(down_weight, "dp", axis=2, tiled=True)
-    gate_full = gate_rows[0]
-    up_full = up_rows[0]
-    down_full = down_cols[0]
+    gate_full = lax.all_gather(gate_weight, "dp", axis=1, tiled=True)[0]
+    up_full = lax.all_gather(up_weight, "dp", axis=1, tiled=True)[0]
+    down_full = lax.all_gather(down_weight, "dp", axis=2, tiled=True)[0]
     x_slots = jnp.einsum(
         "stec,std->escd", placing_half, tokens, preferred_element_type=jnp.float32
     ).astype(jnp.bfloat16)
@@ -59,23 +73,310 @@
     )
     totals = lax.psum(partial_terms, "dp")
     saliency = jnp.abs(totals)[:, None, :]
-    blocks = jnp.arange(NBLK, dtype=jnp.int32)
-    kept_flag = jnp.all(dropped[0][:, None] != blocks[None, :], axis=0)
-    ranking = jnp.cumsum(kept_flag.astype(jnp.int32)) - 1
     rows_out = KEEP * BLOCK // tensor_count
     whole_rows = lax.all_gather(down_weight, "tensor", axis=1, tiled=True)[0]
     target_rows = tensor_pos * rows_out + jnp.arange(rows_out, dtype=jnp.int32)
-    wanted_rank = target_rows // BLOCK
-    chosen_block = kept_flag[None, :] & (ranking[None, :] == wanted_rank[:, None])
-    source_block = jnp.sum(jnp.where(chosen_block, blocks[None, :], 0), axis=1)
-    source_rows = source_block * BLOCK + target_rows % BLOCK
+    source_rows = kept_blocks(dropped)[0][target_rows // BLOCK] * BLOCK + target_rows % BLOCK
     compact_down = jnp.take(whole_rows, source_rows, axis=0)[None]
     return (saliency, compact_down)
 
 
+def full(shape):
+    return pl.BlockSpec(shape, lambda *_: (0,) * len(shape))
+
+
+def pack_kernel(experts, cap, info, routes, gates, tokens, cotangent, *outs):
+    messages, near, local, slot_gates = outs[:-3], outs[-3], outs[-2], outs[-1]
+    z, x, core, y = info[0], info[1], info[2], info[3]
+    rows = tokens.shape[1]
+    chunk = near.shape[1] // 2
+    lane = lax.broadcasted_iota(jnp.int32, (rows, LANES), 1)
+    ahead = jnp.zeros_like(lane)
+    for k in range(1, experts):
+        ahead = ahead + (lane >= k * cap).astype(jnp.int32)
+    slot = lane - ahead * cap
+    expert = z + ahead
+    expert = jnp.where(expert >= experts, expert - experts, expert)
+    expert = jnp.where(lane < experts * cap, expert, -1)
+    lower = (
+        lax.broadcasted_iota(jnp.int32, (rows, rows), 1)
+        < lax.broadcasted_iota(jnp.int32, (rows, rows), 0)
+    ).astype(jnp.bfloat16)
+    sets, placings, gate_rows = (y, 1 - y), [], []
+    for s in sets:
+        route, weight = routes[s], gates[s].astype(jnp.float32)
+        match = jnp.zeros(lane.shape, jnp.float32)
+        named = jnp.zeros(lane.shape, jnp.float32)
+        for k in range(route.shape[1]):
+            same = route[:, k : k + 1] == expert
+            match = match + jnp.where(same, 1.0, 0.0)
+            named = named + jnp.where(same, weight[:, k : k + 1], 0.0)
+        rank = jnp.dot(lower, match.astype(jnp.bfloat16), preferred_element_type=jnp.float32)
+        placing = jnp.where(rank == slot.astype(jnp.float32), match, 0.0)
+        gate_rows.append(jnp.sum(placing * named, axis=0, keepdims=True))
+        placings.append(placing.astype(jnp.bfloat16))
+    slot_gates[...] = jnp.concatenate(
+        gate_rows + [jnp.zeros((slot_gates.shape[0] - 2, LANES), jnp.float32)], axis=0
+    )
+    for dx in range(2):
+        half = x if dx == 0 else 1 - x
+        for h in range(2):
+            column = pl.multiple_of((2 * half + (core if h == 0 else 1 - core)) * chunk, LANES)
+            here = slice(h * chunk, (h + 1) * chunk)
+            found = [
+                lax.dot_general(
+                    placing,
+                    source[s, :, pl.ds(column, chunk)],
+                    (((0,), (0,)), ((), ())),
+                    preferred_element_type=jnp.float32,
+                )
+                for s, placing in zip(sets, placings)
+                for source in (tokens, cotangent)
+            ]
+            for k in range(1, experts):
+                span = slice(k * cap, (k + 1) * cap)
+                messages[2 * (k - 1) + dx][:, here] = jnp.concatenate(
+                    [found[0][span], found[1][span]], axis=0
+                ).astype(jnp.bfloat16)
+            (local if dx == 0 else near)[:, here] = jnp.concatenate(
+                [part[:cap] for part in found], axis=0
+            ).astype(jnp.bfloat16)
+
+
+def pack(info, routes, gates, tokens, cotangent, experts, cap, width):
+    one = jax.ShapeDtypeStruct((2 * cap, width), jnp.bfloat16)
+    two = jax.ShapeDtypeStruct((4 * cap, width), jnp.bfloat16)
+    outs = [one] * (2 * (experts - 1)) + [two, two, jax.ShapeDtypeStruct((8, LANES), jnp.float32)]
+    return pl.pallas_call(
+        functools.partial(pack_kernel, experts, cap),
+        out_shape=outs,
+        in_specs=[pl.BlockSpec(memory_space=pltpu.SMEM)] + [pl.BlockSpec(memory_space=pltpu.VMEM)] * 4,
+        out_specs=[pl.BlockSpec(memory_space=pltpu.VMEM)] * len(outs),
+        compiler_params=pltpu.CompilerParams(vmem_limit_bytes=32 * MIB),
+        cost_estimate=pl.CostEstimate(flops=10**9, bytes_accessed=6 * 10**6, transcendentals=0),
+        name="pack_rows",
+    )(info, routes, gates, tokens, cotangent)
+
+
+def products_kernel(cap, counts, steps, *refs):
+    n = sum(counts)
+    parts, weights = refs[:n], refs[n : n + 6]
+    outs, acc = refs[n + 6 : -1], refs[-1]
+    j = pl.program_id(0)
+    rows = jnp.concatenate([part[...] for part in parts], axis=0)
+    inner = acc.shape[1] // 3
+
+    def add(gate, up, down):
+        terms = (
+            jnp.dot(rows, gate[...], preferred_element_type=jnp.float32),
+            jnp.dot(rows, up[...], preferred_element_type=jnp.float32),
+            lax.dot_general(
+                rows, down[...], (((1,), (1,)), ((), ())), preferred_element_type=jnp.float32
+            ),
+        )
+        for i, term in enumerate(terms):
+            where = slice(i * inner, (i + 1) * inner)
+
+            @pl.when(j == 0)
+            def _():
+                acc[:, where] = term
+
+            @pl.when(j > 0)
+            def _():
+                acc[:, where] += term
+
+    @pl.when(j < steps)
+    def _():
+        add(*weights[:3])
+
+    @pl.when(j >= steps)
+    def _():
+        add(*weights[3:])
+
+    @pl.when(j == 2 * steps - 1)
+    def _():
+        row = 0
+        for out in outs:
+            for b in range(out.shape[0] // cap):
+                where = slice(b * cap, (b + 1) * cap)
+                out[where, : 2 * inner] = acc[row : row + cap, : 2 * inner]
+                out[where, 2 * inner :] = acc[row + cap : row + 2 * cap, 2 * inner :]
+                row += 2 * cap
+
+
+def products(groups, own, other, cap, steps=2):
+    parts = [part for group in groups for part in group]
+    counts = [len(group) for group in groups]
+    chunk, inner = own[0].shape
+    tile = chunk // steps
+    sizes = [sum(part.shape[0] for part in group) // 2 for group in groups]
+    total = sum(part.shape[0] for part in parts)
+
+    def first(j):
+        return jnp.minimum(j, steps - 1)
+
+    def second(j):
+        return jnp.maximum(j - steps, 0)
+
+    def weight_specs(at):
+        return [
+            pl.BlockSpec((tile, inner), lambda j: (at(j), 0)),
+            pl.BlockSpec((tile, inner), lambda j: (at(j), 0)),
+            pl.BlockSpec((inner, tile), lambda j: (0, at(j))),
+        ]
+
+    return pl.pallas_call(
+        functools.partial(products_kernel, cap, counts, steps),
+        grid=(2 * steps,),
+        in_specs=[pl.BlockSpec((part.shape[0], tile), lambda j: (0, j)) for part in parts]
+        + weight_specs(first)
+        + weight_specs(second),
+        out_specs=[full((size, 3 * inner)) for size in sizes],
+        out_shape=[jax.ShapeDtypeStruct((size, 3 * inner), jnp.float32) for size in sizes],
+        scratch_shapes=[pltpu.VMEM((total, 3 * inner), jnp.float32)],
+        compiler_params=pltpu.CompilerParams(
+            vmem_limit_bytes=40 * MIB, dimension_semantics=("arbitrary",)
+        ),
+        cost_estimate=pl.CostEstimate(
+            flops=2 * total * 6 * chunk * inner, bytes_accessed=12 * chunk * inner, transcendentals=0
+        ),
+        name="partial_products",
+    )(*parts, *own, *other)
+
+
+def neuron_sums(cap, mine, came, gates):
+    total = mine + came
+    inner = total.shape[1] // 3
+    gate, up, product = total[:, :inner], total[:, inner : 2 * inner], total[:, 2 * inner :]
+    terms = jax.nn.silu(gate) * up * (gates[:, None] * product)
+    return jnp.sum(terms.reshape(2, -1, inner), axis=1)
+
+
+def compact_kernel(near_at, far_at, flags, near, far, out):
+    j = pl.program_id(0)
+
+    @pl.when(flags[j] == 0)
+    def _():
+        out[...] = near[...]
+
+    @pl.when(flags[j] != 0)
+    def _():
+        out[...] = far[...]
+
+
+def paired_body(tokens, cotangent, route_gate, routes, gate_weight, up_weight, down_weight, dropped):
+    experts = lax.axis_size("expert")
+    groups = lax.axis_size("dp")
+    z, dp, y = lax.axis_index("expert"), lax.axis_index("dp"), lax.axis_index("tensor")
+    x, core = dp // 2, dp % 2
+    cap = capacity_of(tokens.shape[1], routes.shape[2], experts)
+    chunk, inner = gate_weight.shape[1], gate_weight.shape[2]
+
+    def over_core(value):
+        return lax.ppermute(value, "dp", [(d, d ^ 1) for d in range(groups)])
+
+    def over_x(value):
+        return lax.ppermute(value, "dp", [(d, d ^ 2) for d in range(groups)])
+
+    def over_tensor(value):
+        return lax.ppermute(value, "tensor", [(0, 1), (1, 0)])
+
+    def ahead(value, k, dx):
+        return lax.ppermute(
+            value,
+            ("expert", "dp"),
+            [
+                (e * groups + d, (e + k) % experts * groups + (d ^ (2 * dx)))
+                for e in range(experts)
+                for d in range(groups)
+            ],
+        )
+
+    info = jnp.stack([z, x, core, y]).astype(jnp.int32)
+    *messages, near, local, slot_gates = pack(
+        info, routes, route_gate, tokens, cotangent, experts, cap, 2 * chunk
+    )
+    own = (gate_weight[0], up_weight[0], down_weight[0])
+    order = [(1, 0), (1, 1), (3, 1), (3, 0), (2, 1), (2, 0)]
+    window = 2
+    came, passed = {}, {}
+    came_near = None
+    for i, (k, dx) in enumerate(order):
+        message = messages[2 * (k - 1) + dx]
+        if i >= window:
+            message, came[order[i - window]] = lax.optimization_barrier(
+                (message, came[order[i - window]])
+            )
+        came[k, dx] = ahead(message, k, dx)
+        if i == 1:
+            came_near = over_x(near)
+    for at in order:
+        passed[at] = over_tensor(came[at])
+    other = tuple(over_core(weight) for weight in own)
+
+    all_gates = lax.all_gather(slot_gates[:2, : experts * cap], "expert", axis=0, tiled=False)
+    all_gates = all_gates.reshape(experts, 2, experts, cap)
+
+    def gates_of(k):
+        source = lax.rem(z + experts - k, experts)
+        return lax.dynamic_index_in_dim(all_gates, source, 0, False)[:, k].reshape(2 * cap)
+
+    sums = jnp.zeros((2, inner), jnp.float32)
+    kept, sent = products([[local], [near_part for near_part in (came_near,)]], own, other, cap)
+    sums = sums + neuron_sums(cap, kept, over_x(sent), gates_of(0))
+    for k in (1, 3, 2):
+        kept, sent = products(
+            [[came[k, 0], passed[k, 0]], [came[k, 1], passed[k, 1]]], own, other, cap
+        )
+        sums = sums + neuron_sums(cap, kept, over_x(sent), gates_of(k))
+    totals = jnp.abs(lax.psum(sums, "dp"))
+    saliency = jnp.where(y == 0, totals, totals[::-1])[:, None, :]
+
+    block_of, kept_flag = kept_blocks(dropped)
+    pieces_out = KEEP * BLOCK // HALF // 2
+    own_blocks = NBLK // 2
+    low_pieces = 2 * jnp.sum(kept_flag[:own_blocks].astype(jnp.int32))
+    down = own[2].reshape(2 * own_blocks, HALF, chunk)
+    most = 3
+
+    def place_of(piece):
+        piece = jnp.clip(piece, 0, 2 * KEEP - 1)
+        return (block_of[piece // 2] - own_blocks * y) * 2 + piece % 2
+
+    first_sent = jnp.where(y == 0, pieces_out, low_pieces)
+    send_at = jnp.clip(place_of(first_sent + jnp.arange(most, dtype=jnp.int32)), 0, 2 * own_blocks - 1)
+    down_sent = jnp.concatenate(
+        [lax.dynamic_slice_in_dim(down, send_at[i], 1, 0) for i in range(most)], axis=0
+    )
+    down_came = over_tensor(down_sent)
+    target = y * pieces_out + jnp.arange(pieces_out, dtype=jnp.int32)
+    far = jnp.where(y == 0, target >= low_pieces, target < low_pieces)
+    first_came = jnp.where(y == 0, low_pieces, pieces_out)
+    near_at = jnp.clip(place_of(target), 0, 2 * own_blocks - 1)
+    far_at = jnp.clip(target - first_came, 0, most - 1)
+    compact_down = pl.pallas_call(
+        compact_kernel,
+        grid_spec=pltpu.PrefetchScalarGridSpec(
+            num_scalar_prefetch=3,
+            grid=(pieces_out,),
+            in_specs=[
+                pl.BlockSpec((1, HALF, chunk), lambda j, n, f, w: (n[j], 0, 0)),
+                pl.BlockSpec((1, HALF, chunk), lambda j, n, f, w: (f[j], 0, 0)),
+            ],
+            out_specs=pl.BlockSpec((1, HALF, chunk), lambda j, n, f, w: (j, 0, 0)),
+        ),
+        out_shape=jax.ShapeDtypeStruct((pieces_out, HALF, chunk), jnp.bfloat16),
+        cost_estimate=pl.CostEstimate(flops=0, bytes_accessed=4 * 10**6, transcendentals=0),
+        name="kept_rows",
+    )(near_at, far_at, far.astype(jnp.int32), down, down_came)
+    return saliency, compact_down.reshape(1, pieces_out * HALF, chunk)
+
+
 def solution(mesh):
+    sizes = mesh.shape
+    paired = sizes["tensor"] == 2 and sizes["dp"] == 4 and sizes["expert"] == 4
     return jax.shard_map(
-        body,
+        paired_body if paired else general_body,
         mesh=mesh,
         in_specs=(
             P(None, ("expert", "dp"), None),

time: 245 us -> 157 us (0.64)
  waiting for transfers between devices: 176 us -> 21.4 us
  Pallas kernels: 0 us -> 37.9 us
  matrix products: 21 us -> 0 us
  local copies, waits for them, and re-layouts: 9.24 us -> 30.2 us
  starting transfers between devices: 15.7 us -> 29.1 us
  blocking collectives: 5.92 us -> 17.6 us
  other arithmetic: 2.32 us -> 12.4 us
  between operations: 13.9 us -> 7.12 us
    all_gather x4 -> x0, waiting for transfers between devices: 112 us -> none  [the longest x1 48.4 us: body(): lax.all_gather(up_weight, 'dp', axis=1, tiled=True)]
    all_to_all x3 -> x0, waiting for transfers between devices: 61.5 us -> none  [the longest x1 58.7 us: body(): lax.all_to_all(x_slots, 'expert', split_axis=0, concat_axis=0, tiled=True)]
    pallas_call x0 -> x6, Pallas kernels: none -> 37.9 us  [the longest x4 29.8 us: products(): pl.pallas_call(functools.partial(products_kernel, cap, counts, steps), gr...]
    ppermute x0 -> x21, starting transfers between devices: none -> 29.1 us  [the longest x6 16.2 us: ahead(): lax.ppermute(value, ('expert', 'dp'), [(e * groups + d, (e + k) % experts...]
    ppermute x0 -> x21, waiting for transfers between devices: none -> 21.4 us  [the longest x6 16.8 us: ahead(): lax.ppermute(value, ('expert', 'dp'), [(e * groups + d, (e + k) % experts...]
    dot_general x6 -> x0, matrix products: 21 us -> none  [the longest x1 6.46 us: neuron_terms(): jnp.einsum('pscd,fd->pscf', grad_recv, down_full, preferred_element_type=...]
    all_to_all x3 -> x0, starting transfers between devices: 15.5 us -> none  [the longest x1 6.32 us: body(): lax.all_to_all(gate_slots, 'expert', split_axis=0, concat_axis=0, tiled=T...]
    all_gather x0 -> x1, blocking collectives: none -> 11.9 us  [paired_body(): lax.all_gather(slot_gates[:2, :experts * cap], 'expert', axis=0, tiled=Fa...]
  transfers between devices with their start and end apart: 7 -> 21, of which waited for: 5 -> 5; matrix products, arithmetic and copies ran while one was open for 10% -> 20% of each run, Pallas kernels for 0% -> 22%
where the time goes in v1:
time: 157 us; the launch traced here: 156 us
  Pallas kernels  37.9 us (24%)
  local copies, waits for them, and re-layouts  30.2 us (19%)
  starting transfers between devices  29.1 us (19%)
  waiting for transfers between devices  21.4 us (14%)
  blocking collectives  17.6 us (11%)
  other arithmetic  12.4 us (8%)
  between operations  7.12 us (5%)
    pallas_call x4, Pallas kernels, products(): pl.pallas_call(functools.partial(products_kernel, cap, counts, steps), gr...  29.8 us
    ppermute x6, waiting for transfers between devices, ahead(): lax.ppermute(value, ('expert', 'dp'), [(e * groups + d, (e + k) % experts...  16.8 us
    ppermute x6, starting transfers between devices, ahead(): lax.ppermute(value, ('expert', 'dp'), [(e * groups + d, (e + k) % experts...  16.2 us
    all_gather x1, blocking collectives, paired_body(): lax.all_gather(slot_gates[:2, :experts * cap], 'expert', axis=0, tiled=Fa...  11.9 us
    unnamed x37, local copies, waits for them, and re-layouts  10.8 us
    ppermute x7, starting transfers between devices, over_tensor(): return lax.ppermute(value, 'tensor', [(0, 1), (1, 0)])  7.86 us
    psum x1, blocking collectives, paired_body(): totals = jnp.abs(lax.psum(sums, 'dp'))  5.67 us
    mul x4, local copies, waits for them, and re-layouts, neuron_sums(): terms = jax.nn.silu(gate) * up * (gates[:, None] * product)  5.22 us
  transfers between devices with their start and end apart: 21, of which 5 were waited for; matrix products, arithmetic and copies ran while one was open for 20% of the time, Pallas kernels for 22%

profile of v1, /device:TPU:0, one launch (start us, length us, event | category | flops | bytes accessed | tf_op | source)
XLA Modules:
  0.0 155.8 jit_solution(9100788241826113784)
XLA Ops:
  5.9 3.4 %pack_rows.1 = (bf16[48,3584]{1,0:T(8,128)(2,1)S(1)}, bf16[48,3584]{1,0:T(8,128)(2,1)}, bf16[48,3584]{1,0:T(8,128)(2,1)S(1)}, bf16[48,3584]{1,0:T(8,128)(2,1)}, ...) custom-call(s32[4]{0:T(128)S(1)} %get-tuple-element.63.info, ...), custom_call_target="tpu_custom_call" | custom-call | flops 1000000000 | bytes 6000000 | tf_op jit(solution)/shard_map/pack_rows/pallas_call | solution.py:150
  13.0 3.0 %collective-permute-start.5 = (bf16[48,3584]{1,0:T(8,128)(2,1)S(1)}, bf16[48,3584]{1,0:T(8,128)(2,1)S(1)}, u32[]{:S(2)}, u32[]{:S(2)}) collective-permute-start(bf16[48,3584]{1,0:T(8,128)(2,1)S(1)} %get-tuple-element.33), channel_id=1, source_target_pairs={{0,8},{2,10},{4,12},{6,14},{8,16},{10,18},{12,20},{14,22},{16,24},... | collective-permute-start | bytes 1032200 | tf_op jit(solution)/shard_map/ppermute | solution.py:285
  16.1 2.5 %collective-permute-start.7 = (bf16[48,3584]{1,0:T(8,128)(2,1)}, bf16[48,3584]{1,0:T(8,128)(2,1)S(1)}, u32[]{:S(2)}, u32[]{:S(2)}) collective-permute-start(bf16[48,3584]{1,0:T(8,128)(2,1)} %get-tuple-element.36), channel_id=1, source_target_pairs={{0,12},{2,14},{4,8},{6,10},{8,20},{10,22},{12,16},{14,18},{16,28},... | collective-permute-start | bytes 1032200 | tf_op jit(solution)/shard_map/ppermute | solution.py:285
  20.8 1.3 reduce-window.8
  22.7 1.4 select_reduce_fusion
  24.1 2.9 %collective-permute-done.5.refs_0_ = bf16[48,3584]{1,0:T(8,128)(2,1)S(1)} collective-permute-done((bf16[48,3584]{1,0:T(8,128)(2,1)S(1)}, bf16[48,3584]{1,0:T(8,128)(2,1)S(1)}, u32[]{:S(2)}, u32[]{:S(2)}) %collective-permute-start.5) | collective-permute-done | bytes 344096 | tf_op jit(solution)/shard_map/ppermute | solution.py:285
  27.0 1.8 %collective-permute-start.6 = (bf16[48,3584]{1,0:T(8,128)(2,1)S(1)}, bf16[48,3584]{1,0:T(8,128)(2,1)S(1)}, u32[]{:S(2)}, u32[]{:S(2)}) collective-permute-start(bf16[48,3584]{1,0:T(8,128)(2,1)S(1)} %collective-permute-done.5.refs_0_), channel_id=1, source_target_pairs={{0,1},{1,0},{2,3},{3,2},{4,5},{5,4},{6,7},{7,6},{8,9},{9,8},{10,11... | collective-permute-start | bytes 1032200 | tf_op jit(solution)/shard_map/ppermute | solution.py:282
  29.3 2.0 %gather_fusion.1 = s32[3]{0:T(128)} fusion(s32[5]{0:T(128)} %select_reduce_fusion, s32[1024]{0:T(1024)} %pad_clamp_fusion), kind=kCustom, calls=%fused_computation.1 | custom fusion | bytes 36 | tf_op jit(solution)/shard_map/gather | solution.py:344
  32.0 2.4 %collective-permute-done.7.refs_2_ = bf16[48,3584]{1,0:T(8,128)(2,1)S(1)} collective-permute-done((bf16[48,3584]{1,0:T(8,128)(2,1)}, bf16[48,3584]{1,0:T(8,128)(2,1)S(1)}, u32[]{:S(2)}, u32[]{:S(2)}) %collective-permute-start.7) | collective-permute-done | bytes 344096 | tf_op jit(solution)/shard_map/ppermute | solution.py:285
  34.4 1.5 collective-permute-start.8
  42.3 1.8 %collective-permute-start.12 = (bf16[48,3584]{1,0:T(8,128)(2,1)}, bf16[48,3584]{1,0:T(8,128)(2,1)}, u32[]{:S(2)}, u32[]{:S(2)}) collective-permute-start(bf16[48,3584]{1,0:T(8,128)(2,1)} %copy-done.11), channel_id=1, source_target_pairs={{0,28},{2,30},{4,24},{6,26},{8,4},{10,6},{12,0},{14,2},{16,12},{18... | collective-permute-start | bytes 1032200 | tf_op jit(solution)/shard_map/ppermute | solution.py:285
  46.7 7.9 %collective-permute-done.12.refs_2_ = bf16[48,3584]{1,0:T(8,128)(2,1)} collective-permute-done((bf16[48,3584]{1,0:T(8,128)(2,1)}, bf16[48,3584]{1,0:T(8,128)(2,1)}, u32[]{:S(2)}, u32[]{:S(2)}) %collective-permute-start.12) | collective-permute-done | bytes 344096 | tf_op jit(solution)/shard_map/ppermute | solution.py:285
  55.0 3.6 %collective-permute-done.10.refs_0_ = bf16[48,3584]{1,0:T(8,128)(2,1)} collective-permute-done((bf16[48,3584]{1,0:T(8,128)(2,1)}, bf16[48,3584]{1,0:T(8,128)(2,1)}, u32[]{:S(2)}, u32[]{:S(2)}) %collective-permute-start.10) | collective-permute-done | bytes 344096 | tf_op jit(solution)/shard_map/ppermute | solution.py:285
  58.7 1.6 %collective-permute-start.17 = (bf16[48,3584]{1,0:T(8,128)(2,1)}, bf16[48,3584]{1,0:T(8,128)(2,1)}, u32[]{:S(2)}, u32[]{:S(2)}) collective-permute-start(bf16[48,3584]{1,0:T(8,128)(2,1)} %get-tuple-element.49), channel_id=1, source_target_pairs={{0,20},{2,22},{4,16},{6,18},{8,28},{10,30},{12,24},{14,26},{16,4},... | collective-permute-start | bytes 1032200 | tf_op jit(solution)/shard_map/ppermute | solution.py:285
  60.3 1.3 slice_bitcast_fusion
  61.6 11.9 %all-gather.1 = f32[4,2,96]{2,1,0:T(2,128)} all-gather(f32[1,2,96]{2,1,0:T(2,128)} %slice_bitcast_fusion), channel_id=2, replica_groups=mesh['expert'=4,'dp'=4,'tensor'=2] {'expert'}, dimensions={0}, use_global_device_ids=true | all-gather | bytes 3840 | tf_op jit(solution)/shard_map/all_gather | solution.py:317
  73.5 1.4 reshape.188
  74.8 1.3 constant_dynamic-slice_fusion.5
  77.0 6.8 %collective-permute-start.15 = (bf16[48,3584]{1,0:T(8,128)(2,1)}, bf16[48,3584]{1,0:T(8,128)(2,1)}, u32[]{:S(2)}, u32[]{:S(2)}) collective-permute-start(bf16[48,3584]{1,0:T(8,128)(2,1)} %copy-done.9), channel_id=1, source_target_pairs={{0,16},{2,18},{4,20},{6,22},{8,24},{10,26},{12,28},{14,30},{16,0},... | collective-permute-start | bytes 1032200 | tf_op jit(solution)/shard_map/ppermute | solution.py:285
  85.6 1.3 mul.101
  88.1 1.3 mul.95
  93.2 1.3 mul.113
  94.5 1.9 %gather_fusion = s32[5]{0:T(128)} fusion(s32[5]{0:T(128)} %select_reduce_fusion, s32[1024]{0:T(1024)} %pad_clamp_fusion.1), kind=kCustom, calls=%fused_computation | custom fusion | bytes 60 | tf_op jit(solution)/shard_map/gather | solution.py:344
  98.3 4.7 %kept_rows.1 = bf16[5,64,1792]{2,1,0:T(8,128)(2,1)} custom-call(s32[5]{0:T(128)} %fusion.14.near_at, s32[5]{0:T(128)} %subtract_clamp_fusion.far_at, s32[5]{0:T(128)} %select_convert_fusion.flags, bf16[8,64,1792]{2,1,0:T(8,128)(2,1)} %bitcast.20.near, bf16[3,64,1792]{2,1,0:T(8,128)(2,1)} %collective-permute-done.20.far), custom_call_target="tpu_custom_call" | custom-call | bytes 4000000 | tf_op jit(solution)/shard_map/kept_rows/pallas_call | solution.py:357
  109.0 7.4 %partial_products.5 = (f32[48,1536]{1,0:T(8,128)S(1)}, f32[48,1536]{1,0:T(8,128)S(1)}) custom-call(bf16[48,3584]{1,0:T(8,128)(2,1)S(1)} %collective-permute-done.5.refs_0_, bf16[48,3584]{1,0:T(8,128)(2,1)S(1)} %copy-done.4, bf16[48,3584]{1,0:T(8,128)(2,1)S(1)} %copy-done.2, bf16[48,3584]{1,0:T(8,128)(2,1)} %collective-permute-done.8.refs_3_, ...), custom_call_target="tpu_custom_call" | custom-call | flops 2113929216 | bytes 11010048 | tf_op jit(solution)/shard_map/partial_products/pallas_call | solution.py:228
  116.4 1.4 collective-permute-start.9
  117.8 7.4 %partial_products.4 = (f32[48,1536]{1,0:T(8,128)S(1)}, f32[48,1536]{1,0:T(8,128)S(1)}) custom-call(bf16[96,3584]{1,0:T(8,128)(2,1)S(1)} %get-tuple-element.27.refs_0_, bf16[96,3584]{1,0:T(8,128)(2,1)S(1)} %collective-permute-done.refs_1_, bf16[1792,512]{1,0:T(8,128)(2,1)S(1)} %bitcast.49, bf16[1792,512]{1,0:T(8,128)(2,1)} %bitcast.5.refs_3_.refs_5_, ...), custom_call_target="tpu_custom_call" | custom-call | flops 2113929216 | bytes 11010048 | tf_op jit(solution)/shard_map/partial_products/pallas_call | solution.py:228
  126.0 7.5 %partial_products.6 = (f32[48,1536]{1,0:T(8,128)S(1)}, f32[48,1536]{1,0:T(8,128)S(1)}) custom-call(bf16[48,3584]{1,0:T(8,128)(2,1)} %collective-permute-done.10.refs_0_, bf16[48,3584]{1,0:T(8,128)(2,1)S(1)} %collective-permute-done.11.refs_1_, bf16[48,3584]{1,0:T(8,128)(2,1)} %collective-permute-done.12.refs_2_, ...), custom_call_target="tpu_custom_call" | custom-call | flops 2113929216 | bytes 11010048 | tf_op jit(solution)/shard_map/partial_products/pallas_call | solution.py:228
  133.5 1.4 collective-permute-start.14
  134.9 7.5 %partial_products.7 = (f32[48,1536]{1,0:T(8,128)S(1)}, f32[48,1536]{1,0:T(8,128)S(1)}) custom-call(bf16[48,3584]{1,0:T(8,128)(2,1)} %collective-permute-done.15.refs_0_, bf16[48,3584]{1,0:T(8,128)(2,1)S(1)} %collective-permute-done.16.refs_1_, bf16[48,3584]{1,0:T(8,128)(2,1)} %collective-permute-done.17.refs_2_, ...), custom_call_target="tpu_custom_call" | custom-call | flops 2113929216 | bytes 11010048 | tf_op jit(solution)/shard_map/partial_products/pallas_call | solution.py:228
  144.7 4.5 %collective-permute-done.19 = f32[48,1536]{1,0:T(8,128)S(1)} collective-permute-done((f32[48,1536]{1,0:T(8,128)S(1)}, f32[48,1536]{1,0:T(8,128)S(1)}, u32[]{:S(2)}, u32[]{:S(2)}) %collective-permute-start.19) | collective-permute-done | bytes 294944 | tf_op jit(solution)/shard_map/ppermute | solution.py:279
  149.4 5.7 %psum.7 = f32[2,512]{1,0:T(2,128)S(1)} all-reduce(f32[2,512]{1,0:T(2,128)S(1)} %add_add_fusion), channel_id=1, replica_groups=mesh['expert'=4,'dp'=4,'tensor'=2] {'dp'}, use_global_device_ids=true, to_apply=%region_4.5 | all-reduce | flops 1024 | bytes 8192 | tf_op jit(solution)/shard_map/psum | solution.py:332
  (105 shorter events, 35.5 us)
Async XLA Ops:
  1.4 2.2 %copy-start.16 = (pred[8]{0:T(512)(128)(4,1)}, pred[8]{0:T(512)(128)(4,1)S(1)}, u32[]{:S(2)}) copy-start(pred[8]{0:T(512)(128)(4,1)S(1)} %fusion.5) | copy-start | bytes 28
  3.6 1.2 copy-start.6
  4.8 1.2 copy-start.7
  5.9 12.6 %copy-start = (bf16[1,1792,512]{2,1,0:T(8,128)(2,1)S(1)}, bf16[1,1792,512]{2,1,0:T(8,128)(2,1)}, u32[]{:S(2)}) copy-start(bf16[1,1792,512]{2,1,0:T(8,128)(2,1)} %param.12) | copy-start | bytes 5505028
  13.0 13.9 %collective-permute-start.5 = (bf16[48,3584]{1,0:T(8,128)(2,1)S(1)}, bf16[48,3584]{1,0:T(8,128)(2,1)S(1)}, u32[]{:S(2)}, u32[]{:S(2)}) collective-permute-start(bf16[48,3584]{1,0:T(8,128)(2,1)S(1)} %get-tuple-element.33), channel_id=1, source_target_pairs={{0,8},{2,10},{4,12},{6,14},{8,16},{10,18},{12,20},{14,22},{16,24},... | collective-permute-start | bytes 1032200 | tf_op jit(solution)/shard_map/ppermute | solution.py:285
  16.1 18.4 %collective-permute-start.7 = (bf16[48,3584]{1,0:T(8,128)(2,1)}, bf16[48,3584]{1,0:T(8,128)(2,1)S(1)}, u32[]{:S(2)}, u32[]{:S(2)}) collective-permute-start(bf16[48,3584]{1,0:T(8,128)(2,1)} %get-tuple-element.36), channel_id=1, source_target_pairs={{0,12},{2,14},{4,8},{6,10},{8,20},{10,22},{12,16},{14,18},{16,28},... | collective-permute-start | bytes 1032200 | tf_op jit(solution)/shard_map/ppermute | solution.py:285
  18.6 85.5 %collective-permute-start.1 = (bf16[1792,512]{1,0:T(8,128)(2,1)S(1)}, bf16[1792,512]{1,0:T(8,128)(2,1)}, u32[]{:S(2)}, u32[]{:S(2)}) collective-permute-start(bf16[1792,512]{1,0:T(8,128)(2,1)S(1)} %bitcast.47), channel_id=1, source_target_pairs={{0,2},{2,0},{4,6},{6,4},{1,3},{3,1},{5,7},{7,5},{8,10},{10,8},{12,... | collective-permute-start | bytes 5505032 | tf_op jit(solution)/shard_map/ppermute | solution.py:276
  18.6 86.4 %collective-permute-start.2 = (bf16[1792,512]{1,0:T(8,128)(2,1)}, bf16[1792,512]{1,0:T(8,128)(2,1)}, u32[]{:S(2)}, u32[]{:S(2)}) collective-permute-start(bf16[1792,512]{1,0:T(8,128)(2,1)} %bitcast.5.refs_3_.refs_5_), channel_id=1, source_target_pairs={{0,2},{2,0},{4,6},{6,4},{1,3},{3,1},{5,7},{7,5},{8,10},{10,8},{12,... | collective-permute-start | bytes 5505032 | tf_op jit(solution)/shard_map/ppermute | solution.py:276
  19.1 87.1 %collective-permute-start.3 = (bf16[512,1792]{1,0:T(8,128)(2,1)}, bf16[512,1792]{1,0:T(8,128)(2,1)}, u32[]{:S(2)}, u32[]{:S(2)}) collective-permute-start(bf16[512,1792]{1,0:T(8,128)(2,1)} %bitcast.6.refs_4_.refs_6_), channel_id=1, source_target_pairs={{0,2},{2,0},{4,6},{6,4},{1,3},{3,1},{5,7},{7,5},{8,10},{10,8},{12,... | collective-permute-start | bytes 5505032 | tf_op jit(solution)/shard_map/ppermute | solution.py:276
  27.0 15.3 %collective-permute-start.6 = (bf16[48,3584]{1,0:T(8,128)(2,1)S(1)}, bf16[48,3584]{1,0:T(8,128)(2,1)S(1)}, u32[]{:S(2)}, u32[]{:S(2)}) collective-permute-start(bf16[48,3584]{1,0:T(8,128)(2,1)S(1)} %collective-permute-done.5.refs_0_), channel_id=1, source_target_pairs={{0,1},{1,0},{2,3},{3,2},{4,5},{5,4},{6,7},{7,6},{8,9},{9,8},{10,11... | collective-permute-start | bytes 1032200 | tf_op jit(solution)/shard_map/ppermute | solution.py:282
  34.4 41.7 %copy-start.1 = (bf16[48,3584]{1,0:T(8,128)(2,1)}, bf16[48,3584]{1,0:T(8,128)(2,1)S(1)}, u32[]{:S(2)}) copy-start(bf16[48,3584]{1,0:T(8,128)(2,1)S(1)} %collective-permute-done.7.refs_2_) | copy-start | bytes 1032196
  34.4 10.8 %collective-permute-start.8 = (bf16[48,3584]{1,0:T(8,128)(2,1)S(1)}, bf16[48,3584]{1,0:T(8,128)(2,1)}, u32[]{:S(2)}, u32[]{:S(2)}) collective-permute-start(bf16[48,3584]{1,0:T(8,128)(2,1)S(1)} %collective-permute-done.7.refs_2_), channel_id=1, source_target_pairs={{0,1},{1,0},{2,3},{3,2},{4,5},{5,4},{6,7},{7,6},{8,9},{9,8},{10,11... | collective-permute-start | bytes 1032200 | tf_op jit(solution)/shard_map/ppermute | solution.py:282
  42.2 33.9 %copy-start.3 = (bf16[48,3584]{1,0:T(8,128)(2,1)}, bf16[48,3584]{1,0:T(8,128)(2,1)S(1)}, u32[]{:S(2)}) copy-start(bf16[48,3584]{1,0:T(8,128)(2,1)S(1)} %collective-permute-done.6.refs_1_) | copy-start | bytes 1032196
  42.3 12.3 %collective-permute-start.12 = (bf16[48,3584]{1,0:T(8,128)(2,1)}, bf16[48,3584]{1,0:T(8,128)(2,1)}, u32[]{:S(2)}, u32[]{:S(2)}) collective-permute-start(bf16[48,3584]{1,0:T(8,128)(2,1)} %copy-done.11), channel_id=1, source_target_pairs={{0,28},{2,30},{4,24},{6,26},{8,4},{10,6},{12,0},{14,2},{16,12},{18... | collective-permute-start | bytes 1032200 | tf_op jit(solution)/shard_map/ppermute | solution.py:285
  45.2 13.4 %collective-permute-start.10 = (bf16[48,3584]{1,0:T(8,128)(2,1)}, bf16[48,3584]{1,0:T(8,128)(2,1)}, u32[]{:S(2)}, u32[]{:S(2)}) collective-permute-start(bf16[48,3584]{1,0:T(8,128)(2,1)} %copy-done.10), channel_id=1, source_target_pairs={{0,24},{2,26},{4,28},{6,30},{8,0},{10,2},{12,4},{14,6},{16,8},{18,... | collective-permute-start | bytes 1032200 | tf_op jit(solution)/shard_map/ppermute | solution.py:285
  54.5 21.6 %collective-permute-start.20 = (bf16[3,64,1792]{2,1,0:T(8,128)(2,1)}, bf16[3,64,1792]{2,1,0:T(8,128)(2,1)}, u32[]{:S(2)}, u32[]{:S(2)}) collective-permute-start(bf16[3,64,1792]{2,1,0:T(8,128)(2,1)} %pad_maximum_fusion), channel_id=1, source_target_pairs={{0,1},{1,0},{2,3},{3,2},{4,5},{5,4},{6,7},{7,6},{8,9},{9,8},{10,11... | collective-permute-start | bytes 2064392 | tf_op jit(solution)/shard_map/ppermute | solution.py:282
  58.7 18.4 %collective-permute-start.17 = (bf16[48,3584]{1,0:T(8,128)(2,1)}, bf16[48,3584]{1,0:T(8,128)(2,1)}, u32[]{:S(2)}, u32[]{:S(2)}) collective-permute-start(bf16[48,3584]{1,0:T(8,128)(2,1)} %get-tuple-element.49), channel_id=1, source_target_pairs={{0,20},{2,22},{4,16},{6,18},{8,28},{10,30},{12,24},{14,26},{16,4},... | collective-permute-start | bytes 1032200 | tf_op jit(solution)/shard_map/ppermute | solution.py:285
  76.2 40.2 %collective-permute-start = (bf16[96,3584]{1,0:T(8,128)(2,1)}, bf16[96,3584]{1,0:T(8,128)(2,1)S(1)}, u32[]{:S(2)}, u32[]{:S(2)}) collective-permute-start(bf16[96,3584]{1,0:T(8,128)(2,1)} %copy-done.8), channel_id=1, source_target_pairs={{0,4},{2,6},{4,0},{6,2},{1,5},{3,7},{5,1},{7,3},{8,12},{10,14},{12... | collective-permute-start | bytes 2064392 | tf_op jit(solution)/shard_map/ppermute | solution.py:279
  77.0 25.9 %collective-permute-start.15 = (bf16[48,3584]{1,0:T(8,128)(2,1)}, bf16[48,3584]{1,0:T(8,128)(2,1)}, u32[]{:S(2)}, u32[]{:S(2)}) collective-permute-start(bf16[48,3584]{1,0:T(8,128)(2,1)} %copy-done.9), channel_id=1, source_target_pairs={{0,16},{2,18},{4,20},{6,22},{8,24},{10,26},{12,28},{14,30},{16,0},... | collective-permute-start | bytes 1032200 | tf_op jit(solution)/shard_map/ppermute | solution.py:285
  103.0 22.2 %collective-permute-start.13 = (bf16[48,3584]{1,0:T(8,128)(2,1)}, bf16[48,3584]{1,0:T(8,128)(2,1)S(1)}, u32[]{:S(2)}, u32[]{:S(2)}) collective-permute-start(bf16[48,3584]{1,0:T(8,128)(2,1)} %collective-permute-done.12.refs_2_), channel_id=1, source_target_pairs={{0,1},{1,0},{2,3},{3,2},{4,5},{5,4},{6,7},{7,6},{8,9},{9,8},{10,11... | collective-permute-start | bytes 1032200 | tf_op jit(solution)/shard_map/ppermute | solution.py:282
  104.1 21.9 %collective-permute-start.11 = (bf16[48,3584]{1,0:T(8,128)(2,1)}, bf16[48,3584]{1,0:T(8,128)(2,1)S(1)}, u32[]{:S(2)}, u32[]{:S(2)}) collective-permute-start(bf16[48,3584]{1,0:T(8,128)(2,1)} %collective-permute-done.10.refs_0_), channel_id=1, source_target_pairs={{0,1},{1,0},{2,3},{3,2},{4,5},{5,4},{6,7},{7,6},{8,9},{9,8},{10,11... | collective-permute-start | bytes 1032200 | tf_op jit(solution)/shard_map/ppermute | solution.py:282
  105.0 29.9 %collective-permute-start.18 = (bf16[48,3584]{1,0:T(8,128)(2,1)}, bf16[48,3584]{1,0:T(8,128)(2,1)S(1)}, u32[]{:S(2)}, u32[]{:S(2)}) collective-permute-start(bf16[48,3584]{1,0:T(8,128)(2,1)} %collective-permute-done.17.refs_2_), channel_id=1, source_target_pairs={{0,1},{1,0},{2,3},{3,2},{4,5},{5,4},{6,7},{7,6},{8,9},{9,8},{10,11... | collective-permute-start | bytes 1032200 | tf_op jit(solution)/shard_map/ppermute | solution.py:282
  106.1 28.7 %collective-permute-start.16 = (bf16[48,3584]{1,0:T(8,128)(2,1)}, bf16[48,3584]{1,0:T(8,128)(2,1)S(1)}, u32[]{:S(2)}, u32[]{:S(2)}) collective-permute-start(bf16[48,3584]{1,0:T(8,128)(2,1)} %collective-permute-done.15.refs_0_), channel_id=1, source_target_pairs={{0,1},{1,0},{2,3},{3,2},{4,5},{5,4},{6,7},{7,6},{8,9},{9,8},{10,11... | collective-permute-start | bytes 1032200 | tf_op jit(solution)/shard_map/ppermute | solution.py:282
  107.0 1.0 copy-start.2
  116.4 26.8 %collective-permute-start.9 = (f32[48,1536]{1,0:T(8,128)S(1)}, f32[48,1536]{1,0:T(8,128)S(1)}, u32[]{:S(2)}, u32[]{:S(2)}) collective-permute-start(f32[48,1536]{1,0:T(8,128)S(1)} %get-tuple-element.39), channel_id=1, source_target_pairs={{0,4},{2,6},{4,0},{6,2},{1,5},{3,7},{5,1},{7,3},{8,12},{10,14},{12... | collective-permute-start | bytes 884744 | tf_op jit(solution)/shard_map/ppermute | solution.py:279
  125.2 18.1 %collective-permute-start.4 = (f32[48,1536]{1,0:T(8,128)S(1)}, f32[48,1536]{1,0:T(8,128)S(1)}, u32[]{:S(2)}, u32[]{:S(2)}) collective-permute-start(f32[48,1536]{1,0:T(8,128)S(1)} %get-tuple-element.30), channel_id=1, source_target_pairs={{0,4},{2,6},{4,0},{6,2},{1,5},{3,7},{5,1},{7,3},{8,12},{10,14},{12... | collective-permute-start | bytes 884744 | tf_op jit(solution)/shard_map/ppermute | solution.py:279
  133.5 9.7 %copy-start.15 = (f32[48]{0:T(128)S(1)}, f32[48]{0:T(128)}, u32[]{:S(2)}) copy-start(f32[48]{0:T(128)} %mul.101) | copy-start | bytes 580
  133.5 10.0 %collective-permute-start.14 = (f32[48,1536]{1,0:T(8,128)S(1)}, f32[48,1536]{1,0:T(8,128)}, u32[]{:S(2)}, u32[]{:S(2)}) collective-permute-start(f32[48,1536]{1,0:T(8,128)S(1)} %get-tuple-element.47), channel_id=1, source_target_pairs={{0,4},{2,6},{4,0},{6,2},{1,5},{3,7},{5,1},{7,3},{8,12},{10,14},{12... | collective-permute-start | bytes 884744 | tf_op jit(solution)/shard_map/ppermute | solution.py:279
  142.4 1.0 copy-start.14
  142.4 2.1 %copy-start.13 = (f32[48]{0:T(128)S(1)}, f32[48]{0:T(128)}, u32[]{:S(2)}) copy-start(f32[48]{0:T(128)} %mul.107) | copy-start | bytes 580
  142.4 6.8 %collective-permute-start.19 = (f32[48,1536]{1,0:T(8,128)S(1)}, f32[48,1536]{1,0:T(8,128)S(1)}, u32[]{:S(2)}, u32[]{:S(2)}) collective-permute-start(f32[48,1536]{1,0:T(8,128)S(1)} %get-tuple-element.51), channel_id=1, source_target_pairs={{0,4},{2,6},{4,0},{6,2},{1,5},{3,7},{5,1},{7,3},{8,12},{10,14},{12... | collective-permute-start | bytes 884744 | tf_op jit(solution)/shard_map/ppermute | solution.py:279
  143.3 5.9 %copy-start.12 = (f32[48]{0:T(128)S(1)}, f32[48]{0:T(128)}, u32[]{:S(2)}) copy-start(f32[48]{0:T(128)} %mul.113) | copy-start | bytes 580
  (6 other events, 4.6 us)

commit v2 on v0

--- a/solution.py
+++ b/solution.py
@@ -1,11 +1,23 @@
+import functools
+
 import jax
 import jax.numpy as jnp
 from jax import lax
+from jax.experimental import pallas as pl
+from jax.experimental.pallas import tpu as pltpu
 from jax.sharding import PartitionSpec as P
 
 BLOCK = 128
 NBLK = 8
 KEEP = 5
+LANES = 128
+HALF = 64
+MIB = 1 << 20
+SMALL = pl.CostEstimate(flops=0, bytes_accessed=0, transcendentals=0)
+
+
+def capacity_of(tok_rows, top_count, experts):
+    return min(tok_rows, max(2, 3 * tok_rows * top_count // (2 * experts)))
 
 
 def neuron_terms(x_recv, grad_recv, gate_recv, gate_full, up_full, down_full):
@@ -17,13 +29,21 @@
     return jnp.sum(hidden * hidden_grad, axis=(0, 2))
 
 
-def body(tokens, cotangent, route_gate, routes, gate_weight, up_weight, down_weight, dropped):
+def kept_blocks(dropped):
+    blocks = jnp.arange(NBLK, dtype=jnp.int32)
+    kept_flag = jnp.all(dropped[0][:, None] != blocks[None, :], axis=0)
+    ranking = jnp.cumsum(kept_flag.astype(jnp.int32)) - 1
+    ranks = jnp.arange(KEEP, dtype=jnp.int32)
+    chosen = kept_flag[None, :] & (ranking[None, :] == ranks[:, None])
+    return jnp.sum(jnp.where(chosen, blocks[None, :], 0), axis=1), kept_flag
+
+
+def general_body(tokens, cotangent, route_gate, routes, gate_weight, up_weight, down_weight, dropped):
     experts = lax.axis_size("expert")
     tensor_count = lax.axis_size("tensor")
     tensor_pos = lax.axis_index("tensor")
     tok_rows = tokens.shape[1]
-    top_count = routes.shape[2]
-    capacity = min(tok_rows, max(2, 3 * tok_rows * top_count // (2 * experts)))
+    capacity = capacity_of(tok_rows, routes.shape[2], experts)
     expert_ids = jnp.arange(experts, dtype=jnp.int32)
     matched = routes[:, :, :, None] == expert_ids
     chosen = jnp.any(matched, axis=2).astype(jnp.float32)
@@ -35,14 +55,9 @@
     slot_gate = jnp.einsum("stec,ste->esc", placing, weight_sum, precision=lax.Precision.HIGHEST)
     gate_slots = slot_gate.astype(jnp.bfloat16)
     placing_half = placing.astype(jnp.bfloat16)
-    gate_rows, up_rows = (
-        lax.all_gather(gate_weight, "dp", axis=1, tiled=True),
-        lax.all_gather(up_weight, "dp", axis=1, tiled=True),
-    )
-    down_cols = lax.all_gather(down_weight, "dp", axis=2, tiled=True)
-    gate_full = gate_rows[0]
-    up_full = up_rows[0]
-    down_full = down_cols[0]
+    gate_full = lax.all_gather(gate_weight, "dp", axis=1, tiled=True)[0]
+    up_full = lax.all_gather(up_weight, "dp", axis=1, tiled=True)[0]
+    down_full = lax.all_gather(down_weight, "dp", axis=2, tiled=True)[0]
     x_slots = jnp.einsum(
         "stec,std->escd", placing_half, tokens, preferred_element_type=jnp.float32
     ).astype(jnp.bfloat16)
@@ -59,23 +74,406 @@
     )
     totals = lax.psum(partial_terms, "dp")
     saliency = jnp.abs(totals)[:, None, :]
-    blocks = jnp.arange(NBLK, dtype=jnp.int32)
-    kept_flag = jnp.all(dropped[0][:, None] != blocks[None, :], axis=0)
-    ranking = jnp.cumsum(kept_flag.astype(jnp.int32)) - 1
     rows_out = KEEP * BLOCK // tensor_count
     whole_rows = lax.all_gather(down_weight, "tensor", axis=1, tiled=True)[0]
     target_rows = tensor_pos * rows_out + jnp.arange(rows_out, dtype=jnp.int32)
-    wanted_rank = target_rows // BLOCK
-    chosen_block = kept_flag[None, :] & (ranking[None, :] == wanted_rank[:, None])
-    source_block = jnp.sum(jnp.where(chosen_block, blocks[None, :], 0), axis=1)
-    source_rows = source_block * BLOCK + target_rows % BLOCK
+    source_rows = kept_blocks(dropped)[0][target_rows // BLOCK] * BLOCK + target_rows % BLOCK
     compact_down = jnp.take(whole_rows, source_rows, axis=0)[None]
     return (saliency, compact_down)
 
 
+VMEM = pl.BlockSpec(memory_space=pltpu.VMEM)
+HBM = pl.BlockSpec(memory_space=pltpu.HBM)
+SMEM = pl.BlockSpec(memory_space=pltpu.SMEM)
+
+
+def place():
+    dp = lax.axis_index("dp")
+    return lax.axis_index("expert"), dp // 2, lax.rem(dp, 2), lax.axis_index("tensor")
+
+
+def pack_kernel(experts, cap, routes, gates, tokens, cotangent, *refs):
+    outs, buffers, sems = refs[:-2], refs[-2], refs[-1]
+    messages, near, local = outs[:-2], outs[-2], outs[-1]
+    z, x, core, y = place()
+    rows = tokens.shape[1]
+    chunk = near.shape[1] // 2
+    steps = [(dx, h) for dx in (1, 0) for h in (0, 1)]
+    copies = []
+    for i, (dx, h) in enumerate(steps):
+        half = x if dx == 0 else 1 - x
+        column = pl.multiple_of((2 * half + (core if h == 0 else 1 - core)) * chunk, LANES)
+        for j, source in enumerate((tokens, cotangent)):
+            copy = pltpu.make_async_copy(
+                source.at[:, :, pl.ds(column, chunk)], buffers.at[i, j], sems.at[i, j]
+            )
+            copy.start()
+            copies.append(copy)
+    count = experts * cap
+    line = lax.broadcasted_iota(jnp.int32, (count, rows), 0)
+    ahead = jnp.zeros_like(line)
+    for k in range(1, experts):
+        ahead = ahead + (line >= k * cap).astype(jnp.int32)
+    slot = (line - ahead * cap).astype(jnp.float32)
+    expert = z + ahead
+    expert = jnp.where(expert >= experts, expert - experts, expert)
+    earlier = (
+        lax.broadcasted_iota(jnp.int32, (rows, rows), 0)
+        < lax.broadcasted_iota(jnp.int32, (rows, rows), 1)
+    ).astype(jnp.bfloat16)
+    sets, placings, slot_gates = (y, 1 - y), [], []
+    for s in sets:
+        route, weight = routes[s], gates[s].astype(jnp.float32)
+        match = jnp.zeros(line.shape, jnp.float32)
+        named = jnp.zeros(line.shape, jnp.float32)
+        for k in range(route.shape[0]):
+            same = route[k : k + 1, :] == expert
+            match = match + jnp.where(same, 1.0, 0.0)
+            named = named + jnp.where(same, weight[k : k + 1, :], 0.0)
+        rank = jnp.dot(match.astype(jnp.bfloat16), earlier, preferred_element_type=jnp.float32)
+        placing = jnp.where(rank == slot, match, 0.0)
+        slot_gates.append(jnp.sum(placing * named, axis=1, keepdims=True))
+        placings.append(placing.astype(jnp.bfloat16))
+    few = -(-cap // 16) * 16
+    placings[1] = placings[1][:few]
+    blank = jnp.zeros((cap, LANES), jnp.float32)
+    extra = slice(2 * chunk, 2 * chunk + LANES)
+
+    def spread(which, k):
+        return jnp.broadcast_to(slot_gates[which][k * cap : (k + 1) * cap], (cap, LANES))
+
+    for k in range(1, experts):
+        messages[2 * (k - 1)][:, extra] = jnp.concatenate([spread(0, k), blank], axis=0).astype(jnp.bfloat16)
+    local[:, extra] = jnp.concatenate([spread(0, 0), blank, spread(1, 0), blank], axis=0).astype(jnp.bfloat16)
+    for i, (dx, h) in enumerate(steps):
+        copies[2 * i].wait()
+        copies[2 * i + 1].wait()
+        here = slice(h * chunk, (h + 1) * chunk)
+        found = [
+            jnp.dot(placing, buffers[i, j, s], preferred_element_type=jnp.float32)
+            for s, placing in zip(sets, placings)
+            for j in range(2)
+        ]
+        for k in range(1, experts):
+            span = slice(k * cap, (k + 1) * cap)
+            messages[2 * (k - 1) + dx][:, here] = jnp.concatenate(
+                [found[0][span], found[1][span]], axis=0
+            ).astype(jnp.bfloat16)
+        (local if dx == 0 else near)[:, here] = jnp.concatenate(
+            [part[:cap] for part in found], axis=0
+        ).astype(jnp.bfloat16)
+
+
+def pack(routes, gates, tokens, cotangent, experts, cap, chunk):
+    def shape(rows, gated):
+        return jax.ShapeDtypeStruct((rows, 2 * chunk + (LANES if gated else 0)), jnp.bfloat16)
+
+    outs = [shape(2 * cap, dx == 0) for _ in range(1, experts) for dx in range(2)]
+    outs += [shape(4 * cap, False), shape(4 * cap, True)]
+    sets, rows = tokens.shape[:2]
+    return pl.pallas_call(
+        functools.partial(pack_kernel, experts, cap),
+        out_shape=outs,
+        in_specs=[VMEM, VMEM, HBM, HBM],
+        out_specs=[VMEM] * len(outs),
+        scratch_shapes=[
+            pltpu.VMEM((4, 2, sets, rows, chunk), jnp.bfloat16),
+            pltpu.SemaphoreType.DMA((4, 2)),
+        ],
+        compiler_params=pltpu.CompilerParams(vmem_limit_bytes=24 * MIB),
+        cost_estimate=SMALL,
+        name="pack_rows",
+    )(routes, gates, tokens, cotangent)
+
+
+def block_products(parts, weights, cap, put, width=256):
+    chunk, inner = weights[0].shape
+    left = jnp.concatenate([part[:, :chunk] for part in parts], axis=0)
+    right = jnp.concatenate([part[:, chunk : 2 * chunk] for part in parts], axis=0)
+    across = (((1,), (1,)), ((), ()))
+
+    def along(columns, own, other):
+        return jnp.dot(left, own[:, columns], preferred_element_type=jnp.float32) + jnp.dot(
+            right, other[:, columns], preferred_element_type=jnp.float32
+        )
+
+    for at in range(0, inner, width):
+        columns = slice(at, at + width)
+        gate = along(columns, weights[0], weights[3])
+        up = along(columns, weights[1], weights[4])
+        product = lax.dot_general(
+            left, weights[2][columns], across, preferred_element_type=jnp.float32
+        ) + lax.dot_general(right, weights[5][columns], across, preferred_element_type=jnp.float32)
+        for b in range(left.shape[0] // (2 * cap)):
+            row = 2 * cap * b
+            put(b, at, gate[row : row + cap], up[row : row + cap], product[row + cap : row + 2 * cap])
+
+
+def gates_from(parts, cap, chunk):
+    found = []
+    for part in parts:
+        lanes = part[:, 2 * chunk : 2 * chunk + LANES].astype(jnp.float32)
+        found += [lanes[b : b + cap] for b in range(0, part.shape[0], 2 * cap)]
+    return jnp.concatenate(found, axis=0)
+
+
+def products_kernel(cap, width, n_sent, n_kept, *refs):
+    n = n_sent + n_kept
+    parts, weights, outs = refs[:n], refs[n : n + 6], refs[n + 6 :]
+    chunk, inner = weights[0].shape
+    half = outs[0].shape[0] // cap
+
+    def put(b, at, *terms):
+        rows = slice(b % half * cap, (b % half + 1) * cap)
+        for i, term in enumerate(terms):
+            outs[b // half][rows, i * inner + at : i * inner + at + width] = term
+
+    if n_kept:
+        outs[2][...] = gates_from(parts[n_sent:], cap, chunk)
+    block_products(parts, weights, cap, put, width)
+
+
+def products(sent, kept, weights, cap, width=256):
+    chunk, inner = weights[0].shape
+    half = sum(part.shape[0] for part in sent) // 2
+    outs = [jax.ShapeDtypeStruct((half, 3 * inner), jnp.float32)]
+    if kept:
+        outs += [outs[0], jax.ShapeDtypeStruct((half, LANES), jnp.float32)]
+    return pl.pallas_call(
+        functools.partial(products_kernel, cap, width, len(sent), len(kept)),
+        out_shape=outs,
+        in_specs=[VMEM] * (len(sent) + len(kept) + 6),
+        out_specs=[VMEM] * len(outs),
+        compiler_params=pltpu.CompilerParams(vmem_limit_bytes=16 * MIB),
+        cost_estimate=SMALL,
+        name="partial_products",
+    )(*sent, *kept, *weights)
+
+
+def neuron_terms_of(gate, up, product, gates):
+    return gate / (1.0 + jnp.exp(-gate)) * up * (gates * product)
+
+
+def in_set_order(mine, other):
+    y = lax.axis_index("tensor")
+    return jnp.concatenate(
+        [jnp.where(y == 0, mine, other), jnp.where(y == 0, other, mine)], axis=0
+    )
+
+
+def finish_kernel(cap, n, *refs):
+    out = refs[-1]
+    inner = out.shape[1]
+    sums = [jnp.zeros((1, inner), jnp.float32)] * 2
+    for g in range(n):
+        kept, came, gates = refs[3 * g : 3 * g + 3]
+        total = kept[...] + came[...]
+        terms = neuron_terms_of(
+            total[:, :inner], total[:, inner : 2 * inner], total[:, 2 * inner :], gates[:, :1]
+        )
+        for s in range(2):
+            sums[s] = sums[s] + jnp.sum(terms[s * cap : (s + 1) * cap], axis=0, keepdims=True)
+    out[...] = in_set_order(*sums)
+
+
+def finish(groups, cap):
+    inner = groups[0][0].shape[1] // 3
+    return pl.pallas_call(
+        functools.partial(finish_kernel, cap, len(groups)),
+        out_shape=jax.ShapeDtypeStruct((2, inner), jnp.float32),
+        in_specs=[VMEM] * (3 * len(groups)),
+        out_specs=VMEM,
+        compiler_params=pltpu.CompilerParams(vmem_limit_bytes=16 * MIB),
+        cost_estimate=SMALL,
+        name="neuron_sums",
+    )(*[value for group in groups for value in group])
+
+
+def last_kernel(cap, width, mine, other, *refs):
+    weights, (came, before, out) = refs[:6], refs[6:]
+    chunk, inner = weights[0].shape
+    gates = gates_from([mine, other], cap, chunk)
+    found = {}
+
+    def put(b, at, *terms):
+        rows = slice(b * cap, (b + 1) * cap)
+        gate, up, product = (
+            term + came[rows, i * inner + at : i * inner + at + width] for i, term in enumerate(terms)
+        )
+        found[b, at] = jnp.sum(
+            neuron_terms_of(gate, up, product, gates[rows, :1]), axis=0, keepdims=True
+        )
+
+    block_products([mine, other], weights, cap, put, width)
+    for at in range(0, inner, width):
+        columns = slice(at, at + width)
+        out[:, columns] = before[:, columns] + in_set_order(found[0, at], found[1, at])
+
+
+def last(mine, other, weights, came, before, cap, width=256):
+    chunk, inner = weights[0].shape
+    return pl.pallas_call(
+        functools.partial(last_kernel, cap, width),
+        out_shape=jax.ShapeDtypeStruct((2, inner), jnp.float32),
+        in_specs=[VMEM] * 10,
+        out_specs=VMEM,
+        compiler_params=pltpu.CompilerParams(vmem_limit_bytes=16 * MIB),
+        cost_estimate=SMALL,
+        name="last_products",
+    )(mine, other, *weights, came, before)
+
+
+def kept_pieces(dropped):
+    a, b, c = dropped[0, 0], dropped[0, 1], dropped[0, 2]
+    low, high = jnp.minimum(jnp.minimum(a, b), c), jnp.maximum(jnp.maximum(a, b), c)
+    middle = a + b + c - low - high
+
+    def place_of(piece):
+        block = piece // 2
+        for one in (low, middle, high):
+            block = block + (block >= one).astype(jnp.int32)
+        return 2 * block + lax.rem(piece, 2)
+
+    below = sum((one < NBLK // 2).astype(jnp.int32) for one in (a, b, c))
+    return place_of, 2 * (NBLK // 2 - below)
+
+
+def send_pieces_kernel(dropped, down, out, sems):
+    y = lax.axis_index("tensor")
+    place_of, low_pieces = kept_pieces(dropped)
+    first = jnp.where(y == 0, KEEP, low_pieces)
+    copies = []
+    for i in range(out.shape[0]):
+        piece = jnp.minimum(first + i, 2 * KEEP - 1)
+        at = jnp.clip(place_of(piece) - NBLK * y, 0, NBLK - 1)
+        copies.append(pltpu.make_async_copy(down.at[at], out.at[i], sems.at[i]))
+    for copy in copies:
+        copy.start()
+    for copy in copies:
+        copy.wait()
+
+
+def keep_pieces_kernel(dropped, down, came, out, sems):
+    y = lax.axis_index("tensor")
+    place_of, low_pieces = kept_pieces(dropped)
+    for i in range(KEEP):
+        piece = KEEP * y + i
+        is_low = (piece < low_pieces).astype(jnp.int32)
+        near = jnp.where(y == 0, is_low, 1 - is_low)
+        at = jnp.clip(place_of(piece) - NBLK * y, 0, NBLK - 1)
+        far_at = jnp.clip(piece - jnp.where(y == 0, low_pieces, KEEP), 0, came.shape[0] - 1)
+
+        @pl.when(near == 1)
+        def _():
+            pltpu.make_async_copy(down.at[at], out.at[i], sems.at[i]).start()
+
+        @pl.when(near == 0)
+        def _():
+            pltpu.make_async_copy(came.at[far_at], out.at[i], sems.at[i]).start()
+
+    for i in range(KEEP):
+        pltpu.make_async_copy(down.at[0], out.at[i], sems.at[i]).wait()
+
+
+def pieces_call(kernel, count, dropped, *sources):
+    return pl.pallas_call(
+        kernel,
+        out_shape=jax.ShapeDtypeStruct((count,) + sources[0].shape[1:], sources[0].dtype),
+        in_specs=[SMEM] + [HBM] * len(sources),
+        out_specs=VMEM,
+        scratch_shapes=[pltpu.SemaphoreType.DMA((count,))],
+        compiler_params=pltpu.CompilerParams(vmem_limit_bytes=8 * MIB),
+        cost_estimate=SMALL,
+        name="kept_rows",
+    )(dropped, *sources)
+
+
+def after(value, *others):
+    return lax.optimization_barrier((value,) + others)[0]
+
+
+def paired_body(tokens, cotangent, route_gate, routes, gate_weight, up_weight, down_weight, dropped):
+    experts = lax.axis_size("expert")
+    groups = lax.axis_size("dp")
+    cap = capacity_of(tokens.shape[1], routes.shape[2], experts)
+    chunk = gate_weight.shape[1]
+
+    def over_core(value):
+        return lax.ppermute(value, "dp", [(d, d ^ 1) for d in range(groups)])
+
+    def over_x(value):
+        return lax.ppermute(value, "dp", [(d, d ^ 2) for d in range(groups)])
+
+    def over_tensor(value):
+        return lax.ppermute(value, "tensor", [(0, 1), (1, 0)])
+
+    def ahead(value, k, dx):
+        return lax.ppermute(
+            value,
+            ("expert", "dp"),
+            [
+                (e * groups + d, (e + k) % experts * groups + (d ^ (2 * dx)))
+                for e in range(experts)
+                for d in range(groups)
+            ],
+        )
+
+    *messages, near, local = pack(
+        jnp.swapaxes(routes, 1, 2), jnp.swapaxes(route_gate, 1, 2), tokens, cotangent, experts, cap, chunk
+    )
+    own = (gate_weight[0], up_weight[0], down_weight[0])
+    order = [(1, 0), (3, 0), (1, 1), (3, 1), (2, 1), (2, 0)]
+
+    def message(i):
+        k, dx = order[i]
+        return messages[2 * (k - 1) + dx]
+
+    came, passed = [None] * 6, [None] * 6
+
+    def send(i, *others):
+        came[i] = ahead(after(message(i), *others) if others else message(i), *order[i])
+
+    def hand_on(i, *others):
+        passed[i] = over_tensor(after(came[i], *others) if others else came[i])
+
+    other = tuple(over_core(weight) for weight in own)
+    weights = own + other
+    send(0)
+    send(1)
+    came_near = over_x(after(near, *other))
+    send(2, came[0])
+    down = own[2].reshape(NBLK, HALF, chunk)
+    down_sent = pieces_call(send_pieces_kernel, 3, after(dropped, came[0]), down)
+    down_came = over_tensor(down_sent)
+    send(3, came[1])
+    hand_on(0, down_came)
+    hand_on(1)
+    terms = {}
+    sent, kept, gates = products([came_near], [local], weights, cap)
+    terms[0] = (kept, over_x(sent), gates)
+    send(4, came[2])
+    compact_down = pieces_call(keep_pieces_kernel, KEEP, dropped, down, down_came)
+    hand_on(2, compact_down)
+    sent, kept, gates = products([came[2], passed[2]], [came[0], passed[0]], weights, cap)
+    terms[1] = (kept, over_x(after(sent, terms[0][1])), gates)
+    send(5, came[3])
+    hand_on(3)
+    sent, kept, gates = products([came[3], passed[3]], [came[1], passed[1]], weights, cap)
+    terms[3] = (kept, over_x(after(sent, terms[1][1])), gates)
+    hand_on(4)
+    sums = finish([terms[0], terms[1], terms[3]], cap)
+    (sent,) = products([came[4], passed[4]], [], weights, cap)
+    hand_on(5, sums)
+    totals = last(came[5], passed[5], weights, over_x(sent), sums, cap)
+    saliency = jnp.abs(lax.psum(totals, "dp"))[:, None, :]
+    return saliency, compact_down.reshape(1, KEEP * HALF, chunk)
+
+
 def solution(mesh):
+    sizes = mesh.shape
+    paired = sizes["tensor"] == 2 and sizes["dp"] == 4 and sizes["expert"] == 4
     return jax.shard_map(
-        body,
+        paired_body if paired else general_body,
         mesh=mesh,
         in_specs=(
             P(None, ("expert", "dp"), None),

time: 245 us -> 115 us (0.47)
  waiting for transfers between devices: 176 us -> 57.4 us
  matrix products: 21 us -> 0 us
  Pallas kernels: 0 us -> 20.1 us
  between operations: 13.9 us -> 0.75 us
  starting transfers between devices: 15.7 us -> 26.3 us
  local copies, waits for them, and re-layouts: 9.24 us -> 4.33 us
    all_gather x4 -> x0, waiting for transfers between devices: 112 us -> none  [the longest x1 48.4 us: body(): lax.all_gather(up_weight, 'dp', axis=1, tiled=True)]
    all_to_all x3 -> x0, waiting for transfers between devices: 61.5 us -> none  [the longest x1 58.7 us: body(): lax.all_to_all(x_slots, 'expert', split_axis=0, concat_axis=0, tiled=True)]
    ppermute x0 -> x21, waiting for transfers between devices: none -> 57.4 us  [the longest x6 35.2 us: ahead(): lax.ppermute(value, ('expert', 'dp'), [(e * groups + d, (e + k) % experts...]
    ppermute x0 -> x21, starting transfers between devices: none -> 26.3 us  [the longest x6 13.3 us: ahead(): lax.ppermute(value, ('expert', 'dp'), [(e * groups + d, (e + k) % experts...]
    dot_general x6 -> x0, matrix products: 21 us -> none  [the longest x1 6.46 us: neuron_terms(): jnp.einsum('pscd,fd->pscf', grad_recv, down_full, preferred_element_type=...]
    pallas_call x0 -> x9, Pallas kernels: none -> 20.1 us  [the longest x4 10.5 us: products(): pl.pallas_call(functools.partial(products_kernel, cap, width, len(sent),...]
    all_to_all x3 -> x0, starting transfers between devices: 15.5 us -> none  [the longest x1 6.32 us: body(): lax.all_to_all(gate_slots, 'expert', split_axis=0, concat_axis=0, tiled=T...]
    gather x1 -> x0, local copies, waits for them, and re-layouts: 6.49 us -> none  [body(): compact_down = jnp.take(whole_rows, source_rows, axis=0)[None]]
  transfers between devices with their start and end apart: 7 -> 21, of which waited for: 5 -> 10; matrix products, arithmetic and copies ran while one was open for 10% -> 0% of each run, Pallas kernels for 0% -> 15%
where the time goes in v2:
time: 115 us
  waiting for transfers between devices  57.4 us (50%)
  starting transfers between devices  26.3 us (23%)
  Pallas kernels  20.1 us (17%)
  blocking collectives  5.77 us (5%)
  local copies, waits for them, and re-layouts  4.33 us (4%)
    ppermute x6, waiting for transfers between devices, ahead(): lax.ppermute(value, ('expert', 'dp'), [(e * groups + d, (e + k) % experts...  35.2 us
    ppermute x5, waiting for transfers between devices, over_x(): return lax.ppermute(value, 'dp', [(d, d ^ 2) for d in range(groups)])  18.9 us
    ppermute x6, starting transfers between devices, ahead(): lax.ppermute(value, ('expert', 'dp'), [(e * groups + d, (e + k) % experts...  13.3 us
    pallas_call x4, Pallas kernels, products(): pl.pallas_call(functools.partial(products_kernel, cap, width, len(sent),...  10.5 us
    ppermute x7, starting transfers between devices, over_tensor(): return lax.ppermute(value, 'tensor', [(0, 1), (1, 0)])  6.78 us
    psum x1, blocking collectives, paired_body(): saliency = jnp.abs(lax.psum(totals, 'dp'))[:, None, :]  5.77 us
    ppermute x5, starting transfers between devices, over_x(): return lax.ppermute(value, 'dp', [(d, d ^ 2) for d in range(groups)])  5.22 us
    pallas_call x2, Pallas kernels, pieces_call(): pl.pallas_call(kernel, out_shape=jax.ShapeDtypeStruct((count,) + sources[...  4.88 us
  transfers between devices with their start and end apart: 21, of which 10 were waited for; matrix products, arithmetic and copies ran while one was open for 0% of the time, Pallas kernels for 15%

profile of v2, /device:TPU:0, one launch (start us, length us, event | category | flops | bytes accessed | tf_op | source)
XLA Modules:
  0.0 114.6 jit_solution(14715108959213609148)
XLA Ops:
  1.7 1.2 %copy-done.3 = bf16[2,32,7168]{2,1,0:T(8,128)(2,1)S(1)} copy-done((bf16[2,32,7168]{2,1,0:T(8,128)(2,1)S(1)}, bf16[2,32,7168]{2,1,0:T(8,128)(2,1)}, u32[]{:S(2)}) %copy-start.3) | copy-done | bytes 917528
  2.9 1.2 %copy-done.4 = bf16[2,32,7168]{2,1,0:T(8,128)(2,1)S(1)} copy-done((bf16[2,32,7168]{2,1,0:T(8,128)(2,1)S(1)}, bf16[2,32,7168]{2,1,0:T(8,128)(2,1)}, u32[]{:S(2)}) %copy-start.4) | copy-done | bytes 917528
  4.0 0.7 copy-done.5
  4.7 0.7 copy-done.7
  5.4 2.1 %pack_rows.1 = (bf16[48,3712]{1,0:T(8,128)(2,1)S(1)}, bf16[48,3584]{1,0:T(8,128)(2,1)S(1)}, bf16[48,3712]{1,0:T(8,128)(2,1)S(1)}, bf16[48,3584]{1,0:T(8,128)(2,1...) custom-call(s32[2,2,32]{2,1,0:T(2,128)S(1)} %bitcast.29, ...), custom_call_target="tpu_custom_call" | custom-call | tf_op jit(solution)/shard_map/pack_rows/pallas_call | solution.py:174
  7.5 2.7 %collective-permute-start.8 = (bf16[48,3712]{1,0:T(8,128)(2,1)S(1)}, bf16[48,3712]{1,0:T(8,128)(2,1)S(1)}, u32[]{:S(2)}, u32[]{:S(2)}) collective-permute-start(bf16[48,3712]{1,0:T(8,128)(2,1)S(1)} %get-tuple-element.42), channel_id=1, source_target_pairs={{0,8},{2,10},{4,12},{6,14},{8,16},{10,18},{12,20},{14,22},{16,24},... | collective-permute-start | bytes 1069064 | tf_op jit(solution)/shard_map/ppermute | solution.py:411
  10.2 10.9 %collective-permute-done.8.refs_2_ = bf16[48,3712]{1,0:T(8,128)(2,1)S(1)} collective-permute-done((bf16[48,3712]{1,0:T(8,128)(2,1)S(1)}, bf16[48,3712]{1,0:T(8,128)(2,1)S(1)}, u32[]{:S(2)}, u32[]{:S(2)}) %collective-permute-start.8) | collective-permute-done | bytes 356384 | tf_op jit(solution)/shard_map/ppermute | solution.py:411
  21.1 1.5 %kept_rows.2 = bf16[3,64,1792]{2,1,0:T(8,128)(2,1)S(1)} custom-call(s32[1,3]{1,0:T(1,128)S(1)} %copy-done.6, bf16[8,64,1792]{2,1,0:T(8,128)(2,1)S(1)} %bitcast.10), custom_call_target="tpu_custom_call" | custom-call | tf_op jit(solution)/shard_map/kept_rows/pallas_call | solution.py:379
  22.6 1.6 %collective-permute-start.10 = (bf16[3,64,1792]{2,1,0:T(8,128)(2,1)S(1)}, bf16[3,64,1792]{2,1,0:T(8,128)(2,1)S(1)}, u32[]{:S(2)}, u32[]{:S(2)}) collective-permute-start(bf16[3,64,1792]{2,1,0:T(8,128)(2,1)S(1)} %kept_rows.2), channel_id=1, source_target_pairs={{0,1},{1,0},{2,3},{3,2},{4,5},{5,4},{6,7},{7,6},{8,9},{9,8},{10,11... | collective-permute-start | bytes 2064392 | tf_op jit(solution)/shard_map/ppermute | solution.py:408
  24.2 1.6 %collective-permute-start.6 = (bf16[96,3584]{1,0:T(8,128)(2,1)S(1)}, bf16[96,3584]{1,0:T(8,128)(2,1)S(1)}, u32[]{:S(2)}, u32[]{:S(2)}) collective-permute-start(bf16[96,3584]{1,0:T(8,128)(2,1)S(1)} %get-tuple-element.36), channel_id=1, source_target_pairs={{0,4},{2,6},{4,0},{6,2},{1,5},{3,7},{5,1},{7,3},{8,12},{10,14},{12... | collective-permute-start | bytes 2064392 | tf_op jit(solution)/shard_map/ppermute | solution.py:405
  25.8 1.8 %collective-permute-start = (bf16[48,3712]{1,0:T(8,128)(2,1)S(1)}, bf16[48,3712]{1,0:T(8,128)(2,1)S(1)}, u32[]{:S(2)}, u32[]{:S(2)}) collective-permute-start(bf16[48,3712]{1,0:T(8,128)(2,1)S(1)} %get-tuple-element.32), channel_id=1, source_target_pairs={{0,24},{2,26},{4,28},{6,30},{8,0},{10,2},{12,4},{14,6},{16,8},{18,... | collective-permute-start | bytes 1069064 | tf_op jit(solution)/shard_map/ppermute | solution.py:411
  27.8 13.5 %collective-permute-done.refs_2_ = bf16[48,3712]{1,0:T(8,128)(2,1)S(1)} collective-permute-done((bf16[48,3712]{1,0:T(8,128)(2,1)S(1)}, bf16[48,3712]{1,0:T(8,128)(2,1)S(1)}, u32[]{:S(2)}, u32[]{:S(2)}) %collective-permute-start) | collective-permute-done | bytes 356384 | tf_op jit(solution)/shard_map/ppermute | solution.py:411
  41.3 3.4 %kept_rows.3 = bf16[5,64,1792]{2,1,0:T(8,128)(2,1)} custom-call(s32[1,3]{1,0:T(1,128)S(1)} %copy-done.6, bf16[8,64,1792]{2,1,0:T(8,128)(2,1)S(1)} %bitcast.11, bf16[3,64,1792]{2,1,0:T(8,128)(2,1)S(1)} %collective-permute-done.10.came), custom_call_target="tpu_custom_call" | custom-call | tf_op jit(solution)/shard_map/kept_rows/pallas_call | solution.py:379
  45.2 1.6 %collective-permute-start.12 = (bf16[48,3712]{1,0:T(8,128)(2,1)S(1)}, bf16[48,3712]{1,0:T(8,128)(2,1)S(1)}, u32[]{:S(2)}, u32[]{:S(2)}) collective-permute-start(bf16[48,3712]{1,0:T(8,128)(2,1)S(1)} %collective-permute-done.8.refs_2_), channel_id=1, source_target_pairs={{0,1},{1,0},{2,3},{3,2},{4,5},{5,4},{6,7},{7,6},{8,9},{9,8},{10,11... | collective-permute-start | bytes 1069064 | tf_op jit(solution)/shard_map/ppermute | solution.py:408
  46.8 9.0 %collective-permute-done.6.refs_0_ = bf16[96,3584]{1,0:T(8,128)(2,1)S(1)} collective-permute-done((bf16[96,3584]{1,0:T(8,128)(2,1)S(1)}, bf16[96,3584]{1,0:T(8,128)(2,1)S(1)}, u32[]{:S(2)}, u32[]{:S(2)}) %collective-permute-start.6) | collective-permute-done | bytes 688160 | tf_op jit(solution)/shard_map/ppermute | solution.py:405
  55.8 2.7 %partial_products.4 = (f32[48,1536]{1,0:T(8,128)S(1)}, f32[48,1536]{1,0:T(8,128)S(1)}, f32[48,128]{1,0:T(8,128)S(1)}) custom-call(bf16[96,3584]{1,0:T(8,128)(2,1)S(1)} %collective-permute-done.6.refs_0_, bf16[96,3712]{1,0:T(8,128)(2,1)S(1)} %get-tuple-element.37.refs_1_, bf16[1792,512]{1,0:T(8,128)(2,1)S(1)} %bitcast.18, bf16[1792,512]{1,0:T(8,128)(2,1)S(1)} %bitcast.24, ...), custom_call_target="tpu_custom_call" | custom-call | tf_op jit(solution)/shard_map/partial_products/pallas_call | solution.py:242
  58.5 1.6 %collective-permute-start.7 = (f32[48,1536]{1,0:T(8,128)S(1)}, f32[48,1536]{1,0:T(8,128)S(1)}, u32[]{:S(2)}, u32[]{:S(2)}) collective-permute-start(f32[48,1536]{1,0:T(8,128)S(1)} %get-tuple-element.39), channel_id=1, source_target_pairs={{0,4},{2,6},{4,0},{6,2},{1,5},{3,7},{5,1},{7,3},{8,12},{10,14},{12... | collective-permute-start | bytes 884744 | tf_op jit(solution)/shard_map/ppermute | solution.py:405
  60.6 1.5 %collective-permute-start.14 = (bf16[48,3584]{1,0:T(8,128)(2,1)S(1)}, bf16[48,3584]{1,0:T(8,128)(2,1)S(1)}, u32[]{:S(2)}, u32[]{:S(2)}) collective-permute-start(bf16[48,3584]{1,0:T(8,128)(2,1)S(1)} %collective-permute-done.1.refs_0_), channel_id=1, source_target_pairs={{0,1},{1,0},{2,3},{3,2},{4,5},{5,4},{6,7},{7,6},{8,9},{9,8},{10,11... | collective-permute-start | bytes 1032200 | tf_op jit(solution)/shard_map/ppermute | solution.py:408
  62.1 0.7 collective-permute-start.18
  62.8 2.7 %partial_products.5 = (f32[48,1536]{1,0:T(8,128)S(1)}, f32[48,1536]{1,0:T(8,128)S(1)}, f32[48,128]{1,0:T(8,128)S(1)}) custom-call(bf16[48,3584]{1,0:T(8,128)(2,1)S(1)} %collective-permute-done.9.refs_0_, bf16[48,3584]{1,0:T(8,128)(2,1)S(1)} %collective-permute-done.11.refs_1_, bf16[48,3712]{1,0:T(8,128)(2,1)S(1)} %collective-permute-done.8.refs_2_, ...), custom_call_target="tpu_custom_call" | custom-call | tf_op jit(solution)/shard_map/partial_products/pallas_call | solution.py:242
  65.5 0.7 collective-permute-done.7.refs_1_
  66.2 1.4 %collective-permute-start.13 = (f32[48,1536]{1,0:T(8,128)S(1)}, f32[48,1536]{1,0:T(8,128)S(1)}, u32[]{:S(2)}, u32[]{:S(2)}) collective-permute-start(f32[48,1536]{1,0:T(8,128)S(1)} %get-tuple-element.49), channel_id=1, source_target_pairs={{0,4},{2,6},{4,0},{6,2},{1,5},{3,7},{5,1},{7,3},{8,12},{10,14},{12... | collective-permute-start | bytes 884744 | tf_op jit(solution)/shard_map/ppermute | solution.py:405
  67.6 7.9 %collective-permute-start.2 = (bf16[48,3712]{1,0:T(8,128)(2,1)S(1)}, bf16[48,3712]{1,0:T(8,128)(2,1)S(1)}, u32[]{:S(2)}, u32[]{:S(2)}) collective-permute-start(bf16[48,3712]{1,0:T(8,128)(2,1)S(1)} %get-tuple-element.34), channel_id=1, source_target_pairs={{0,16},{2,18},{4,20},{6,22},{8,24},{10,26},{12,28},{14,30},{16,0},... | collective-permute-start | bytes 1069064 | tf_op jit(solution)/shard_map/ppermute | solution.py:411
  75.9 2.7 %partial_products.6 = (f32[48,1536]{1,0:T(8,128)S(1)}, f32[48,1536]{1,0:T(8,128)S(1)}, f32[48,128]{1,0:T(8,128)S(1)}) custom-call(bf16[48,3584]{1,0:T(8,128)(2,1)S(1)} %collective-permute-done.1.refs_0_, bf16[48,3584]{1,0:T(8,128)(2,1)S(1)} %collective-permute-done.14.refs_1_, bf16[48,3712]{1,0:T(8,128)(2,1)S(1)} %collective-permute-done.refs_2_, ...), custom_call_target="tpu_custom_call" | custom-call | tf_op jit(solution)/shard_map/partial_products/pallas_call | solution.py:242
  79.3 6.5 %collective-permute-done.18.refs_0_ = bf16[48,3584]{1,0:T(8,128)(2,1)S(1)} collective-permute-done((bf16[48,3584]{1,0:T(8,128)(2,1)S(1)}, bf16[48,3584]{1,0:T(8,128)(2,1)S(1)}, u32[]{:S(2)}, u32[]{:S(2)}) %collective-permute-start.18) | collective-permute-done | bytes 344096 | tf_op jit(solution)/shard_map/ppermute | solution.py:411
  86.3 1.8 %collective-permute-done.16.refs_7_ = f32[48,1536]{1,0:T(8,128)S(1)} collective-permute-done((f32[48,1536]{1,0:T(8,128)S(1)}, f32[48,1536]{1,0:T(8,128)S(1)}, u32[]{:S(2)}, u32[]{:S(2)}) %collective-permute-start.16) | collective-permute-done | bytes 294944 | tf_op jit(solution)/shard_map/ppermute | solution.py:405
  88.3 4.2 %collective-permute-done.2.mine = bf16[48,3712]{1,0:T(8,128)(2,1)S(1)} collective-permute-done((bf16[48,3712]{1,0:T(8,128)(2,1)S(1)}, bf16[48,3712]{1,0:T(8,128)(2,1)S(1)}, u32[]{:S(2)}, u32[]{:S(2)}) %collective-permute-start.2) | collective-permute-done | bytes 356384 | tf_op jit(solution)/shard_map/ppermute | solution.py:411
  93.0 2.9 %collective-permute-done.19.refs_1_ = bf16[48,3584]{1,0:T(8,128)(2,1)S(1)} collective-permute-done((bf16[48,3584]{1,0:T(8,128)(2,1)S(1)}, bf16[48,3584]{1,0:T(8,128)(2,1)S(1)}, u32[]{:S(2)}, u32[]{:S(2)}) %collective-permute-start.19) | collective-permute-done | bytes 344096 | tf_op jit(solution)/shard_map/ppermute | solution.py:408
  95.9 2.3 %partial_products.7 = f32[48,1536]{1,0:T(8,128)S(1)} custom-call(bf16[48,3584]{1,0:T(8,128)(2,1)S(1)} %collective-permute-done.18.refs_0_, bf16[48,3584]{1,0:T(8,128)(2,1)S(1)} %collective-permute-done.19.refs_1_, bf16[1792,512]{1,0:T(8,128)(2,1)S(1)} %bitcast.21, bf16[1792,512]{1,0:T(8,128)(2,1)S(1)} %bitcast.27, bf16[512,1792]{1,0:T(8,128)(2,1)S(1)} %bitcast.15, ...), custom_call_target="tpu_custom_call" | custom-call | tf_op jit(solution)/shard_map/partial_products/pallas_call | solution.py:242
  98.4 7.4 %collective-permute-done.20.refs_6_ = f32[48,1536]{1,0:T(8,128)S(1)} collective-permute-done((f32[48,1536]{1,0:T(8,128)S(1)}, f32[48,1536]{1,0:T(8,128)S(1)}, u32[]{:S(2)}, u32[]{:S(2)}) %collective-permute-start.20) | collective-permute-done | bytes 294944 | tf_op jit(solution)/shard_map/ppermute | solution.py:405
  105.8 2.4 %last_products.1 = f32[2,512]{1,0:T(2,128)S(1)} custom-call(bf16[48,3712]{1,0:T(8,128)(2,1)S(1)} %collective-permute-done.2.mine, bf16[48,3712]{1,0:T(8,128)(2,1)S(1)} %collective-permute-done.17.other, bf16[1792,512]{1,0:T(8,128)(2,1)S(1)} %bitcast.22, bf16[1792,512]{1,0:T(8,128)(2,1)S(1)} %bitcast.28, bf16[512,1792]{1,0:T(8,128)(2,1)S(1)} %bitcast.16, ...), custom_call_target="tpu_custom_call" | custom-call | tf_op jit(solution)/shard_map/last_products/pallas_call | solution.py:315
  108.2 5.8 %psum.7 = f32[2,512]{1,0:T(2,128)S(1)} all-reduce(f32[2,512]{1,0:T(2,128)S(1)} %last_products.1), channel_id=1, replica_groups=mesh['expert'=4,'dp'=4,'tensor'=2] {'dp'}, use_global_device_ids=true, to_apply=%region_0.0 | all-reduce | flops 1024 | bytes 8192 | tf_op jit(solution)/shard_map/psum | solution.py:468
  (38 shorter events, 5.3 us)
Async XLA Ops:
  0.6 20.5 %copy-start = (bf16[1,512,1792]{2,1,0:T(8,128)(2,1)S(1)}, bf16[1,512,1792]{2,1,0:T(8,128)(2,1)}, u32[]{:S(2)}) copy-start(bf16[1,512,1792]{2,1,0:T(8,128)(2,1)} %param.14) | copy-start | bytes 5505028
  0.6 23.6 %collective-permute-start.3 = (bf16[1792,512]{1,0:T(8,128)(2,1)}, bf16[1792,512]{1,0:T(8,128)(2,1)S(1)}, u32[]{:S(2)}, u32[]{:S(2)}) collective-permute-start(bf16[1792,512]{1,0:T(8,128)(2,1)} %bitcast.17), channel_id=1, source_target_pairs={{0,2},{2,0},{4,6},{6,4},{1,3},{3,1},{5,7},{7,5},{8,10},{10,8},{12,... | collective-permute-start | bytes 5505032 | tf_op jit(solution)/shard_map/ppermute | solution.py:402
  1.2 23.1 %collective-permute-start.4 = (bf16[1792,512]{1,0:T(8,128)(2,1)}, bf16[1792,512]{1,0:T(8,128)(2,1)S(1)}, u32[]{:S(2)}, u32[]{:S(2)}) collective-permute-start(bf16[1792,512]{1,0:T(8,128)(2,1)} %bitcast.23), channel_id=1, source_target_pairs={{0,2},{2,0},{4,6},{6,4},{1,3},{3,1},{5,7},{7,5},{8,10},{10,8},{12,... | collective-permute-start | bytes 5505032 | tf_op jit(solution)/shard_map/ppermute | solution.py:402
  1.2 23.0 %collective-permute-start.5 = (bf16[512,1792]{1,0:T(8,128)(2,1)}, bf16[512,1792]{1,0:T(8,128)(2,1)S(1)}, u32[]{:S(2)}, u32[]{:S(2)}) collective-permute-start(bf16[512,1792]{1,0:T(8,128)(2,1)} %bitcast.9), channel_id=1, source_target_pairs={{0,2},{2,0},{4,6},{6,4},{1,3},{3,1},{5,7},{7,5},{8,10},{10,8},{12,... | collective-permute-start | bytes 5505032 | tf_op jit(solution)/shard_map/ppermute | solution.py:402
  1.7 1.2 %copy-start.3 = (bf16[2,32,7168]{2,1,0:T(8,128)(2,1)S(1)}, bf16[2,32,7168]{2,1,0:T(8,128)(2,1)}, u32[]{:S(2)}) copy-start(bf16[2,32,7168]{2,1,0:T(8,128)(2,1)} %tokens.1) | copy-start | bytes 2752516
  2.9 1.2 %copy-start.4 = (bf16[2,32,7168]{2,1,0:T(8,128)(2,1)S(1)}, bf16[2,32,7168]{2,1,0:T(8,128)(2,1)}, u32[]{:S(2)}) copy-start(bf16[2,32,7168]{2,1,0:T(8,128)(2,1)} %cotangent.1) | copy-start | bytes 2752516
  4.0 0.7 copy-start.5
  4.7 0.7 copy-start.7
  5.4 15.7 %copy-start.6 = (s32[1,3]{1,0:T(1,128)S(1)}, s32[1,3]{1,0:T(1,128)}, u32[]{:S(2)}) copy-start(s32[1,3]{1,0:T(1,128)} %dropped.2) | copy-start | bytes 40
  7.5 13.6 %collective-permute-start.8 = (bf16[48,3712]{1,0:T(8,128)(2,1)S(1)}, bf16[48,3712]{1,0:T(8,128)(2,1)S(1)}, u32[]{:S(2)}, u32[]{:S(2)}) collective-permute-start(bf16[48,3712]{1,0:T(8,128)(2,1)S(1)} %get-tuple-element.42), channel_id=1, source_target_pairs={{0,8},{2,10},{4,12},{6,14},{8,16},{10,18},{12,20},{14,22},{16,24},... | collective-permute-start | bytes 1069064 | tf_op jit(solution)/shard_map/ppermute | solution.py:411
  22.6 18.7 %collective-permute-start.10 = (bf16[3,64,1792]{2,1,0:T(8,128)(2,1)S(1)}, bf16[3,64,1792]{2,1,0:T(8,128)(2,1)S(1)}, u32[]{:S(2)}, u32[]{:S(2)}) collective-permute-start(bf16[3,64,1792]{2,1,0:T(8,128)(2,1)S(1)} %kept_rows.2), channel_id=1, source_target_pairs={{0,1},{1,0},{2,3},{3,2},{4,5},{5,4},{6,7},{7,6},{8,9},{9,8},{10,11... | collective-permute-start | bytes 2064392 | tf_op jit(solution)/shard_map/ppermute | solution.py:408
  24.2 31.6 %collective-permute-start.6 = (bf16[96,3584]{1,0:T(8,128)(2,1)S(1)}, bf16[96,3584]{1,0:T(8,128)(2,1)S(1)}, u32[]{:S(2)}, u32[]{:S(2)}) collective-permute-start(bf16[96,3584]{1,0:T(8,128)(2,1)S(1)} %get-tuple-element.36), channel_id=1, source_target_pairs={{0,4},{2,6},{4,0},{6,2},{1,5},{3,7},{5,1},{7,3},{8,12},{10,14},{12... | collective-permute-start | bytes 2064392 | tf_op jit(solution)/shard_map/ppermute | solution.py:405
  25.8 15.5 %collective-permute-start = (bf16[48,3712]{1,0:T(8,128)(2,1)S(1)}, bf16[48,3712]{1,0:T(8,128)(2,1)S(1)}, u32[]{:S(2)}, u32[]{:S(2)}) collective-permute-start(bf16[48,3712]{1,0:T(8,128)(2,1)S(1)} %get-tuple-element.32), channel_id=1, source_target_pairs={{0,24},{2,26},{4,28},{6,30},{8,0},{10,2},{12,4},{14,6},{16,8},{18,... | collective-permute-start | bytes 1069064 | tf_op jit(solution)/shard_map/ppermute | solution.py:411
  27.6 17.2 %collective-permute-start.9 = (bf16[48,3584]{1,0:T(8,128)(2,1)S(1)}, bf16[48,3584]{1,0:T(8,128)(2,1)S(1)}, u32[]{:S(2)}, u32[]{:S(2)}) collective-permute-start(bf16[48,3584]{1,0:T(8,128)(2,1)S(1)} %get-tuple-element.43), channel_id=1, source_target_pairs={{0,12},{2,14},{4,8},{6,10},{8,20},{10,22},{12,16},{14,18},{16,28},... | collective-permute-start | bytes 1032200 | tf_op jit(solution)/shard_map/ppermute | solution.py:411
  41.3 14.5 %copy-start.1 = (bf16[1,1792,512]{2,1,0:T(8,128)(2,1)S(1)}, bf16[1,1792,512]{2,1,0:T(8,128)(2,1)}, u32[]{:S(2)}) copy-start(bf16[1,1792,512]{2,1,0:T(8,128)(2,1)} %param.12) | copy-start | bytes 5505028
  41.3 14.5 %copy-start.2 = (bf16[1,1792,512]{2,1,0:T(8,128)(2,1)S(1)}, bf16[1,1792,512]{2,1,0:T(8,128)(2,1)}, u32[]{:S(2)}) copy-start(bf16[1,1792,512]{2,1,0:T(8,128)(2,1)} %param.13) | copy-start | bytes 5505028
  41.3 19.3 %collective-permute-start.1 = (bf16[48,3584]{1,0:T(8,128)(2,1)S(1)}, bf16[48,3584]{1,0:T(8,128)(2,1)S(1)}, u32[]{:S(2)}, u32[]{:S(2)}) collective-permute-start(bf16[48,3584]{1,0:T(8,128)(2,1)S(1)} %get-tuple-element.33), channel_id=1, source_target_pairs={{0,28},{2,30},{4,24},{6,26},{8,4},{10,6},{12,0},{14,2},{16,12},{18... | collective-permute-start | bytes 1032200 | tf_op jit(solution)/shard_map/ppermute | solution.py:411
  44.7 17.4 %collective-permute-start.11 = (bf16[48,3584]{1,0:T(8,128)(2,1)S(1)}, bf16[48,3584]{1,0:T(8,128)(2,1)S(1)}, u32[]{:S(2)}, u32[]{:S(2)}) collective-permute-start(bf16[48,3584]{1,0:T(8,128)(2,1)S(1)} %collective-permute-done.9.refs_0_), channel_id=1, source_target_pairs={{0,1},{1,0},{2,3},{3,2},{4,5},{5,4},{6,7},{7,6},{8,9},{9,8},{10,11... | collective-permute-start | bytes 1032200 | tf_op jit(solution)/shard_map/ppermute | solution.py:408
  45.2 17.6 %collective-permute-start.12 = (bf16[48,3712]{1,0:T(8,128)(2,1)S(1)}, bf16[48,3712]{1,0:T(8,128)(2,1)S(1)}, u32[]{:S(2)}, u32[]{:S(2)}) collective-permute-start(bf16[48,3712]{1,0:T(8,128)(2,1)S(1)} %collective-permute-done.8.refs_2_), channel_id=1, source_target_pairs={{0,1},{1,0},{2,3},{3,2},{4,5},{5,4},{6,7},{7,6},{8,9},{9,8},{10,11... | collective-permute-start | bytes 1069064 | tf_op jit(solution)/shard_map/ppermute | solution.py:408
  58.5 7.6 %collective-permute-start.7 = (f32[48,1536]{1,0:T(8,128)S(1)}, f32[48,1536]{1,0:T(8,128)S(1)}, u32[]{:S(2)}, u32[]{:S(2)}) collective-permute-start(f32[48,1536]{1,0:T(8,128)S(1)} %get-tuple-element.39), channel_id=1, source_target_pairs={{0,4},{2,6},{4,0},{6,2},{1,5},{3,7},{5,1},{7,3},{8,12},{10,14},{12... | collective-permute-start | bytes 884744 | tf_op jit(solution)/shard_map/ppermute | solution.py:405
  60.1 15.4 %collective-permute-start.15 = (bf16[48,3712]{1,0:T(8,128)(2,1)S(1)}, bf16[48,3712]{1,0:T(8,128)(2,1)S(1)}, u32[]{:S(2)}, u32[]{:S(2)}) collective-permute-start(bf16[48,3712]{1,0:T(8,128)(2,1)S(1)} %collective-permute-done.refs_2_), channel_id=1, source_target_pairs={{0,1},{1,0},{2,3},{3,2},{4,5},{5,4},{6,7},{7,6},{8,9},{9,8},{10,11... | collective-permute-start | bytes 1069064 | tf_op jit(solution)/shard_map/ppermute | solution.py:408
  60.6 15.3 %collective-permute-start.14 = (bf16[48,3584]{1,0:T(8,128)(2,1)S(1)}, bf16[48,3584]{1,0:T(8,128)(2,1)S(1)}, u32[]{:S(2)}, u32[]{:S(2)}) collective-permute-start(bf16[48,3584]{1,0:T(8,128)(2,1)S(1)} %collective-permute-done.1.refs_0_), channel_id=1, source_target_pairs={{0,1},{1,0},{2,3},{3,2},{4,5},{5,4},{6,7},{7,6},{8,9},{9,8},{10,11... | collective-permute-start | bytes 1032200 | tf_op jit(solution)/shard_map/ppermute | solution.py:408
  62.1 23.7 %collective-permute-start.18 = (bf16[48,3584]{1,0:T(8,128)(2,1)S(1)}, bf16[48,3584]{1,0:T(8,128)(2,1)S(1)}, u32[]{:S(2)}, u32[]{:S(2)}) collective-permute-start(bf16[48,3584]{1,0:T(8,128)(2,1)S(1)} %get-tuple-element.57), channel_id=1, source_target_pairs={{0,20},{2,22},{4,16},{6,18},{8,28},{10,30},{12,24},{14,26},{16,4},... | collective-permute-start | bytes 1032200 | tf_op jit(solution)/shard_map/ppermute | solution.py:411
  66.2 12.5 %collective-permute-start.13 = (f32[48,1536]{1,0:T(8,128)S(1)}, f32[48,1536]{1,0:T(8,128)S(1)}, u32[]{:S(2)}, u32[]{:S(2)}) collective-permute-start(f32[48,1536]{1,0:T(8,128)S(1)} %get-tuple-element.49), channel_id=1, source_target_pairs={{0,4},{2,6},{4,0},{6,2},{1,5},{3,7},{5,1},{7,3},{8,12},{10,14},{12... | collective-permute-start | bytes 884744 | tf_op jit(solution)/shard_map/ppermute | solution.py:405
  67.6 24.9 %collective-permute-start.2 = (bf16[48,3712]{1,0:T(8,128)(2,1)S(1)}, bf16[48,3712]{1,0:T(8,128)(2,1)S(1)}, u32[]{:S(2)}, u32[]{:S(2)}) collective-permute-start(bf16[48,3712]{1,0:T(8,128)(2,1)S(1)} %get-tuple-element.34), channel_id=1, source_target_pairs={{0,16},{2,18},{4,20},{6,22},{8,24},{10,26},{12,28},{14,30},{16,0},... | collective-permute-start | bytes 1069064 | tf_op jit(solution)/shard_map/ppermute | solution.py:411
  78.7 9.4 %collective-permute-start.16 = (f32[48,1536]{1,0:T(8,128)S(1)}, f32[48,1536]{1,0:T(8,128)S(1)}, u32[]{:S(2)}, u32[]{:S(2)}) collective-permute-start(f32[48,1536]{1,0:T(8,128)S(1)} %get-tuple-element.53), channel_id=1, source_target_pairs={{0,4},{2,6},{4,0},{6,2},{1,5},{3,7},{5,1},{7,3},{8,12},{10,14},{12... | collective-permute-start | bytes 884744 | tf_op jit(solution)/shard_map/ppermute | solution.py:405
  85.8 10.1 %collective-permute-start.19 = (bf16[48,3584]{1,0:T(8,128)(2,1)S(1)}, bf16[48,3584]{1,0:T(8,128)(2,1)S(1)}, u32[]{:S(2)}, u32[]{:S(2)}) collective-permute-start(bf16[48,3584]{1,0:T(8,128)(2,1)S(1)} %collective-permute-done.18.refs_0_), channel_id=1, source_target_pairs={{0,1},{1,0},{2,3},{3,2},{4,5},{5,4},{6,7},{7,6},{8,9},{9,8},{10,11... | collective-permute-start | bytes 1032200 | tf_op jit(solution)/shard_map/ppermute | solution.py:408
  92.5 13.3 %collective-permute-start.17 = (bf16[48,3712]{1,0:T(8,128)(2,1)S(1)}, bf16[48,3712]{1,0:T(8,128)(2,1)S(1)}, u32[]{:S(2)}, u32[]{:S(2)}) collective-permute-start(bf16[48,3712]{1,0:T(8,128)(2,1)S(1)} %collective-permute-done.2.mine), channel_id=1, source_target_pairs={{0,1},{1,0},{2,3},{3,2},{4,5},{5,4},{6,7},{7,6},{8,9},{9,8},{10,11... | collective-permute-start | bytes 1069064 | tf_op jit(solution)/shard_map/ppermute | solution.py:408
  98.3 7.5 %collective-permute-start.20 = (f32[48,1536]{1,0:T(8,128)S(1)}, f32[48,1536]{1,0:T(8,128)S(1)}, u32[]{:S(2)}, u32[]{:S(2)}) collective-permute-start(f32[48,1536]{1,0:T(8,128)S(1)} %partial_products.7), channel_id=1, source_target_pairs={{0,4},{2,6},{4,0},{6,2},{1,5},{3,7},{5,1},{7,3},{8,12},{10,14},{12... | collective-permute-start | bytes 884744 | tf_op jit(solution)/shard_map/ppermute | solution.py:405

commit v3 on v2

--- a/solution.py
+++ b/solution.py
@@ -13,6 +13,18 @@
 LANES = 128
 HALF = 64
 MIB = 1 << 20
+RAW_LIMIT = 24
+ORDER = {
+    "c10": ("r1",),
+    "c30": ("p21", "x0",),
+    "c31": ("n", "p11",),
+    "e": ("l",),
+    "m": ("a",),
+    "n": ("w0", "w1", "w2",),
+    "p10": ("d",),
+    "p20": ("t",),
+    "p31": ("k",),
+}
 SMALL = pl.CostEstimate(flops=0, bytes_accessed=0, transcendentals=0)
 
 
@@ -92,59 +104,113 @@
     return lax.axis_index("expert"), dp // 2, lax.rem(dp, 2), lax.axis_index("tensor")
 
 
-def pack_kernel(experts, cap, routes, gates, tokens, cotangent, *refs):
-    outs, buffers, sems = refs[:-2], refs[-2], refs[-1]
-    messages, near, local = outs[:-2], outs[-2], outs[-1]
-    z, x, core, y = place()
-    rows = tokens.shape[1]
-    chunk = near.shape[1] // 2
-    steps = [(dx, h) for dx in (1, 0) for h in (0, 1)]
-    copies = []
-    for i, (dx, h) in enumerate(steps):
-        half = x if dx == 0 else 1 - x
-        column = pl.multiple_of((2 * half + (core if h == 0 else 1 - core)) * chunk, LANES)
-        for j, source in enumerate((tokens, cotangent)):
-            copy = pltpu.make_async_copy(
-                source.at[:, :, pl.ds(column, chunk)], buffers.at[i, j], sems.at[i, j]
-            )
-            copy.start()
-            copies.append(copy)
-    count = experts * cap
+def slots_of(route, weight, experts, cap):
+    rows = route[0].shape[1]
+    count = len(experts) * cap
     line = lax.broadcasted_iota(jnp.int32, (count, rows), 0)
-    ahead = jnp.zeros_like(line)
-    for k in range(1, experts):
-        ahead = ahead + (line >= k * cap).astype(jnp.int32)
-    slot = (line - ahead * cap).astype(jnp.float32)
-    expert = z + ahead
-    expert = jnp.where(expert >= experts, expert - experts, expert)
+    expert = jnp.full((count, rows), experts[0], jnp.int32)
+    slot = line
+    for i, other in enumerate(experts[1:], 1):
+        expert = jnp.where(line >= i * cap, other, expert)
+        slot = jnp.where(line >= i * cap, line - i * cap, slot)
     earlier = (
         lax.broadcasted_iota(jnp.int32, (rows, rows), 0)
         < lax.broadcasted_iota(jnp.int32, (rows, rows), 1)
     ).astype(jnp.bfloat16)
+    match = jnp.zeros((count, rows), jnp.float32)
+    named = jnp.zeros((count, rows), jnp.float32)
+    for r, w in zip(route, weight):
+        same = r == expert
+        match = match + jnp.where(same, 1.0, 0.0)
+        named = named + jnp.where(same, w, 0.0)
+    rank = jnp.dot(match.astype(jnp.bfloat16), earlier, preferred_element_type=jnp.float32)
+    placing = jnp.where(rank == slot.astype(jnp.float32), match, 0.0)
+    return placing.astype(jnp.bfloat16), jnp.sum(placing * named, axis=1, keepdims=True)
+
+
+def gate_lanes(columns):
+    blocks = []
+    for column in columns:
+        blocks += [jnp.broadcast_to(column, (column.shape[0], LANES)), jnp.zeros((column.shape[0], LANES), jnp.float32)]
+    return jnp.concatenate(blocks, axis=0).astype(jnp.bfloat16)
+
+
+def rows_of(value):
+    return [value[k : k + 1] for k in range(value.shape[0])]
+
+
+def column_of(x, core, dx, h, chunk):
+    half = x if dx == 0 else 1 - x
+    return pl.multiple_of((2 * half + (core if h == 0 else 1 - core)) * chunk, LANES)
+
+
+def raw_kernel(routes, gates, tokens, cotangent, near, far, sems):
+    _, x, core, y = place()
+    rows = tokens.shape[1]
+    chunk = (far.shape[1] - LANES) // 2
+    copies = []
+    for dx, out in ((1, far), (0, near)):
+        for h in range(2):
+            for j, source in enumerate((tokens, cotangent)):
+                copies.append(
+                    pltpu.make_async_copy(
+                        source.at[y, :, pl.ds(column_of(x, core, dx, h, chunk), chunk)],
+                        out.at[pl.ds(j * rows, rows), pl.ds(h * chunk, chunk)],
+                        sems.at[dx, h, j],
+                    )
+                )
+                copies[-1].start()
+    line = lax.broadcasted_iota(jnp.int32, (2 * rows, rows), 0)
+    notes = jnp.zeros((2 * rows, rows), jnp.float32)
+    for i, row in enumerate(rows_of(routes[y].astype(jnp.float32)) + rows_of(gates[y].astype(jnp.float32))):
+        notes = jnp.where(line == i, row, notes)
+    notes = notes.astype(jnp.bfloat16)
+    for out in (far, near):
+        out[:, 2 * chunk :] = jnp.zeros((2 * rows, LANES), jnp.bfloat16)
+        out[:, 2 * chunk : 2 * chunk + rows] = notes
+    for copy in copies:
+        copy.wait()
+
+
+def raw_rows(routes, gates, tokens, cotangent, chunk):
+    one = jax.ShapeDtypeStruct((2 * tokens.shape[1], 2 * chunk + LANES), jnp.bfloat16)
+    return pl.pallas_call(
+        raw_kernel,
+        out_shape=[one, one],
+        in_specs=[VMEM, VMEM, HBM, HBM],
+        out_specs=[VMEM] * 2,
+        scratch_shapes=[pltpu.SemaphoreType.DMA((2, 2, 2))],
+        compiler_params=pltpu.CompilerParams(vmem_limit_bytes=RAW_LIMIT * MIB),
+        cost_estimate=SMALL,
+        name="raw_rows",
+    )(routes, gates, tokens, cotangent)
+
+
+def pack_kernel(cap, routes, gates, tokens, cotangent, *refs):
+    (next_near, next_far, near, local), (buffers, sems) = refs[:4], refs[4:]
+    z, x, core, y = place()
+    chunk = near.shape[1] // 2
+    steps = [(dx, h) for dx in (0, 1) for h in (0, 1)]
+    copies = []
+    for i, (dx, h) in enumerate(steps):
+        for j, source in enumerate((tokens, cotangent)):
+            copies.append(
+                pltpu.make_async_copy(
+                    source.at[:, :, pl.ds(column_of(x, core, dx, h, chunk), chunk)],
+                    buffers.at[i, j],
+                    sems.at[i, j],
+                )
+            )
+            copies[-1].start()
     sets, placings, slot_gates = (y, 1 - y), [], []
     for s in sets:
-        route, weight = routes[s], gates[s].astype(jnp.float32)
-        match = jnp.zeros(line.shape, jnp.float32)
-        named = jnp.zeros(line.shape, jnp.float32)
-        for k in range(route.shape[0]):
-            same = route[k : k + 1, :] == expert
-            match = match + jnp.where(same, 1.0, 0.0)
-            named = named + jnp.where(same, weight[k : k + 1, :], 0.0)
-        rank = jnp.dot(match.astype(jnp.bfloat16), earlier, preferred_element_type=jnp.float32)
-        placing = jnp.where(rank == slot, match, 0.0)
-        slot_gates.append(jnp.sum(placing * named, axis=1, keepdims=True))
-        placings.append(placing.astype(jnp.bfloat16))
-    few = -(-cap // 16) * 16
-    placings[1] = placings[1][:few]
-    blank = jnp.zeros((cap, LANES), jnp.float32)
-    extra = slice(2 * chunk, 2 * chunk + LANES)
-
-    def spread(which, k):
-        return jnp.broadcast_to(slot_gates[which][k * cap : (k + 1) * cap], (cap, LANES))
-
-    for k in range(1, experts):
-        messages[2 * (k - 1)][:, extra] = jnp.concatenate([spread(0, k), blank], axis=0).astype(jnp.bfloat16)
-    local[:, extra] = jnp.concatenate([spread(0, 0), blank, spread(1, 0), blank], axis=0).astype(jnp.bfloat16)
+        placing, gate = slots_of(
+            rows_of(routes[s]), rows_of(gates[s].astype(jnp.float32)), (z, z ^ 1), cap
+        )
+        placings.append(placing)
+        slot_gates.append(gate)
+    next_near[:, 2 * chunk :] = gate_lanes([slot_gates[0][cap:]])
+    local[:, 2 * chunk :] = gate_lanes([slot_gates[0][:cap], slot_gates[1][:cap]])
     for i, (dx, h) in enumerate(steps):
         copies[2 * i].wait()
         copies[2 * i + 1].wait()
@@ -154,28 +220,24 @@
             for s, placing in zip(sets, placings)
             for j in range(2)
         ]
-        for k in range(1, experts):
-            span = slice(k * cap, (k + 1) * cap)
-            messages[2 * (k - 1) + dx][:, here] = jnp.concatenate(
-                [found[0][span], found[1][span]], axis=0
-            ).astype(jnp.bfloat16)
+        (next_near if dx == 0 else next_far)[:, here] = jnp.concatenate(
+            [part[cap:] for part in found[:2]], axis=0
+        ).astype(jnp.bfloat16)
         (local if dx == 0 else near)[:, here] = jnp.concatenate(
             [part[:cap] for part in found], axis=0
         ).astype(jnp.bfloat16)
 
 
-def pack(routes, gates, tokens, cotangent, experts, cap, chunk):
+def pack(routes, gates, tokens, cotangent, cap, chunk):
     def shape(rows, gated):
         return jax.ShapeDtypeStruct((rows, 2 * chunk + (LANES if gated else 0)), jnp.bfloat16)
 
-    outs = [shape(2 * cap, dx == 0) for _ in range(1, experts) for dx in range(2)]
-    outs += [shape(4 * cap, False), shape(4 * cap, True)]
     sets, rows = tokens.shape[:2]
     return pl.pallas_call(
-        functools.partial(pack_kernel, experts, cap),
-        out_shape=outs,
+        functools.partial(pack_kernel, cap),
+        out_shape=[shape(2 * cap, True), shape(2 * cap, False), shape(4 * cap, False), shape(4 * cap, True)],
         in_specs=[VMEM, VMEM, HBM, HBM],
-        out_specs=[VMEM] * len(outs),
+        out_specs=[VMEM] * 4,
         scratch_shapes=[
             pltpu.VMEM((4, 2, sets, rows, chunk), jnp.bfloat16),
             pltpu.SemaphoreType.DMA((4, 2)),
@@ -184,6 +246,40 @@
         cost_estimate=SMALL,
         name="pack_rows",
     )(routes, gates, tokens, cotangent)
+
+
+def unpack_kernel(cap, top, gated, raw, mine, onward):
+    z = lax.axis_index("expert")
+    rows = raw.shape[0] // 2
+    chunk = (raw.shape[1] - LANES) // 2
+    notes = raw[:rows, 2 * chunk :].astype(jnp.float32)[:, :rows]
+    route = [notes[k : k + 1].astype(jnp.int32) for k in range(top)]
+    weight = [notes[top + k : top + k + 1] for k in range(top)]
+    placing, gate = slots_of(route, weight, (z, z ^ 1), cap)
+    if gated:
+        mine[:, 2 * chunk :] = gate_lanes([gate[:cap]])
+        onward[:, 2 * chunk :] = gate_lanes([gate[cap:]])
+    for h in range(2):
+        here = slice(h * chunk, (h + 1) * chunk)
+        found = [
+            jnp.dot(placing, raw[j * rows : (j + 1) * rows, here], preferred_element_type=jnp.float32)
+            for j in range(2)
+        ]
+        mine[:, here] = jnp.concatenate([part[:cap] for part in found], axis=0).astype(jnp.bfloat16)
+        onward[:, here] = jnp.concatenate([part[cap:] for part in found], axis=0).astype(jnp.bfloat16)
+
+
+def unpack(raw, cap, top, gated):
+    one = jax.ShapeDtypeStruct((2 * cap, raw.shape[1] - (0 if gated else LANES)), jnp.bfloat16)
+    return pl.pallas_call(
+        functools.partial(unpack_kernel, cap, top, gated),
+        out_shape=[one, one],
+        in_specs=[VMEM],
+        out_specs=[VMEM] * 2,
+        compiler_params=pltpu.CompilerParams(vmem_limit_bytes=16 * MIB),
+        cost_estimate=SMALL,
+        name="unpack_rows",
+    )(raw)
 
 
 def block_products(parts, weights, cap, put, width=256):
@@ -388,10 +484,6 @@
     )(dropped, *sources)
 
 
-def after(value, *others):
-    return lax.optimization_barrier((value,) + others)[0]
-
-
 def paired_body(tokens, cotangent, route_gate, routes, gate_weight, up_weight, down_weight, dropped):
     experts = lax.axis_size("expert")
     groups = lax.axis_size("dp")
@@ -407,66 +499,85 @@
     def over_tensor(value):
         return lax.ppermute(value, "tensor", [(0, 1), (1, 0)])
 
-    def ahead(value, k, dx):
+    def over_expert(value, bit, dx):
         return lax.ppermute(
             value,
             ("expert", "dp"),
             [
-                (e * groups + d, (e + k) % experts * groups + (d ^ (2 * dx)))
+                (e * groups + d, (e ^ bit) * groups + (d ^ (2 * dx)))
                 for e in range(experts)
                 for d in range(groups)
             ],
         )
 
-    *messages, near, local = pack(
-        jnp.swapaxes(routes, 1, 2), jnp.swapaxes(route_gate, 1, 2), tokens, cotangent, experts, cap, chunk
-    )
+    routes_in, gates_in = jnp.swapaxes(routes, 1, 2), jnp.swapaxes(route_gate, 1, 2)
     own = (gate_weight[0], up_weight[0], down_weight[0])
-    order = [(1, 0), (3, 0), (1, 1), (3, 1), (2, 1), (2, 0)]
-
-    def message(i):
-        k, dx = order[i]
-        return messages[2 * (k - 1) + dx]
-
-    came, passed = [None] * 6, [None] * 6
-
-    def send(i, *others):
-        came[i] = ahead(after(message(i), *others) if others else message(i), *order[i])
-
-    def hand_on(i, *others):
-        passed[i] = over_tensor(after(came[i], *others) if others else came[i])
-
-    other = tuple(over_core(weight) for weight in own)
-    weights = own + other
-    send(0)
-    send(1)
-    came_near = over_x(after(near, *other))
-    send(2, came[0])
     down = own[2].reshape(NBLK, HALF, chunk)
-    down_sent = pieces_call(send_pieces_kernel, 3, after(dropped, came[0]), down)
-    down_came = over_tensor(down_sent)
-    send(3, came[1])
-    hand_on(0, down_came)
-    hand_on(1)
-    terms = {}
-    sent, kept, gates = products([came_near], [local], weights, cap)
-    terms[0] = (kept, over_x(sent), gates)
-    send(4, came[2])
-    compact_down = pieces_call(keep_pieces_kernel, KEEP, dropped, down, down_came)
-    hand_on(2, compact_down)
-    sent, kept, gates = products([came[2], passed[2]], [came[0], passed[0]], weights, cap)
-    terms[1] = (kept, over_x(after(sent, terms[0][1])), gates)
-    send(5, came[3])
-    hand_on(3)
-    sent, kept, gates = products([came[3], passed[3]], [came[1], passed[1]], weights, cap)
-    terms[3] = (kept, over_x(after(sent, terms[1][1])), gates)
-    hand_on(4)
-    sums = finish([terms[0], terms[1], terms[3]], cap)
-    (sent,) = products([came[4], passed[4]], [], weights, cap)
-    hand_on(5, sums)
-    totals = last(came[5], passed[5], weights, over_x(sent), sums, cap)
+    made = {}
+
+    def get(name):
+        if name not in made:
+            made[name] = make(name[0], name[1:])
+        return made[name]
+
+    def after(value, name):
+        others = tuple(get(one) for one in ORDER.get(name, ()))
+        return lax.optimization_barrier((value,) + others)[0] if others else value
+
+    def weights():
+        return own + tuple(get("w" + str(i)) for i in range(3))
+
+    def make(kind, rest):
+        name = kind + rest
+        if kind == "a":
+            return raw_rows(routes_in, gates_in, tokens, cotangent, chunk)
+        if kind == "m":
+            return pack(after(routes_in, name), gates_in, tokens, cotangent, cap, chunk)
+        if kind == "l":
+            return get("m")[3]
+        if kind == "n":
+            return over_x(after(get("m")[2], name))
+        if kind == "r":
+            return over_expert(after(get("a")[int(rest)], name), 2, int(rest))
+        if kind == "u":
+            return unpack(get("r" + rest), cap, routes.shape[2], rest == "0")
+        if kind == "c":
+            k, dx = rest
+            if k == "2":
+                return get("u" + dx)[0]
+            value = get("m")[int(dx)] if k == "1" else get("u" + dx)[1]
+            return over_expert(after(value, name), 1, int(dx) if k == "1" else 0)
+        if kind == "p":
+            return over_tensor(after(get("c" + rest), name))
+        if kind == "f":
+            if rest == "0":
+                return products([get("n")], [get("l")], weights(), cap)
+            sent = [get("c" + rest + "1"), get("p" + rest + "1")]
+            kept = [get("c" + rest + "0"), get("p" + rest + "0")] if rest == "1" else []
+            return products(sent, kept, weights(), cap)
+        if kind == "v":
+            return last(get("c20"), get("p20"), weights(), get("x2"), get("t"), cap)
+        if kind == "w":
+            return over_core(after(own[int(rest)], name))
+        if kind == "f":
+            return products_of(rest)
+        if kind == "s":
+            return get("f" + rest)[0]
+        if kind == "x":
+            return over_x(after(get("s" + rest), name))
+        if kind == "e":
+            return pieces_call(send_pieces_kernel, 3, after(dropped, name), down)
+        if kind == "d":
+            return over_tensor(after(get("e"), name))
+        if kind == "k":
+            return pieces_call(keep_pieces_kernel, KEEP, dropped, down, get("d"))
+        if kind == "t":
+            return finish([(get("f" + g)[1], get("x" + g), get("f" + g)[2]) for g in "01"], cap)
+        raise ValueError(name)
+
+    totals = last(get("c30"), get("p30"), weights(), get("x3"), get("v"), cap)
     saliency = jnp.abs(lax.psum(totals, "dp"))[:, None, :]
-    return saliency, compact_down.reshape(1, KEEP * HALF, chunk)
+    return saliency, get("k").reshape(1, KEEP * HALF, chunk)
 
 
 def solution(mesh):

time: 115 us -> 101 us (0.88)
  waiting for transfers between devices: 57.4 us -> 43.5 us
  starting transfers between devices: 26.3 us -> 23.2 us
  Pallas kernels: 20.1 us -> 23 us
    ppermute x5, waiting for transfers between devices: 18.9 us -> 9.93 us  [over_x(): return lax.ppermute(value, 'dp', [(d, d ^ 2) for d in range(groups)])]
    ppermute x6, starting transfers between devices: 13.3 us -> 9.47 us  [over_expert(): lax.ppermute(value, ('expert', 'dp'), [(e * groups + d, (e ^ bit) * group...]
    ppermute x7, waiting for transfers between devices: 3.34 us -> 0.02 us  [over_tensor(): return lax.ppermute(value, 'tensor', [(0, 1), (1, 0)])]
    pallas_call x1 -> x2, Pallas kernels: 2.43 us -> 4.78 us  [last(): pl.pallas_call(functools.partial(last_kernel, cap, width), out_shape=jax....]
    ppermute x6, waiting for transfers between devices: 35.2 us -> 33.5 us  [over_expert(): lax.ppermute(value, ('expert', 'dp'), [(e * groups + d, (e ^ bit) * group...]
    pallas_call x1 -> x4, Pallas kernels: 2.08 us -> 3.11 us  [the longest x1 1.85 us: pack(): pl.pallas_call(functools.partial(pack_kernel, cap), out_shape=[shape(2 *...]
  transfers between devices with their start and end apart: 21 -> 21, of which waited for: 10 -> 9; matrix products, arithmetic and copies ran while one was open for 0% -> 0% of each run, Pallas kernels for 15% -> 20%
where the time goes in v3:
time: 101 us
  waiting for transfers between devices  43.5 us (43%)
  starting transfers between devices  23.2 us (23%)
  Pallas kernels  23 us (23%)
  blocking collectives  5.67 us (6%)
  local copies, waits for them, and re-layouts  4.33 us (4%)
    ppermute x6, waiting for transfers between devices, over_expert(): lax.ppermute(value, ('expert', 'dp'), [(e * groups + d, (e ^ bit) * group...  33.5 us
    pallas_call x4, Pallas kernels, products(): pl.pallas_call(functools.partial(products_kernel, cap, width, len(sent),...  10.1 us
    ppermute x5, waiting for transfers between devices, over_x(): return lax.ppermute(value, 'dp', [(d, d ^ 2) for d in range(groups)])  9.93 us
    ppermute x6, starting transfers between devices, over_expert(): lax.ppermute(value, ('expert', 'dp'), [(e * groups + d, (e ^ bit) * group...  9.47 us
    ppermute x7, starting transfers between devices, over_tensor(): return lax.ppermute(value, 'tensor', [(0, 1), (1, 0)])  7.33 us
    psum x1, blocking collectives, paired_body(): saliency = jnp.abs(lax.psum(totals, 'dp'))[:, None, :]  5.67 us
    ppermute x5, starting transfers between devices, over_x(): return lax.ppermute(value, 'dp', [(d, d ^ 2) for d in range(groups)])  5.42 us
    pallas_call x2, Pallas kernels, pieces_call(): pl.pallas_call(kernel, out_shape=jax.ShapeDtypeStruct((count,) + sources[...  4.88 us
  transfers between devices with their start and end apart: 21, of which 9 were waited for; matrix products, arithmetic and copies ran while one was open for 0% of the time, Pallas kernels for 20%

profile of v3, /device:TPU:0, one launch (start us, length us, event | category | flops | bytes accessed | tf_op | source)
XLA Modules:
  0.0 100.5 jit_solution(18159826002568312831)
XLA Ops:
  1.7 1.2 %copy-done.3 = bf16[2,32,7168]{2,1,0:T(8,128)(2,1)S(1)} copy-done((bf16[2,32,7168]{2,1,0:T(8,128)(2,1)S(1)}, bf16[2,32,7168]{2,1,0:T(8,128)(2,1)}, u32[]{:S(2)}) %copy-start.3) | copy-done | bytes 917528
  2.8 1.2 %copy-done.4 = bf16[2,32,7168]{2,1,0:T(8,128)(2,1)S(1)} copy-done((bf16[2,32,7168]{2,1,0:T(8,128)(2,1)S(1)}, bf16[2,32,7168]{2,1,0:T(8,128)(2,1)}, u32[]{:S(2)}) %copy-start.4) | copy-done | bytes 917528
  5.8 4.7 %collective-permute-start.1 = (bf16[64,3712]{1,0:T(8,128)(2,1)S(1)}, bf16[64,3712]{1,0:T(8,128)(2,1)S(1)}, u32[]{:S(2)}, u32[]{:S(2)}) collective-permute-start(bf16[64,3712]{1,0:T(8,128)(2,1)S(1)} %get-tuple-element.29), channel_id=1, source_target_pairs={{0,20},{2,22},{4,16},{6,18},{8,28},{10,30},{12,24},{14,26},{16,4},... | collective-permute-start | bytes 1425416 | tf_op jit(solution)/shard_map/ppermute | solution.py:503
  10.4 1.9 %pack_rows.1 = (bf16[48,3712]{1,0:T(8,128)(2,1)S(1)}, bf16[48,3584]{1,0:T(8,128)(2,1)S(1)}, bf16[96,3584]{1,0:T(8,128)(2,1)S(1)}, bf16[96,3712]{1,0:T(8,128)(2,1)S(1)}) custom-call(s32[2,2,32]{2,1,0:T(2,128)S(1)} %bitcast.33, bf16[2,2,32]{2,1,0:T(2,128)(2,1)S(1)} %bitcast.35, bf16[2,32,7168]{2,1,0:T(8,128)(2,1)S(1)} %copy-done.3, ...), custom_call_target="tpu_custom_call" | custom-call | tf_op jit(solution)/shard_map/pack_rows/pallas_call | solution.py:236
  12.3 1.5 %kept_rows.2 = bf16[3,64,1792]{2,1,0:T(8,128)(2,1)S(1)} custom-call(s32[1,3]{1,0:T(1,128)S(1)} %copy-done.7, bf16[8,64,1792]{2,1,0:T(8,128)(2,1)S(1)} %bitcast.10), custom_call_target="tpu_custom_call" | custom-call | tf_op jit(solution)/shard_map/kept_rows/pallas_call | solution.py:475
  13.8 1.6 %collective-permute-start.13 = (bf16[3,64,1792]{2,1,0:T(8,128)(2,1)S(1)}, bf16[3,64,1792]{2,1,0:T(8,128)(2,1)S(1)}, u32[]{:S(2)}, u32[]{:S(2)}) collective-permute-start(bf16[3,64,1792]{2,1,0:T(8,128)(2,1)S(1)} %kept_rows.2), channel_id=1, source_target_pairs={{0,1},{1,0},{2,3},{3,2},{4,5},{5,4},{6,7},{7,6},{8,9},{9,8},{10,11... | collective-permute-start | bytes 2064392 | tf_op jit(solution)/shard_map/ppermute | solution.py:500
  16.0 2.5 %collective-permute-start.10 = (bf16[48,3584]{1,0:T(8,128)(2,1)S(1)}, bf16[48,3584]{1,0:T(8,128)(2,1)S(1)}, u32[]{:S(2)}, u32[]{:S(2)}) collective-permute-start(bf16[48,3584]{1,0:T(8,128)(2,1)S(1)} %get-tuple-element.38), channel_id=1, source_target_pairs={{0,12},{2,14},{4,8},{6,10},{8,4},{10,6},{12,0},{14,2},{16,28},{18,... | collective-permute-start | bytes 1032200 | tf_op jit(solution)/shard_map/ppermute | solution.py:503
  18.5 13.7 %collective-permute-done.1.raw = bf16[64,3712]{1,0:T(8,128)(2,1)S(1)} collective-permute-done((bf16[64,3712]{1,0:T(8,128)(2,1)S(1)}, bf16[64,3712]{1,0:T(8,128)(2,1)S(1)}, u32[]{:S(2)}, u32[]{:S(2)}) %collective-permute-start.1) | collective-permute-done | bytes 475168 | tf_op jit(solution)/shard_map/ppermute | solution.py:503
  32.9 2.9 %collective-permute-done.10.refs_0_ = bf16[48,3584]{1,0:T(8,128)(2,1)S(1)} collective-permute-done((bf16[48,3584]{1,0:T(8,128)(2,1)S(1)}, bf16[48,3584]{1,0:T(8,128)(2,1)S(1)}, u32[]{:S(2)}, u32[]{:S(2)}) %collective-permute-start.10) | collective-permute-done | bytes 344096 | tf_op jit(solution)/shard_map/ppermute | solution.py:503
  36.2 1.7 %collective-permute-start = (bf16[64,3712]{1,0:T(8,128)(2,1)S(1)}, bf16[64,3712]{1,0:T(8,128)(2,1)S(1)}, u32[]{:S(2)}, u32[]{:S(2)}) collective-permute-start(bf16[64,3712]{1,0:T(8,128)(2,1)S(1)} %get-tuple-element.27), channel_id=1, source_target_pairs={{0,16},{2,18},{4,20},{6,22},{8,24},{10,26},{12,28},{14,30},{16,0},... | collective-permute-start | bytes 1425416 | tf_op jit(solution)/shard_map/ppermute | solution.py:503
  38.9 10.6 %collective-permute-done.16.refs_2_ = bf16[48,3712]{1,0:T(8,128)(2,1)S(1)} collective-permute-done((bf16[48,3712]{1,0:T(8,128)(2,1)S(1)}, bf16[48,3712]{1,0:T(8,128)(2,1)S(1)}, u32[]{:S(2)}, u32[]{:S(2)}) %collective-permute-start.16) | collective-permute-done | bytes 356384 | tf_op jit(solution)/shard_map/ppermute | solution.py:503
  50.0 2.7 %partial_products.4 = (f32[48,1536]{1,0:T(8,128)S(1)}, f32[48,1536]{1,0:T(8,128)S(1)}, f32[48,128]{1,0:T(8,128)S(1)}) custom-call(bf16[96,3584]{1,0:T(8,128)(2,1)S(1)} %collective-permute-done.6.refs_0_, bf16[96,3712]{1,0:T(8,128)(2,1)S(1)} %get-tuple-element.34.refs_1_, bf16[1792,512]{1,0:T(8,128)(2,1)S(1)} %bitcast.19, bf16[1792,512]{1,0:T(8,128)(2,1)S(1)} %bitcast.26, ...), custom_call_target="tpu_custom_call" | custom-call | tf_op jit(solution)/shard_map/partial_products/pallas_call | solution.py:338
  52.7 1.3 %collective-permute-start.7 = (f32[48,1536]{1,0:T(8,128)S(1)}, f32[48,1536]{1,0:T(8,128)S(1)}, u32[]{:S(2)}, u32[]{:S(2)}) collective-permute-start(f32[48,1536]{1,0:T(8,128)S(1)} %get-tuple-element.35), channel_id=1, source_target_pairs={{0,4},{2,6},{4,0},{6,2},{1,5},{3,7},{5,1},{7,3},{8,12},{10,14},{12... | collective-permute-start | bytes 884744 | tf_op jit(solution)/shard_map/ppermute | solution.py:497
  54.0 4.6 %collective-permute-done.raw = bf16[64,3712]{1,0:T(8,128)(2,1)S(1)} collective-permute-done((bf16[64,3712]{1,0:T(8,128)(2,1)S(1)}, bf16[64,3712]{1,0:T(8,128)(2,1)S(1)}, u32[]{:S(2)}, u32[]{:S(2)}) %collective-permute-start) | collective-permute-done | bytes 475168 | tf_op jit(solution)/shard_map/ppermute | solution.py:503
  59.1 1.2 %collective-permute-done.7.refs_1_ = f32[48,1536]{1,0:T(8,128)S(1)} collective-permute-done((f32[48,1536]{1,0:T(8,128)S(1)}, f32[48,1536]{1,0:T(8,128)S(1)}, u32[]{:S(2)}, u32[]{:S(2)}) %collective-permute-start.7) | collective-permute-done | bytes 294944 | tf_op jit(solution)/shard_map/ppermute | solution.py:497
  60.3 2.7 %partial_products.6 = (f32[48,1536]{1,0:T(8,128)S(1)}, f32[48,1536]{1,0:T(8,128)S(1)}, f32[48,128]{1,0:T(8,128)S(1)}) custom-call(bf16[48,3584]{1,0:T(8,128)(2,1)S(1)} %collective-permute-done.10.refs_0_, bf16[48,3584]{1,0:T(8,128)(2,1)S(1)} %collective-permute-done.11.refs_1_, bf16[48,3712]{1,0:T(8,128)(2,1)S(1)} %collective-permute-done.16.refs_2_, ...), custom_call_target="tpu_custom_call" | custom-call | tf_op jit(solution)/shard_map/partial_products/pallas_call | solution.py:338
  63.0 1.0 %collective-permute-start.18 = (f32[48,1536]{1,0:T(8,128)S(1)}, f32[48,1536]{1,0:T(8,128)S(1)}, u32[]{:S(2)}, u32[]{:S(2)}) collective-permute-start(f32[48,1536]{1,0:T(8,128)S(1)} %get-tuple-element.49), channel_id=1, source_target_pairs={{0,4},{2,6},{4,0},{6,2},{1,5},{3,7},{5,1},{7,3},{8,12},{10,14},{12... | collective-permute-start | bytes 884744 | tf_op jit(solution)/shard_map/ppermute | solution.py:497
  64.0 3.4 %kept_rows.3 = bf16[5,64,1792]{2,1,0:T(8,128)(2,1)} custom-call(s32[1,3]{1,0:T(1,128)S(1)} %copy-done.7, bf16[8,64,1792]{2,1,0:T(8,128)(2,1)S(1)} %bitcast.13, bf16[3,64,1792]{2,1,0:T(8,128)(2,1)S(1)} %collective-permute-done.13.came), custom_call_target="tpu_custom_call" | custom-call | tf_op jit(solution)/shard_map/kept_rows/pallas_call | solution.py:475
  67.4 1.1 %collective-permute-start.14 = (bf16[48,3584]{1,0:T(8,128)(2,1)S(1)}, bf16[48,3584]{1,0:T(8,128)(2,1)S(1)}, u32[]{:S(2)}, u32[]{:S(2)}) collective-permute-start(bf16[48,3584]{1,0:T(8,128)(2,1)S(1)} %collective-permute-done.12.refs_0_), channel_id=1, source_target_pairs={{0,1},{1,0},{2,3},{3,2},{4,5},{5,4},{6,7},{7,6},{8,9},{9,8},{10,11... | collective-permute-start | bytes 1032200 | tf_op jit(solution)/shard_map/ppermute | solution.py:500
  68.5 1.2 %collective-permute-done.18.refs_4_ = f32[48,1536]{1,0:T(8,128)S(1)} collective-permute-done((f32[48,1536]{1,0:T(8,128)S(1)}, f32[48,1536]{1,0:T(8,128)S(1)}, u32[]{:S(2)}, u32[]{:S(2)}) %collective-permute-start.18) | collective-permute-done | bytes 294944 | tf_op jit(solution)/shard_map/ppermute | solution.py:497
  69.9 1.9 %collective-permute-start.19 = (bf16[48,3712]{1,0:T(8,128)(2,1)S(1)}, bf16[48,3712]{1,0:T(8,128)(2,1)S(1)}, u32[]{:S(2)}, u32[]{:S(2)}) collective-permute-start(bf16[48,3712]{1,0:T(8,128)(2,1)S(1)} %get-tuple-element.51.mine), channel_id=1, source_target_pairs={{0,1},{1,0},{2,3},{3,2},{4,5},{5,4},{6,7},{7,6},{8,9},{9,8},{10,11... | collective-permute-start | bytes 1069064 | tf_op jit(solution)/shard_map/ppermute | solution.py:500
  71.8 1.7 %collective-permute-done.8.mine = bf16[48,3712]{1,0:T(8,128)(2,1)S(1)} collective-permute-done((bf16[48,3712]{1,0:T(8,128)(2,1)S(1)}, bf16[48,3712]{1,0:T(8,128)(2,1)S(1)}, u32[]{:S(2)}, u32[]{:S(2)}) %collective-permute-start.8) | collective-permute-done | bytes 356384 | tf_op jit(solution)/shard_map/ppermute | solution.py:503
  73.5 1.2 %collective-permute-start.9 = (bf16[48,3712]{1,0:T(8,128)(2,1)S(1)}, bf16[48,3712]{1,0:T(8,128)(2,1)S(1)}, u32[]{:S(2)}, u32[]{:S(2)}) collective-permute-start(bf16[48,3712]{1,0:T(8,128)(2,1)S(1)} %collective-permute-done.8.mine), channel_id=1, source_target_pairs={{0,1},{1,0},{2,3},{3,2},{4,5},{5,4},{6,7},{7,6},{8,9},{9,8},{10,11... | collective-permute-start | bytes 1069064 | tf_op jit(solution)/shard_map/ppermute | solution.py:500
  74.7 2.3 %partial_products.7 = f32[48,1536]{1,0:T(8,128)S(1)} custom-call(bf16[48,3584]{1,0:T(8,128)(2,1)S(1)} %get-tuple-element.30.refs_0_, bf16[48,3584]{1,0:T(8,128)(2,1)S(1)} %collective-permute-done.2.refs_1_, bf16[1792,512]{1,0:T(8,128)(2,1)S(1)} %bitcast.21, bf16[1792,512]{1,0:T(8,128)(2,1)S(1)} %bitcast.28, bf16[512,1792]{1,0:T(8,128)(2,1)S(1)} %bitcast.14, ...), custom_call_target="tpu_custom_call" | custom-call | tf_op jit(solution)/shard_map/partial_products/pallas_call | solution.py:338
  77.1 1.5 %collective-permute-start.20 = (f32[48,1536]{1,0:T(8,128)S(1)}, f32[48,1536]{1,0:T(8,128)S(1)}, u32[]{:S(2)}, u32[]{:S(2)}) collective-permute-start(f32[48,1536]{1,0:T(8,128)S(1)} %partial_products.7), channel_id=1, source_target_pairs={{0,4},{2,6},{4,0},{6,2},{1,5},{3,7},{5,1},{7,3},{8,12},{10,14},{12... | collective-permute-start | bytes 884744 | tf_op jit(solution)/shard_map/ppermute | solution.py:497
  78.6 2.3 %partial_products.5 = f32[48,1536]{1,0:T(8,128)S(1)} custom-call(bf16[48,3584]{1,0:T(8,128)(2,1)S(1)} %collective-permute-done.12.refs_0_, bf16[48,3584]{1,0:T(8,128)(2,1)S(1)} %collective-permute-done.14.refs_1_, bf16[1792,512]{1,0:T(8,128)(2,1)S(1)} %bitcast.22, bf16[1792,512]{1,0:T(8,128)(2,1)S(1)} %bitcast.29, bf16[512,1792]{1,0:T(8,128)(2,1)S(1)} %bitcast.15, ...), custom_call_target="tpu_custom_call" | custom-call | tf_op jit(solution)/shard_map/partial_products/pallas_call | solution.py:338
  80.9 1.0 collective-permute-start.15
  81.9 5.1 %collective-permute-done.20.refs_6_ = f32[48,1536]{1,0:T(8,128)S(1)} collective-permute-done((f32[48,1536]{1,0:T(8,128)S(1)}, f32[48,1536]{1,0:T(8,128)S(1)}, u32[]{:S(2)}, u32[]{:S(2)}) %collective-permute-start.20) | collective-permute-done | bytes 294944 | tf_op jit(solution)/shard_map/ppermute | solution.py:497
  87.1 2.3 %last_products.2.refs_7_ = f32[2,512]{1,0:T(2,128)S(1)} custom-call(bf16[48,3712]{1,0:T(8,128)(2,1)S(1)} %get-tuple-element.51.mine, bf16[48,3712]{1,0:T(8,128)(2,1)S(1)} %collective-permute-done.19.other, bf16[1792,512]{1,0:T(8,128)(2,1)S(1)} %bitcast.23, bf16[1792,512]{1,0:T(8,128)(2,1)S(1)} %bitcast.30, bf16[512,1792]{1,0:T(8,128)(2,1)S(1)} %bitcast.16, ...), custom_call_target="tpu_custom_call" | custom-call | tf_op jit(solution)/shard_map/last_products/pallas_call | solution.py:411
  89.4 2.3 %collective-permute-done.15.refs_6_ = f32[48,1536]{1,0:T(8,128)S(1)} collective-permute-done((f32[48,1536]{1,0:T(8,128)S(1)}, f32[48,1536]{1,0:T(8,128)S(1)}, u32[]{:S(2)}, u32[]{:S(2)}) %collective-permute-start.15) | collective-permute-done | bytes 294944 | tf_op jit(solution)/shard_map/ppermute | solution.py:497
  91.8 2.4 %last_products.3 = f32[2,512]{1,0:T(2,128)S(1)} custom-call(bf16[48,3712]{1,0:T(8,128)(2,1)S(1)} %collective-permute-done.8.mine, bf16[48,3712]{1,0:T(8,128)(2,1)S(1)} %collective-permute-done.9.other, bf16[1792,512]{1,0:T(8,128)(2,1)S(1)} %bitcast.24, bf16[1792,512]{1,0:T(8,128)(2,1)S(1)} %bitcast.31, bf16[512,1792]{1,0:T(8,128)(2,1)S(1)} %bitcast.17, ...), custom_call_target="tpu_custom_call" | custom-call | tf_op jit(solution)/shard_map/last_products/pallas_call | solution.py:411
  94.2 5.7 %psum.7 = f32[2,512]{1,0:T(2,128)S(1)} all-reduce(f32[2,512]{1,0:T(2,128)S(1)} %last_products.3), channel_id=1, replica_groups=mesh['expert'=4,'dp'=4,'tensor'=2] {'dp'}, use_global_device_ids=true, to_apply=%region_0.0 | all-reduce | flops 1024 | bytes 8192 | tf_op jit(solution)/shard_map/psum | solution.py:579
  (42 shorter events, 7.2 us)
Async XLA Ops:
  0.6 14.8 %collective-permute-start.3 = (bf16[1792,512]{1,0:T(8,128)(2,1)}, bf16[1792,512]{1,0:T(8,128)(2,1)S(1)}, u32[]{:S(2)}, u32[]{:S(2)}) collective-permute-start(bf16[1792,512]{1,0:T(8,128)(2,1)} %bitcast.18), channel_id=1, source_target_pairs={{0,2},{2,0},{4,6},{6,4},{1,3},{3,1},{5,7},{7,5},{8,10},{10,8},{12,... | collective-permute-start | bytes 5505032 | tf_op jit(solution)/shard_map/ppermute | solution.py:494
  1.1 14.3 %collective-permute-start.4 = (bf16[1792,512]{1,0:T(8,128)(2,1)}, bf16[1792,512]{1,0:T(8,128)(2,1)S(1)}, u32[]{:S(2)}, u32[]{:S(2)}) collective-permute-start(bf16[1792,512]{1,0:T(8,128)(2,1)} %bitcast.25), channel_id=1, source_target_pairs={{0,2},{2,0},{4,6},{6,4},{1,3},{3,1},{5,7},{7,5},{8,10},{10,8},{12,... | collective-permute-start | bytes 5505032 | tf_op jit(solution)/shard_map/ppermute | solution.py:494
  1.2 14.2 %collective-permute-start.5 = (bf16[512,1792]{1,0:T(8,128)(2,1)}, bf16[512,1792]{1,0:T(8,128)(2,1)S(1)}, u32[]{:S(2)}, u32[]{:S(2)}) collective-permute-start(bf16[512,1792]{1,0:T(8,128)(2,1)} %bitcast.9), channel_id=1, source_target_pairs={{0,2},{2,0},{4,6},{6,4},{1,3},{3,1},{5,7},{7,5},{8,10},{10,8},{12,... | collective-permute-start | bytes 5505032 | tf_op jit(solution)/shard_map/ppermute | solution.py:494
  1.7 1.2 %copy-start.3 = (bf16[2,32,7168]{2,1,0:T(8,128)(2,1)S(1)}, bf16[2,32,7168]{2,1,0:T(8,128)(2,1)}, u32[]{:S(2)}) copy-start(bf16[2,32,7168]{2,1,0:T(8,128)(2,1)} %tokens.3) | copy-start | bytes 2752516
  2.8 1.2 %copy-start.4 = (bf16[2,32,7168]{2,1,0:T(8,128)(2,1)S(1)}, bf16[2,32,7168]{2,1,0:T(8,128)(2,1)}, u32[]{:S(2)}) copy-start(bf16[2,32,7168]{2,1,0:T(8,128)(2,1)} %cotangent.3) | copy-start | bytes 2752516
  4.0 0.7 copy-start.5
  4.7 0.7 copy-start.6
  5.4 6.9 %copy-start = (bf16[1,512,1792]{2,1,0:T(8,128)(2,1)S(1)}, bf16[1,512,1792]{2,1,0:T(8,128)(2,1)}, u32[]{:S(2)}) copy-start(bf16[1,512,1792]{2,1,0:T(8,128)(2,1)} %param.14) | copy-start | bytes 5505028
  5.4 6.9 %copy-start.7 = (s32[1,3]{1,0:T(1,128)S(1)}, s32[1,3]{1,0:T(1,128)}, u32[]{:S(2)}) copy-start(s32[1,3]{1,0:T(1,128)} %dropped.2) | copy-start | bytes 40
  5.8 26.5 %collective-permute-start.1 = (bf16[64,3712]{1,0:T(8,128)(2,1)S(1)}, bf16[64,3712]{1,0:T(8,128)(2,1)S(1)}, u32[]{:S(2)}, u32[]{:S(2)}) collective-permute-start(bf16[64,3712]{1,0:T(8,128)(2,1)S(1)} %get-tuple-element.29), channel_id=1, source_target_pairs={{0,20},{2,22},{4,16},{6,18},{8,28},{10,30},{12,24},{14,26},{16,4},... | collective-permute-start | bytes 1425416 | tf_op jit(solution)/shard_map/ppermute | solution.py:503
  10.4 39.6 %copy-start.2 = (bf16[1,1792,512]{2,1,0:T(8,128)(2,1)S(1)}, bf16[1,1792,512]{2,1,0:T(8,128)(2,1)}, u32[]{:S(2)}) copy-start(bf16[1,1792,512]{2,1,0:T(8,128)(2,1)} %param.13) | copy-start | bytes 5505028
  12.3 37.7 %copy-start.1 = (bf16[1,1792,512]{2,1,0:T(8,128)(2,1)S(1)}, bf16[1,1792,512]{2,1,0:T(8,128)(2,1)}, u32[]{:S(2)}) copy-start(bf16[1,1792,512]{2,1,0:T(8,128)(2,1)} %param.12) | copy-start | bytes 5505028
  13.8 24.5 %collective-permute-start.13 = (bf16[3,64,1792]{2,1,0:T(8,128)(2,1)S(1)}, bf16[3,64,1792]{2,1,0:T(8,128)(2,1)S(1)}, u32[]{:S(2)}, u32[]{:S(2)}) collective-permute-start(bf16[3,64,1792]{2,1,0:T(8,128)(2,1)S(1)} %kept_rows.2), channel_id=1, source_target_pairs={{0,1},{1,0},{2,3},{3,2},{4,5},{5,4},{6,7},{7,6},{8,9},{9,8},{10,11... | collective-permute-start | bytes 2064392 | tf_op jit(solution)/shard_map/ppermute | solution.py:500
  15.4 34.6 %collective-permute-start.6 = (bf16[96,3584]{1,0:T(8,128)(2,1)S(1)}, bf16[96,3584]{1,0:T(8,128)(2,1)S(1)}, u32[]{:S(2)}, u32[]{:S(2)}) collective-permute-start(bf16[96,3584]{1,0:T(8,128)(2,1)S(1)} %get-tuple-element.33), channel_id=1, source_target_pairs={{0,4},{2,6},{4,0},{6,2},{1,5},{3,7},{5,1},{7,3},{8,12},{10,14},{12... | collective-permute-start | bytes 2064392 | tf_op jit(solution)/shard_map/ppermute | solution.py:497
  16.0 19.7 %collective-permute-start.10 = (bf16[48,3584]{1,0:T(8,128)(2,1)S(1)}, bf16[48,3584]{1,0:T(8,128)(2,1)S(1)}, u32[]{:S(2)}, u32[]{:S(2)}) collective-permute-start(bf16[48,3584]{1,0:T(8,128)(2,1)S(1)} %get-tuple-element.38), channel_id=1, source_target_pairs={{0,12},{2,14},{4,8},{6,10},{8,4},{10,6},{12,0},{14,2},{16,28},{18,... | collective-permute-start | bytes 1032200 | tf_op jit(solution)/shard_map/ppermute | solution.py:503
  32.2 17.2 %collective-permute-start.16 = (bf16[48,3712]{1,0:T(8,128)(2,1)S(1)}, bf16[48,3712]{1,0:T(8,128)(2,1)S(1)}, u32[]{:S(2)}, u32[]{:S(2)}) collective-permute-start(bf16[48,3712]{1,0:T(8,128)(2,1)S(1)} %get-tuple-element.46), channel_id=1, source_target_pairs={{0,8},{2,10},{4,12},{6,14},{8,0},{10,2},{12,4},{14,6},{16,24},{18,... | collective-permute-start | bytes 1069064 | tf_op jit(solution)/shard_map/ppermute | solution.py:503
  35.8 18.2 %collective-permute-start.11 = (bf16[48,3584]{1,0:T(8,128)(2,1)S(1)}, bf16[48,3584]{1,0:T(8,128)(2,1)S(1)}, u32[]{:S(2)}, u32[]{:S(2)}) collective-permute-start(bf16[48,3584]{1,0:T(8,128)(2,1)S(1)} %collective-permute-done.10.refs_0_), channel_id=1, source_target_pairs={{0,1},{1,0},{2,3},{3,2},{4,5},{5,4},{6,7},{7,6},{8,9},{9,8},{10,11... | collective-permute-start | bytes 1032200 | tf_op jit(solution)/shard_map/ppermute | solution.py:500
  36.2 22.4 %collective-permute-start = (bf16[64,3712]{1,0:T(8,128)(2,1)S(1)}, bf16[64,3712]{1,0:T(8,128)(2,1)S(1)}, u32[]{:S(2)}, u32[]{:S(2)}) collective-permute-start(bf16[64,3712]{1,0:T(8,128)(2,1)S(1)} %get-tuple-element.27), channel_id=1, source_target_pairs={{0,16},{2,18},{4,20},{6,22},{8,24},{10,26},{12,28},{14,30},{16,0},... | collective-permute-start | bytes 1425416 | tf_op jit(solution)/shard_map/ppermute | solution.py:503
  38.3 20.8 %collective-permute-start.2 = (bf16[48,3584]{1,0:T(8,128)(2,1)S(1)}, bf16[48,3584]{1,0:T(8,128)(2,1)S(1)}, u32[]{:S(2)}, u32[]{:S(2)}) collective-permute-start(bf16[48,3584]{1,0:T(8,128)(2,1)S(1)} %get-tuple-element.30.refs_0_), channel_id=1, source_target_pairs={{0,1},{1,0},{2,3},{3,2},{4,5},{5,4},{6,7},{7,6},{8,9},{9,8},{10,11... | collective-permute-start | bytes 1032200 | tf_op jit(solution)/shard_map/ppermute | solution.py:500
  49.5 10.8 %collective-permute-start.17 = (bf16[48,3712]{1,0:T(8,128)(2,1)S(1)}, bf16[48,3712]{1,0:T(8,128)(2,1)S(1)}, u32[]{:S(2)}, u32[]{:S(2)}) collective-permute-start(bf16[48,3712]{1,0:T(8,128)(2,1)S(1)} %collective-permute-done.16.refs_2_), channel_id=1, source_target_pairs={{0,1},{1,0},{2,3},{3,2},{4,5},{5,4},{6,7},{7,6},{8,9},{9,8},{10,11... | collective-permute-start | bytes 1069064 | tf_op jit(solution)/shard_map/ppermute | solution.py:500
  52.7 7.6 %collective-permute-start.7 = (f32[48,1536]{1,0:T(8,128)S(1)}, f32[48,1536]{1,0:T(8,128)S(1)}, u32[]{:S(2)}, u32[]{:S(2)}) collective-permute-start(f32[48,1536]{1,0:T(8,128)S(1)} %get-tuple-element.35), channel_id=1, source_target_pairs={{0,4},{2,6},{4,0},{6,2},{1,5},{3,7},{5,1},{7,3},{8,12},{10,14},{12... | collective-permute-start | bytes 884744 | tf_op jit(solution)/shard_map/ppermute | solution.py:497
  54.0 13.4 %collective-permute-start.12 = (bf16[48,3584]{1,0:T(8,128)(2,1)S(1)}, bf16[48,3584]{1,0:T(8,128)(2,1)S(1)}, u32[]{:S(2)}, u32[]{:S(2)}) collective-permute-start(bf16[48,3584]{1,0:T(8,128)(2,1)S(1)} %get-tuple-element.39), channel_id=1, source_target_pairs={{0,8},{2,10},{4,12},{6,14},{8,0},{10,2},{12,4},{14,6},{16,24},{18,... | collective-permute-start | bytes 1032200 | tf_op jit(solution)/shard_map/ppermute | solution.py:503
  60.3 13.3 %collective-permute-start.8 = (bf16[48,3712]{1,0:T(8,128)(2,1)S(1)}, bf16[48,3712]{1,0:T(8,128)(2,1)S(1)}, u32[]{:S(2)}, u32[]{:S(2)}) collective-permute-start(bf16[48,3712]{1,0:T(8,128)(2,1)S(1)} %get-tuple-element.36), channel_id=1, source_target_pairs={{0,8},{2,10},{4,12},{6,14},{8,0},{10,2},{12,4},{14,6},{16,24},{18,... | collective-permute-start | bytes 1069064 | tf_op jit(solution)/shard_map/ppermute | solution.py:503
  63.0 6.8 %collective-permute-start.18 = (f32[48,1536]{1,0:T(8,128)S(1)}, f32[48,1536]{1,0:T(8,128)S(1)}, u32[]{:S(2)}, u32[]{:S(2)}) collective-permute-start(f32[48,1536]{1,0:T(8,128)S(1)} %get-tuple-element.49), channel_id=1, source_target_pairs={{0,4},{2,6},{4,0},{6,2},{1,5},{3,7},{5,1},{7,3},{8,12},{10,14},{12... | collective-permute-start | bytes 884744 | tf_op jit(solution)/shard_map/ppermute | solution.py:497
  67.4 11.2 %collective-permute-start.14 = (bf16[48,3584]{1,0:T(8,128)(2,1)S(1)}, bf16[48,3584]{1,0:T(8,128)(2,1)S(1)}, u32[]{:S(2)}, u32[]{:S(2)}) collective-permute-start(bf16[48,3584]{1,0:T(8,128)(2,1)S(1)} %collective-permute-done.12.refs_0_), channel_id=1, source_target_pairs={{0,1},{1,0},{2,3},{3,2},{4,5},{5,4},{6,7},{7,6},{8,9},{9,8},{10,11... | collective-permute-start | bytes 1032200 | tf_op jit(solution)/shard_map/ppermute | solution.py:500
  69.9 17.2 %collective-permute-start.19 = (bf16[48,3712]{1,0:T(8,128)(2,1)S(1)}, bf16[48,3712]{1,0:T(8,128)(2,1)S(1)}, u32[]{:S(2)}, u32[]{:S(2)}) collective-permute-start(bf16[48,3712]{1,0:T(8,128)(2,1)S(1)} %get-tuple-element.51.mine), channel_id=1, source_target_pairs={{0,1},{1,0},{2,3},{3,2},{4,5},{5,4},{6,7},{7,6},{8,9},{9,8},{10,11... | collective-permute-start | bytes 1069064 | tf_op jit(solution)/shard_map/ppermute | solution.py:500
  73.5 18.3 %collective-permute-start.9 = (bf16[48,3712]{1,0:T(8,128)(2,1)S(1)}, bf16[48,3712]{1,0:T(8,128)(2,1)S(1)}, u32[]{:S(2)}, u32[]{:S(2)}) collective-permute-start(bf16[48,3712]{1,0:T(8,128)(2,1)S(1)} %collective-permute-done.8.mine), channel_id=1, source_target_pairs={{0,1},{1,0},{2,3},{3,2},{4,5},{5,4},{6,7},{7,6},{8,9},{9,8},{10,11... | collective-permute-start | bytes 1069064 | tf_op jit(solution)/shard_map/ppermute | solution.py:500
  77.1 10.0 %collective-permute-start.20 = (f32[48,1536]{1,0:T(8,128)S(1)}, f32[48,1536]{1,0:T(8,128)S(1)}, u32[]{:S(2)}, u32[]{:S(2)}) collective-permute-start(f32[48,1536]{1,0:T(8,128)S(1)} %partial_products.7), channel_id=1, source_target_pairs={{0,4},{2,6},{4,0},{6,2},{1,5},{3,7},{5,1},{7,3},{8,12},{10,14},{12... | collective-permute-start | bytes 884744 | tf_op jit(solution)/shard_map/ppermute | solution.py:497
  80.9 10.8 %collective-permute-start.15 = (f32[48,1536]{1,0:T(8,128)S(1)}, f32[48,1536]{1,0:T(8,128)S(1)}, u32[]{:S(2)}, u32[]{:S(2)}) collective-permute-start(f32[48,1536]{1,0:T(8,128)S(1)} %partial_products.5), channel_id=1, source_target_pairs={{0,4},{2,6},{4,0},{6,2},{1,5},{3,7},{5,1},{7,3},{8,12},{10,14},{12... | collective-permute-start | bytes 884744 | tf_op jit(solution)/shard_map/ppermute | solution.py:497

commit v4 on v3

--- a/solution.py
+++ b/solution.py
@@ -14,16 +14,18 @@
 HALF = 64
 MIB = 1 << 20
 RAW_LIMIT = 24
+PACK_LIMIT = 24
+SENT = 3
 ORDER = {
     "c10": ("r1",),
     "c30": ("p21", "x0",),
-    "c31": ("n", "p11",),
-    "e": ("l",),
+    "c31": ("p11",),
     "m": ("a",),
     "n": ("w0", "w1", "w2",),
     "p10": ("d",),
-    "p20": ("t",),
+    "p30": ("p20", "s2", "t",),
     "p31": ("k",),
+    "x3": ("x2",),
 }
 SMALL = pl.CostEstimate(flops=0, bytes_accessed=0, transcendentals=0)
 
@@ -186,8 +188,8 @@
     )(routes, gates, tokens, cotangent)
 
 
-def pack_kernel(cap, routes, gates, tokens, cotangent, *refs):
-    (next_near, next_far, near, local), (buffers, sems) = refs[:4], refs[4:]
+def pack_kernel(cap, routes, gates, tokens, cotangent, dropped, down, *refs):
+    (next_near, next_far, near, local, pieces), (buffers, sems, piece_sems) = refs[:5], refs[5:]
     z, x, core, y = place()
     chunk = near.shape[1] // 2
     steps = [(dx, h) for dx in (0, 1) for h in (0, 1)]
@@ -202,6 +204,9 @@
                 )
             )
             copies[-1].start()
+    piece_copies = pieces_to_send(dropped, down, pieces, piece_sems)
+    for copy in piece_copies:
+        copy.start()
     sets, placings, slot_gates = (y, 1 - y), [], []
     for s in sets:
         placing, gate = slots_of(
@@ -226,26 +231,31 @@
         (local if dx == 0 else near)[:, here] = jnp.concatenate(
             [part[:cap] for part in found], axis=0
         ).astype(jnp.bfloat16)
-
-
-def pack(routes, gates, tokens, cotangent, cap, chunk):
+    for copy in piece_copies:
+        copy.wait()
+
+
+def pack(routes, gates, tokens, cotangent, dropped, down, cap):
     def shape(rows, gated):
         return jax.ShapeDtypeStruct((rows, 2 * chunk + (LANES if gated else 0)), jnp.bfloat16)
 
     sets, rows = tokens.shape[:2]
+    half, chunk = down.shape[1:]
+    outs = [shape(2 * cap, True), shape(2 * cap, False), shape(4 * cap, False), shape(4 * cap, True)]
     return pl.pallas_call(
         functools.partial(pack_kernel, cap),
-        out_shape=[shape(2 * cap, True), shape(2 * cap, False), shape(4 * cap, False), shape(4 * cap, True)],
-        in_specs=[VMEM, VMEM, HBM, HBM],
-        out_specs=[VMEM] * 4,
+        out_shape=outs + [jax.ShapeDtypeStruct((SENT, half, chunk), down.dtype)],
+        in_specs=[VMEM, VMEM, HBM, HBM, SMEM, HBM],
+        out_specs=[VMEM] * 5,
         scratch_shapes=[
             pltpu.VMEM((4, 2, sets, rows, chunk), jnp.bfloat16),
             pltpu.SemaphoreType.DMA((4, 2)),
+            pltpu.SemaphoreType.DMA((SENT,)),
         ],
-        compiler_params=pltpu.CompilerParams(vmem_limit_bytes=24 * MIB),
+        compiler_params=pltpu.CompilerParams(vmem_limit_bytes=PACK_LIMIT * MIB),
         cost_estimate=SMALL,
         name="pack_rows",
-    )(routes, gates, tokens, cotangent)
+    )(routes, gates, tokens, cotangent, dropped, down)
 
 
 def unpack_kernel(cap, top, gated, raw, mine, onward):
@@ -359,7 +369,7 @@
 
 def finish_kernel(cap, n, *refs):
     out = refs[-1]
-    inner = out.shape[1]
+    inner = out.shape[2]
     sums = [jnp.zeros((1, inner), jnp.float32)] * 2
     for g in range(n):
         kept, came, gates = refs[3 * g : 3 * g + 3]
@@ -369,14 +379,14 @@
         )
         for s in range(2):
             sums[s] = sums[s] + jnp.sum(terms[s * cap : (s + 1) * cap], axis=0, keepdims=True)
-    out[...] = in_set_order(*sums)
+    out[:, 0, :] = in_set_order(*sums)
 
 
 def finish(groups, cap):
     inner = groups[0][0].shape[1] // 3
     return pl.pallas_call(
         functools.partial(finish_kernel, cap, len(groups)),
-        out_shape=jax.ShapeDtypeStruct((2, inner), jnp.float32),
+        out_shape=jax.ShapeDtypeStruct((2, 1, inner), jnp.float32),
         in_specs=[VMEM] * (3 * len(groups)),
         out_specs=VMEM,
         compiler_params=pltpu.CompilerParams(vmem_limit_bytes=16 * MIB),
@@ -403,14 +413,14 @@
     block_products([mine, other], weights, cap, put, width)
     for at in range(0, inner, width):
         columns = slice(at, at + width)
-        out[:, columns] = before[:, columns] + in_set_order(found[0, at], found[1, at])
+        out[:, 0, columns] = before[:, 0, columns] + in_set_order(found[0, at], found[1, at])
 
 
 def last(mine, other, weights, came, before, cap, width=256):
     chunk, inner = weights[0].shape
     return pl.pallas_call(
         functools.partial(last_kernel, cap, width),
-        out_shape=jax.ShapeDtypeStruct((2, inner), jnp.float32),
+        out_shape=jax.ShapeDtypeStruct((2, 1, inner), jnp.float32),
         in_specs=[VMEM] * 10,
         out_specs=VMEM,
         compiler_params=pltpu.CompilerParams(vmem_limit_bytes=16 * MIB),
@@ -434,7 +444,7 @@
     return place_of, 2 * (NBLK // 2 - below)
 
 
-def send_pieces_kernel(dropped, down, out, sems):
+def pieces_to_send(dropped, down, out, sems):
     y = lax.axis_index("tensor")
     place_of, low_pieces = kept_pieces(dropped)
     first = jnp.where(y == 0, KEEP, low_pieces)
@@ -443,10 +453,7 @@
         piece = jnp.minimum(first + i, 2 * KEEP - 1)
         at = jnp.clip(place_of(piece) - NBLK * y, 0, NBLK - 1)
         copies.append(pltpu.make_async_copy(down.at[at], out.at[i], sems.at[i]))
-    for copy in copies:
-        copy.start()
-    for copy in copies:
-        copy.wait()
+    return copies
 
 
 def keep_pieces_kernel(dropped, down, came, out, sems):
@@ -471,17 +478,17 @@
         pltpu.make_async_copy(down.at[0], out.at[i], sems.at[i]).wait()
 
 
-def pieces_call(kernel, count, dropped, *sources):
+def keep_pieces(dropped, down, came):
     return pl.pallas_call(
-        kernel,
-        out_shape=jax.ShapeDtypeStruct((count,) + sources[0].shape[1:], sources[0].dtype),
-        in_specs=[SMEM] + [HBM] * len(sources),
+        keep_pieces_kernel,
+        out_shape=jax.ShapeDtypeStruct((KEEP,) + down.shape[1:], down.dtype),
+        in_specs=[SMEM, HBM, HBM],
         out_specs=VMEM,
-        scratch_shapes=[pltpu.SemaphoreType.DMA((count,))],
+        scratch_shapes=[pltpu.SemaphoreType.DMA((KEEP,))],
         compiler_params=pltpu.CompilerParams(vmem_limit_bytes=8 * MIB),
         cost_estimate=SMALL,
         name="kept_rows",
-    )(dropped, *sources)
+    )(dropped, down, came)
 
 
 def paired_body(tokens, cotangent, route_gate, routes, gate_weight, up_weight, down_weight, dropped):
@@ -532,7 +539,7 @@
         if kind == "a":
             return raw_rows(routes_in, gates_in, tokens, cotangent, chunk)
         if kind == "m":
-            return pack(after(routes_in, name), gates_in, tokens, cotangent, cap, chunk)
+            return pack(after(routes_in, name), gates_in, tokens, cotangent, dropped, down, cap)
         if kind == "l":
             return get("m")[3]
         if kind == "n":
@@ -565,18 +572,16 @@
             return get("f" + rest)[0]
         if kind == "x":
             return over_x(after(get("s" + rest), name))
-        if kind == "e":
-            return pieces_call(send_pieces_kernel, 3, after(dropped, name), down)
         if kind == "d":
-            return over_tensor(after(get("e"), name))
+            return over_tensor(after(get("m")[4], name))
         if kind == "k":
-            return pieces_call(keep_pieces_kernel, KEEP, dropped, down, get("d"))
+            return keep_pieces(dropped, down, get("d"))
         if kind == "t":
             return finish([(get("f" + g)[1], get("x" + g), get("f" + g)[2]) for g in "01"], cap)
         raise ValueError(name)
 
     totals = last(get("c30"), get("p30"), weights(), get("x3"), get("v"), cap)
-    saliency = jnp.abs(lax.psum(totals, "dp"))[:, None, :]
+    saliency = jnp.abs(lax.psum(totals, "dp"))
     return saliency, get("k").reshape(1, KEEP * HALF, chunk)
 
 

time: 101 us -> 95 us (0.941)
  waiting for transfers between devices: 43.5 us -> 37.4 us
    ppermute x5, waiting for transfers between devices: 9.93 us -> 3.81 us  [over_x(): return lax.ppermute(value, 'dp', [(d, d ^ 2) for d in range(groups)])]
    ppermute x7, waiting for transfers between devices: 0.02 us -> 1.14 us  [over_tensor(): return lax.ppermute(value, 'tensor', [(0, 1), (1, 0)])]
    ppermute x6, waiting for transfers between devices: 33.5 us -> 32.4 us  [over_expert(): lax.ppermute(value, ('expert', 'dp'), [(e * groups + d, (e ^ bit) * group...]
    unnamed x17 -> x16, local copies, waits for them, and re-layouts: 4.33 us -> 3.73 us
    pallas_call x3 -> x2, Pallas kernels: 6.73 us -> 6.75 us  [the longest x1 3.37 us: pack(): pl.pallas_call(functools.partial(pack_kernel, cap), out_shape=outs + [jax...]
  transfers between devices with their start and end apart: 21 -> 21, of which waited for: 9 -> 7; matrix products, arithmetic and copies ran while one was open for 0% -> 0% of each run, Pallas kernels for 20% -> 22%
where the time goes in v4:
time: 95 us; the launch traced here: 94.4 us
  waiting for transfers between devices  37.4 us (39%)
  starting transfers between devices  23.1 us (24%)
  Pallas kernels  23.1 us (24%)
  blocking collectives  5.67 us (6%)
  local copies, waits for them, and re-layouts  3.73 us (4%)
    ppermute x6, waiting for transfers between devices, over_expert(): lax.ppermute(value, ('expert', 'dp'), [(e * groups + d, (e ^ bit) * group...  32.4 us
    pallas_call x4, Pallas kernels, products(): pl.pallas_call(functools.partial(products_kernel, cap, width, len(sent),...  10.1 us
    ppermute x6, starting transfers between devices, over_expert(): lax.ppermute(value, ('expert', 'dp'), [(e * groups + d, (e ^ bit) * group...  9.47 us
    ppermute x7, starting transfers between devices, over_tensor(): return lax.ppermute(value, 'tensor', [(0, 1), (1, 0)])  6.51 us
    ppermute x5, starting transfers between devices, over_x(): return lax.ppermute(value, 'dp', [(d, d ^ 2) for d in range(groups)])  6.09 us
    psum x1, blocking collectives, paired_body(): saliency = jnp.abs(lax.psum(totals, 'dp'))  5.67 us
    pallas_call x2, Pallas kernels, last(): pl.pallas_call(functools.partial(last_kernel, cap, width), out_shape=jax....  4.86 us
    ppermute x5, waiting for transfers between devices, over_x(): return lax.ppermute(value, 'dp', [(d, d ^ 2) for d in range(groups)])  3.81 us
  transfers between devices with their start and end apart: 21, of which 7 were waited for; matrix products, arithmetic and copies ran while one was open for 0% of the time, Pallas kernels for 22%

profile of v4, /device:TPU:0, one launch (start us, length us, event | category | flops | bytes accessed | tf_op | source)
XLA Modules:
  0.0 94.4 jit_solution(4297599055522960081)
XLA Ops:
  1.7 1.2 %copy-done.3 = bf16[2,32,7168]{2,1,0:T(8,128)(2,1)S(1)} copy-done((bf16[2,32,7168]{2,1,0:T(8,128)(2,1)S(1)}, bf16[2,32,7168]{2,1,0:T(8,128)(2,1)}, u32[]{:S(2)}) %copy-start.3) | copy-done | bytes 917528
  2.9 1.2 %copy-done.4 = bf16[2,32,7168]{2,1,0:T(8,128)(2,1)S(1)} copy-done((bf16[2,32,7168]{2,1,0:T(8,128)(2,1)S(1)}, bf16[2,32,7168]{2,1,0:T(8,128)(2,1)}, u32[]{:S(2)}) %copy-start.4) | copy-done | bytes 917528
  4.0 0.7 copy-done.5
  4.7 0.7 copy-done.6
  5.8 4.7 %collective-permute-start.1 = (bf16[64,3712]{1,0:T(8,128)(2,1)S(1)}, bf16[64,3712]{1,0:T(8,128)(2,1)S(1)}, u32[]{:S(2)}, u32[]{:S(2)}) collective-permute-start(bf16[64,3712]{1,0:T(8,128)(2,1)S(1)} %get-tuple-element.30), channel_id=1, source_target_pairs={{0,20},{2,22},{4,16},{6,18},{8,28},{10,30},{12,24},{14,26},{16,4},... | collective-permute-start | bytes 1425416 | tf_op jit(solution)/shard_map/ppermute | solution.py:510
  10.5 3.4 %pack_rows.1 = (bf16[48,3712]{1,0:T(8,128)(2,1)S(1)}, bf16[48,3584]{1,0:T(8,128)(2,1)S(1)}, bf16[96,3584]{1,0:T(8,128)(2,1)S(1)}, bf16[96,3712]{1,0:T(8,128)(2,1)S(1)}, bf16[3,64,1792]{2,1,0:T(8,128)(2,1)S(1)}) custom-call(s32[2,2,32]{2,1,0:T(2,128)S(1)} %bitcast.31, bf16[2,2,32]{2,1,0:T(2,128)(2,1)S(1)} %bitcast.33, bf16[2,32,7168]{2,1,0:T(8,128)(2,1)S(1)} %copy-done.3, ...), custom_call_target="tpu_custom_call" | custom-call | tf_op jit(solution)/shard_map/pack_rows/pallas_call | solution.py:245
  13.8 1.6 %collective-permute-start.13 = (bf16[3,64,1792]{2,1,0:T(8,128)(2,1)S(1)}, bf16[3,64,1792]{2,1,0:T(8,128)(2,1)S(1)}, u32[]{:S(2)}, u32[]{:S(2)}) collective-permute-start(bf16[3,64,1792]{2,1,0:T(8,128)(2,1)S(1)} %get-tuple-element.44), channel_id=1, source_target_pairs={{0,1},{1,0},{2,3},{3,2},{4,5},{5,4},{6,7},{7,6},{8,9},{9,8},{10,11... | collective-permute-start | bytes 2064392 | tf_op jit(solution)/shard_map/ppermute | solution.py:507
  15.4 0.6 collective-permute-start.6
  16.0 2.5 %collective-permute-start.10 = (bf16[48,3584]{1,0:T(8,128)(2,1)S(1)}, bf16[48,3584]{1,0:T(8,128)(2,1)S(1)}, u32[]{:S(2)}, u32[]{:S(2)}) collective-permute-start(bf16[48,3584]{1,0:T(8,128)(2,1)S(1)} %get-tuple-element.41), channel_id=1, source_target_pairs={{0,12},{2,14},{4,8},{6,10},{8,4},{10,6},{12,0},{14,2},{16,28},{18,... | collective-permute-start | bytes 1032200 | tf_op jit(solution)/shard_map/ppermute | solution.py:510
  18.5 13.7 %collective-permute-done.1.raw = bf16[64,3712]{1,0:T(8,128)(2,1)S(1)} collective-permute-done((bf16[64,3712]{1,0:T(8,128)(2,1)S(1)}, bf16[64,3712]{1,0:T(8,128)(2,1)S(1)}, u32[]{:S(2)}, u32[]{:S(2)}) %collective-permute-start.1) | collective-permute-done | bytes 475168 | tf_op jit(solution)/shard_map/ppermute | solution.py:510
  32.3 0.6 collective-permute-start.12
  32.9 2.9 %collective-permute-done.10.refs_0_ = bf16[48,3584]{1,0:T(8,128)(2,1)S(1)} collective-permute-done((bf16[48,3584]{1,0:T(8,128)(2,1)S(1)}, bf16[48,3584]{1,0:T(8,128)(2,1)S(1)}, u32[]{:S(2)}, u32[]{:S(2)}) %collective-permute-start.10) | collective-permute-done | bytes 344096 | tf_op jit(solution)/shard_map/ppermute | solution.py:510
  36.2 1.7 %collective-permute-start = (bf16[64,3712]{1,0:T(8,128)(2,1)S(1)}, bf16[64,3712]{1,0:T(8,128)(2,1)S(1)}, u32[]{:S(2)}, u32[]{:S(2)}) collective-permute-start(bf16[64,3712]{1,0:T(8,128)(2,1)S(1)} %get-tuple-element.28), channel_id=1, source_target_pairs={{0,16},{2,18},{4,20},{6,22},{8,24},{10,26},{12,28},{14,30},{16,0},... | collective-permute-start | bytes 1425416 | tf_op jit(solution)/shard_map/ppermute | solution.py:510
  38.9 10.6 %collective-permute-done.12.refs_2_ = bf16[48,3712]{1,0:T(8,128)(2,1)S(1)} collective-permute-done((bf16[48,3712]{1,0:T(8,128)(2,1)S(1)}, bf16[48,3712]{1,0:T(8,128)(2,1)S(1)}, u32[]{:S(2)}, u32[]{:S(2)}) %collective-permute-start.12) | collective-permute-done | bytes 356384 | tf_op jit(solution)/shard_map/ppermute | solution.py:510
  50.0 2.7 %partial_products.4 = (f32[48,1536]{1,0:T(8,128)S(1)}, f32[48,1536]{1,0:T(8,128)S(1)}, f32[48,128]{1,0:T(8,128)S(1)}) custom-call(bf16[96,3584]{1,0:T(8,128)(2,1)S(1)} %collective-permute-done.6.refs_0_, bf16[96,3712]{1,0:T(8,128)(2,1)S(1)} %get-tuple-element.35.refs_1_, bf16[1792,512]{1,0:T(8,128)(2,1)S(1)} %bitcast.17, bf16[1792,512]{1,0:T(8,128)(2,1)S(1)} %bitcast.24, ...), custom_call_target="tpu_custom_call" | custom-call | tf_op jit(solution)/shard_map/partial_products/pallas_call | solution.py:348
  52.8 1.3 %collective-permute-start.7 = (f32[48,1536]{1,0:T(8,128)S(1)}, f32[48,1536]{1,0:T(8,128)S(1)}, u32[]{:S(2)}, u32[]{:S(2)}) collective-permute-start(f32[48,1536]{1,0:T(8,128)S(1)} %get-tuple-element.36), channel_id=1, source_target_pairs={{0,4},{2,6},{4,0},{6,2},{1,5},{3,7},{5,1},{7,3},{8,12},{10,14},{12... | collective-permute-start | bytes 884744 | tf_op jit(solution)/shard_map/ppermute | solution.py:504
  54.0 4.6 %collective-permute-done.raw = bf16[64,3712]{1,0:T(8,128)(2,1)S(1)} collective-permute-done((bf16[64,3712]{1,0:T(8,128)(2,1)S(1)}, bf16[64,3712]{1,0:T(8,128)(2,1)S(1)}, u32[]{:S(2)}, u32[]{:S(2)}) %collective-permute-start) | collective-permute-done | bytes 475168 | tf_op jit(solution)/shard_map/ppermute | solution.py:510
  59.1 1.5 %collective-permute-start.9 = (bf16[48,3712]{1,0:T(8,128)(2,1)S(1)}, bf16[48,3712]{1,0:T(8,128)(2,1)S(1)}, u32[]{:S(2)}, u32[]{:S(2)}) collective-permute-start(bf16[48,3712]{1,0:T(8,128)(2,1)S(1)} %get-tuple-element.38.mine), channel_id=1, source_target_pairs={{0,1},{1,0},{2,3},{3,2},{4,5},{5,4},{6,7},{7,6},{8,9},{9,8},{10,11... | collective-permute-start | bytes 1069064 | tf_op jit(solution)/shard_map/ppermute | solution.py:507
  60.6 2.7 %partial_products.6 = (f32[48,1536]{1,0:T(8,128)S(1)}, f32[48,1536]{1,0:T(8,128)S(1)}, f32[48,128]{1,0:T(8,128)S(1)}) custom-call(bf16[48,3584]{1,0:T(8,128)(2,1)S(1)} %collective-permute-done.10.refs_0_, bf16[48,3584]{1,0:T(8,128)(2,1)S(1)} %collective-permute-done.11.refs_1_, bf16[48,3712]{1,0:T(8,128)(2,1)S(1)} %collective-permute-done.12.refs_2_, ...), custom_call_target="tpu_custom_call" | custom-call | tf_op jit(solution)/shard_map/partial_products/pallas_call | solution.py:348
  63.3 1.6 %collective-permute-start.15 = (f32[48,1536]{1,0:T(8,128)S(1)}, f32[48,1536]{1,0:T(8,128)S(1)}, u32[]{:S(2)}, u32[]{:S(2)}) collective-permute-start(f32[48,1536]{1,0:T(8,128)S(1)} %get-tuple-element.47), channel_id=1, source_target_pairs={{0,4},{2,6},{4,0},{6,2},{1,5},{3,7},{5,1},{7,3},{8,12},{10,14},{12... | collective-permute-start | bytes 884744 | tf_op jit(solution)/shard_map/ppermute | solution.py:504
  64.9 3.4 %kept_rows.1 = bf16[5,64,1792]{2,1,0:T(8,128)(2,1)} custom-call(s32[1,3]{1,0:T(1,128)S(1)} %copy-done.7, bf16[8,64,1792]{2,1,0:T(8,128)(2,1)S(1)} %bitcast.11, bf16[3,64,1792]{2,1,0:T(8,128)(2,1)S(1)} %collective-permute-done.13.came), custom_call_target="tpu_custom_call" | custom-call | tf_op jit(solution)/shard_map/kept_rows/pallas_call | solution.py:482
  68.9 2.4 %partial_products.5 = f32[48,1536]{1,0:T(8,128)S(1)} custom-call(bf16[48,3584]{1,0:T(8,128)(2,1)S(1)} %get-tuple-element.31.refs_0_, bf16[48,3584]{1,0:T(8,128)(2,1)S(1)} %collective-permute-done.2.refs_1_, bf16[1792,512]{1,0:T(8,128)(2,1)S(1)} %bitcast.19, bf16[1792,512]{1,0:T(8,128)(2,1)S(1)} %bitcast.26, bf16[512,1792]{1,0:T(8,128)(2,1)S(1)} %bitcast.12, ...), custom_call_target="tpu_custom_call" | custom-call | tf_op jit(solution)/shard_map/partial_products/pallas_call | solution.py:348
  71.3 1.4 %collective-permute-start.19 = (f32[48,1536]{1,0:T(8,128)S(1)}, f32[48,1536]{1,0:T(8,128)S(1)}, u32[]{:S(2)}, u32[]{:S(2)}) collective-permute-start(f32[48,1536]{1,0:T(8,128)S(1)} %partial_products.5), channel_id=1, source_target_pairs={{0,4},{2,6},{4,0},{6,2},{1,5},{3,7},{5,1},{7,3},{8,12},{10,14},{12... | collective-permute-start | bytes 884744 | tf_op jit(solution)/shard_map/ppermute | solution.py:504
  72.8 0.7 collective-permute-done.8.mine
  73.5 1.2 %collective-permute-start.16 = (bf16[48,3712]{1,0:T(8,128)(2,1)S(1)}, bf16[48,3712]{1,0:T(8,128)(2,1)S(1)}, u32[]{:S(2)}, u32[]{:S(2)}) collective-permute-start(bf16[48,3712]{1,0:T(8,128)(2,1)S(1)} %collective-permute-done.8.mine), channel_id=1, source_target_pairs={{0,1},{1,0},{2,3},{3,2},{4,5},{5,4},{6,7},{7,6},{8,9},{9,8},{10,11... | collective-permute-start | bytes 1069064 | tf_op jit(solution)/shard_map/ppermute | solution.py:507
  74.8 1.1 %collective-permute-done.18.refs_1_ = bf16[48,3584]{1,0:T(8,128)(2,1)S(1)} collective-permute-done((bf16[48,3584]{1,0:T(8,128)(2,1)S(1)}, bf16[48,3584]{1,0:T(8,128)(2,1)S(1)}, u32[]{:S(2)}, u32[]{:S(2)}) %collective-permute-start.18) | collective-permute-done | bytes 344096 | tf_op jit(solution)/shard_map/ppermute | solution.py:507
  75.9 2.3 %partial_products.7 = f32[48,1536]{1,0:T(8,128)S(1)} custom-call(bf16[48,3584]{1,0:T(8,128)(2,1)S(1)} %collective-permute-done.17.refs_0_, bf16[48,3584]{1,0:T(8,128)(2,1)S(1)} %collective-permute-done.18.refs_1_, bf16[1792,512]{1,0:T(8,128)(2,1)S(1)} %bitcast.20, bf16[1792,512]{1,0:T(8,128)(2,1)S(1)} %bitcast.27, bf16[512,1792]{1,0:T(8,128)(2,1)S(1)} %bitcast.13, ...), custom_call_target="tpu_custom_call" | custom-call | tf_op jit(solution)/shard_map/partial_products/pallas_call | solution.py:348
  78.2 1.2 %collective-permute-start.20 = (f32[48,1536]{1,0:T(8,128)S(1)}, f32[48,1536]{1,0:T(8,128)S(1)}, u32[]{:S(2)}, u32[]{:S(2)}) collective-permute-start(f32[48,1536]{1,0:T(8,128)S(1)} %partial_products.7), channel_id=1, source_target_pairs={{0,4},{2,6},{4,0},{6,2},{1,5},{3,7},{5,1},{7,3},{8,12},{10,14},{12... | collective-permute-start | bytes 884744 | tf_op jit(solution)/shard_map/ppermute | solution.py:504
  79.4 2.4 %last_products.2.refs_7_ = f32[2,1,512]{2,1,0:T(1,128)S(1)} custom-call(bf16[48,3712]{1,0:T(8,128)(2,1)S(1)} %get-tuple-element.38.mine, bf16[48,3712]{1,0:T(8,128)(2,1)S(1)} %collective-permute-done.9.other, bf16[1792,512]{1,0:T(8,128)(2,1)S(1)} %bitcast.21, bf16[1792,512]{1,0:T(8,128)(2,1)S(1)} %bitcast.28, bf16[512,1792]{1,0:T(8,128)(2,1)S(1)} %bitcast.14, ...), custom_call_target="tpu_custom_call" | custom-call | tf_op jit(solution)/shard_map/last_products/pallas_call | solution.py:421
  81.8 3.8 %collective-permute-done.20.refs_6_ = f32[48,1536]{1,0:T(8,128)S(1)} collective-permute-done((f32[48,1536]{1,0:T(8,128)S(1)}, f32[48,1536]{1,0:T(8,128)S(1)}, u32[]{:S(2)}, u32[]{:S(2)}) %collective-permute-start.20) | collective-permute-done | bytes 294944 | tf_op jit(solution)/shard_map/ppermute | solution.py:504
  85.6 2.5 %last_products.3 = f32[2,1,512]{2,1,0:T(1,128)S(1)} custom-call(bf16[48,3712]{1,0:T(8,128)(2,1)S(1)} %collective-permute-done.8.mine, bf16[48,3712]{1,0:T(8,128)(2,1)S(1)} %collective-permute-done.16.other, bf16[1792,512]{1,0:T(8,128)(2,1)S(1)} %bitcast.22, bf16[1792,512]{1,0:T(8,128)(2,1)S(1)} %bitcast.29, bf16[512,1792]{1,0:T(8,128)(2,1)S(1)} %bitcast.15, ...), custom_call_target="tpu_custom_call" | custom-call | tf_op jit(solution)/shard_map/last_products/pallas_call | solution.py:421
  88.1 5.7 %psum.7 = f32[2,1,512]{2,1,0:T(1,128)S(1)} all-reduce(f32[2,1,512]{2,1,0:T(1,128)S(1)} %last_products.3), channel_id=1, replica_groups=mesh['expert'=4,'dp'=4,'tensor'=2] {'dp'}, use_global_device_ids=true, to_apply=%region_0.0 | all-reduce | flops 1024 | bytes 8192 | tf_op jit(solution)/shard_map/psum | solution.py:584
  (40 shorter events, 5.3 us)
Async XLA Ops:
  0.6 9.8 %copy-start = (bf16[1,512,1792]{2,1,0:T(8,128)(2,1)S(1)}, bf16[1,512,1792]{2,1,0:T(8,128)(2,1)}, u32[]{:S(2)}) copy-start(bf16[1,512,1792]{2,1,0:T(8,128)(2,1)} %param.14) | copy-start | bytes 5505028
  0.6 14.8 %collective-permute-start.3 = (bf16[1792,512]{1,0:T(8,128)(2,1)}, bf16[1792,512]{1,0:T(8,128)(2,1)S(1)}, u32[]{:S(2)}, u32[]{:S(2)}) collective-permute-start(bf16[1792,512]{1,0:T(8,128)(2,1)} %bitcast.16), channel_id=1, source_target_pairs={{0,2},{2,0},{4,6},{6,4},{1,3},{3,1},{5,7},{7,5},{8,10},{10,8},{12,... | collective-permute-start | bytes 5505032 | tf_op jit(solution)/shard_map/ppermute | solution.py:501
  1.2 14.3 %collective-permute-start.4 = (bf16[1792,512]{1,0:T(8,128)(2,1)}, bf16[1792,512]{1,0:T(8,128)(2,1)S(1)}, u32[]{:S(2)}, u32[]{:S(2)}) collective-permute-start(bf16[1792,512]{1,0:T(8,128)(2,1)} %bitcast.23), channel_id=1, source_target_pairs={{0,2},{2,0},{4,6},{6,4},{1,3},{3,1},{5,7},{7,5},{8,10},{10,8},{12,... | collective-permute-start | bytes 5505032 | tf_op jit(solution)/shard_map/ppermute | solution.py:501
  1.2 14.2 %collective-permute-start.5 = (bf16[512,1792]{1,0:T(8,128)(2,1)}, bf16[512,1792]{1,0:T(8,128)(2,1)S(1)}, u32[]{:S(2)}, u32[]{:S(2)}) collective-permute-start(bf16[512,1792]{1,0:T(8,128)(2,1)} %bitcast.7), channel_id=1, source_target_pairs={{0,2},{2,0},{4,6},{6,4},{1,3},{3,1},{5,7},{7,5},{8,10},{10,8},{12,... | collective-permute-start | bytes 5505032 | tf_op jit(solution)/shard_map/ppermute | solution.py:501
  1.7 1.2 %copy-start.3 = (bf16[2,32,7168]{2,1,0:T(8,128)(2,1)S(1)}, bf16[2,32,7168]{2,1,0:T(8,128)(2,1)}, u32[]{:S(2)}) copy-start(bf16[2,32,7168]{2,1,0:T(8,128)(2,1)} %tokens.3) | copy-start | bytes 2752516
  2.9 1.2 %copy-start.4 = (bf16[2,32,7168]{2,1,0:T(8,128)(2,1)S(1)}, bf16[2,32,7168]{2,1,0:T(8,128)(2,1)}, u32[]{:S(2)}) copy-start(bf16[2,32,7168]{2,1,0:T(8,128)(2,1)} %cotangent.3) | copy-start | bytes 2752516
  4.0 0.7 copy-start.5
  4.7 0.7 copy-start.6
  5.4 5.1 %copy-start.7 = (s32[1,3]{1,0:T(1,128)S(1)}, s32[1,3]{1,0:T(1,128)}, u32[]{:S(2)}) copy-start(s32[1,3]{1,0:T(1,128)} %dropped.3) | copy-start | bytes 40
  5.8 26.5 %collective-permute-start.1 = (bf16[64,3712]{1,0:T(8,128)(2,1)S(1)}, bf16[64,3712]{1,0:T(8,128)(2,1)S(1)}, u32[]{:S(2)}, u32[]{:S(2)}) collective-permute-start(bf16[64,3712]{1,0:T(8,128)(2,1)S(1)} %get-tuple-element.30), channel_id=1, source_target_pairs={{0,20},{2,22},{4,16},{6,18},{8,28},{10,30},{12,24},{14,26},{16,4},... | collective-permute-start | bytes 1425416 | tf_op jit(solution)/shard_map/ppermute | solution.py:510
  10.5 39.6 %copy-start.1 = (bf16[1,1792,512]{2,1,0:T(8,128)(2,1)S(1)}, bf16[1,1792,512]{2,1,0:T(8,128)(2,1)}, u32[]{:S(2)}) copy-start(bf16[1,1792,512]{2,1,0:T(8,128)(2,1)} %param.12) | copy-start | bytes 5505028
  10.5 39.6 %copy-start.2 = (bf16[1,1792,512]{2,1,0:T(8,128)(2,1)S(1)}, bf16[1,1792,512]{2,1,0:T(8,128)(2,1)}, u32[]{:S(2)}) copy-start(bf16[1,1792,512]{2,1,0:T(8,128)(2,1)} %param.13) | copy-start | bytes 5505028
  13.8 24.5 %collective-permute-start.13 = (bf16[3,64,1792]{2,1,0:T(8,128)(2,1)S(1)}, bf16[3,64,1792]{2,1,0:T(8,128)(2,1)S(1)}, u32[]{:S(2)}, u32[]{:S(2)}) collective-permute-start(bf16[3,64,1792]{2,1,0:T(8,128)(2,1)S(1)} %get-tuple-element.44), channel_id=1, source_target_pairs={{0,1},{1,0},{2,3},{3,2},{4,5},{5,4},{6,7},{7,6},{8,9},{9,8},{10,11... | collective-permute-start | bytes 2064392 | tf_op jit(solution)/shard_map/ppermute | solution.py:507
  15.4 34.6 %collective-permute-start.6 = (bf16[96,3584]{1,0:T(8,128)(2,1)S(1)}, bf16[96,3584]{1,0:T(8,128)(2,1)S(1)}, u32[]{:S(2)}, u32[]{:S(2)}) collective-permute-start(bf16[96,3584]{1,0:T(8,128)(2,1)S(1)} %get-tuple-element.34), channel_id=1, source_target_pairs={{0,4},{2,6},{4,0},{6,2},{1,5},{3,7},{5,1},{7,3},{8,12},{10,14},{12... | collective-permute-start | bytes 2064392 | tf_op jit(solution)/shard_map/ppermute | solution.py:504
  16.0 19.7 %collective-permute-start.10 = (bf16[48,3584]{1,0:T(8,128)(2,1)S(1)}, bf16[48,3584]{1,0:T(8,128)(2,1)S(1)}, u32[]{:S(2)}, u32[]{:S(2)}) collective-permute-start(bf16[48,3584]{1,0:T(8,128)(2,1)S(1)} %get-tuple-element.41), channel_id=1, source_target_pairs={{0,12},{2,14},{4,8},{6,10},{8,4},{10,6},{12,0},{14,2},{16,28},{18,... | collective-permute-start | bytes 1032200 | tf_op jit(solution)/shard_map/ppermute | solution.py:510
  32.3 17.2 %collective-permute-start.12 = (bf16[48,3712]{1,0:T(8,128)(2,1)S(1)}, bf16[48,3712]{1,0:T(8,128)(2,1)S(1)}, u32[]{:S(2)}, u32[]{:S(2)}) collective-permute-start(bf16[48,3712]{1,0:T(8,128)(2,1)S(1)} %get-tuple-element.43), channel_id=1, source_target_pairs={{0,8},{2,10},{4,12},{6,14},{8,0},{10,2},{12,4},{14,6},{16,24},{18,... | collective-permute-start | bytes 1069064 | tf_op jit(solution)/shard_map/ppermute | solution.py:510
  35.7 18.3 %collective-permute-start.11 = (bf16[48,3584]{1,0:T(8,128)(2,1)S(1)}, bf16[48,3584]{1,0:T(8,128)(2,1)S(1)}, u32[]{:S(2)}, u32[]{:S(2)}) collective-permute-start(bf16[48,3584]{1,0:T(8,128)(2,1)S(1)} %collective-permute-done.10.refs_0_), channel_id=1, source_target_pairs={{0,1},{1,0},{2,3},{3,2},{4,5},{5,4},{6,7},{7,6},{8,9},{9,8},{10,11... | collective-permute-start | bytes 1032200 | tf_op jit(solution)/shard_map/ppermute | solution.py:507
  36.2 22.4 %collective-permute-start = (bf16[64,3712]{1,0:T(8,128)(2,1)S(1)}, bf16[64,3712]{1,0:T(8,128)(2,1)S(1)}, u32[]{:S(2)}, u32[]{:S(2)}) collective-permute-start(bf16[64,3712]{1,0:T(8,128)(2,1)S(1)} %get-tuple-element.28), channel_id=1, source_target_pairs={{0,16},{2,18},{4,20},{6,22},{8,24},{10,26},{12,28},{14,30},{16,0},... | collective-permute-start | bytes 1425416 | tf_op jit(solution)/shard_map/ppermute | solution.py:510
  38.3 22.3 %collective-permute-start.2 = (bf16[48,3584]{1,0:T(8,128)(2,1)S(1)}, bf16[48,3584]{1,0:T(8,128)(2,1)S(1)}, u32[]{:S(2)}, u32[]{:S(2)}) collective-permute-start(bf16[48,3584]{1,0:T(8,128)(2,1)S(1)} %get-tuple-element.31.refs_0_), channel_id=1, source_target_pairs={{0,1},{1,0},{2,3},{3,2},{4,5},{5,4},{6,7},{7,6},{8,9},{9,8},{10,11... | collective-permute-start | bytes 1032200 | tf_op jit(solution)/shard_map/ppermute | solution.py:507
  49.5 11.2 %collective-permute-start.14 = (bf16[48,3712]{1,0:T(8,128)(2,1)S(1)}, bf16[48,3712]{1,0:T(8,128)(2,1)S(1)}, u32[]{:S(2)}, u32[]{:S(2)}) collective-permute-start(bf16[48,3712]{1,0:T(8,128)(2,1)S(1)} %collective-permute-done.12.refs_2_), channel_id=1, source_target_pairs={{0,1},{1,0},{2,3},{3,2},{4,5},{5,4},{6,7},{7,6},{8,9},{9,8},{10,11... | collective-permute-start | bytes 1069064 | tf_op jit(solution)/shard_map/ppermute | solution.py:507
  52.8 7.8 %collective-permute-start.7 = (f32[48,1536]{1,0:T(8,128)S(1)}, f32[48,1536]{1,0:T(8,128)S(1)}, u32[]{:S(2)}, u32[]{:S(2)}) collective-permute-start(f32[48,1536]{1,0:T(8,128)S(1)} %get-tuple-element.36), channel_id=1, source_target_pairs={{0,4},{2,6},{4,0},{6,2},{1,5},{3,7},{5,1},{7,3},{8,12},{10,14},{12... | collective-permute-start | bytes 884744 | tf_op jit(solution)/shard_map/ppermute | solution.py:504
  54.0 14.3 %collective-permute-start.17 = (bf16[48,3584]{1,0:T(8,128)(2,1)S(1)}, bf16[48,3584]{1,0:T(8,128)(2,1)S(1)}, u32[]{:S(2)}, u32[]{:S(2)}) collective-permute-start(bf16[48,3584]{1,0:T(8,128)(2,1)S(1)} %get-tuple-element.51), channel_id=1, source_target_pairs={{0,8},{2,10},{4,12},{6,14},{8,0},{10,2},{12,4},{14,6},{16,24},{18,... | collective-permute-start | bytes 1032200 | tf_op jit(solution)/shard_map/ppermute | solution.py:510
  59.1 13.8 %collective-permute-start.9 = (bf16[48,3712]{1,0:T(8,128)(2,1)S(1)}, bf16[48,3712]{1,0:T(8,128)(2,1)S(1)}, u32[]{:S(2)}, u32[]{:S(2)}) collective-permute-start(bf16[48,3712]{1,0:T(8,128)(2,1)S(1)} %get-tuple-element.38.mine), channel_id=1, source_target_pairs={{0,1},{1,0},{2,3},{3,2},{4,5},{5,4},{6,7},{7,6},{8,9},{9,8},{10,11... | collective-permute-start | bytes 1069064 | tf_op jit(solution)/shard_map/ppermute | solution.py:507
  60.6 12.9 %collective-permute-start.8 = (bf16[48,3712]{1,0:T(8,128)(2,1)S(1)}, bf16[48,3712]{1,0:T(8,128)(2,1)S(1)}, u32[]{:S(2)}, u32[]{:S(2)}) collective-permute-start(bf16[48,3712]{1,0:T(8,128)(2,1)S(1)} %get-tuple-element.37), channel_id=1, source_target_pairs={{0,8},{2,10},{4,12},{6,14},{8,0},{10,2},{12,4},{14,6},{16,24},{18,... | collective-permute-start | bytes 1069064 | tf_op jit(solution)/shard_map/ppermute | solution.py:510
  63.3 9.4 %collective-permute-start.15 = (f32[48,1536]{1,0:T(8,128)S(1)}, f32[48,1536]{1,0:T(8,128)S(1)}, u32[]{:S(2)}, u32[]{:S(2)}) collective-permute-start(f32[48,1536]{1,0:T(8,128)S(1)} %get-tuple-element.47), channel_id=1, source_target_pairs={{0,4},{2,6},{4,0},{6,2},{1,5},{3,7},{5,1},{7,3},{8,12},{10,14},{12... | collective-permute-start | bytes 884744 | tf_op jit(solution)/shard_map/ppermute | solution.py:504
  68.3 7.5 %collective-permute-start.18 = (bf16[48,3584]{1,0:T(8,128)(2,1)S(1)}, bf16[48,3584]{1,0:T(8,128)(2,1)S(1)}, u32[]{:S(2)}, u32[]{:S(2)}) collective-permute-start(bf16[48,3584]{1,0:T(8,128)(2,1)S(1)} %collective-permute-done.17.refs_0_), channel_id=1, source_target_pairs={{0,1},{1,0},{2,3},{3,2},{4,5},{5,4},{6,7},{7,6},{8,9},{9,8},{10,11... | collective-permute-start | bytes 1032200 | tf_op jit(solution)/shard_map/ppermute | solution.py:507
  71.3 6.9 %collective-permute-start.19 = (f32[48,1536]{1,0:T(8,128)S(1)}, f32[48,1536]{1,0:T(8,128)S(1)}, u32[]{:S(2)}, u32[]{:S(2)}) collective-permute-start(f32[48,1536]{1,0:T(8,128)S(1)} %partial_products.5), channel_id=1, source_target_pairs={{0,4},{2,6},{4,0},{6,2},{1,5},{3,7},{5,1},{7,3},{8,12},{10,14},{12... | collective-permute-start | bytes 884744 | tf_op jit(solution)/shard_map/ppermute | solution.py:504
  73.5 12.0 %collective-permute-start.16 = (bf16[48,3712]{1,0:T(8,128)(2,1)S(1)}, bf16[48,3712]{1,0:T(8,128)(2,1)S(1)}, u32[]{:S(2)}, u32[]{:S(2)}) collective-permute-start(bf16[48,3712]{1,0:T(8,128)(2,1)S(1)} %collective-permute-done.8.mine), channel_id=1, source_target_pairs={{0,1},{1,0},{2,3},{3,2},{4,5},{5,4},{6,7},{7,6},{8,9},{9,8},{10,11... | collective-permute-start | bytes 1069064 | tf_op jit(solution)/shard_map/ppermute | solution.py:507
  78.2 7.4 %collective-permute-start.20 = (f32[48,1536]{1,0:T(8,128)S(1)}, f32[48,1536]{1,0:T(8,128)S(1)}, u32[]{:S(2)}, u32[]{:S(2)}) collective-permute-start(f32[48,1536]{1,0:T(8,128)S(1)} %partial_products.7), channel_id=1, source_target_pairs={{0,4},{2,6},{4,0},{6,2},{1,5},{3,7},{5,1},{7,3},{8,12},{10,14},{12... | collective-permute-start | bytes 884744 | tf_op jit(solution)/shard_map/ppermute | solution.py:504

commit v5 on v4

--- a/solution.py
+++ b/solution.py
@@ -581,7 +581,8 @@
         raise ValueError(name)
 
     totals = last(get("c30"), get("p30"), weights(), get("x3"), get("v"), cap)
-    saliency = jnp.abs(lax.psum(totals, "dp"))
+    totals = totals + over_core(totals)
+    saliency = jnp.abs(totals + over_x(totals))
     return saliency, get("k").reshape(1, KEEP * HALF, chunk)
 
 

time: 95 us -> 93.8 us (0.987)
  blocking collectives: 5.67 us -> 0 us
  waiting for transfers between devices: 37.4 us -> 40.9 us
  starting transfers between devices: 23.1 us -> 24.4 us
    psum x1 -> x0, blocking collectives: 5.67 us -> none  [paired_body(): saliency = jnp.abs(lax.psum(totals, 'dp'))]
    ppermute x5 -> x6, waiting for transfers between devices: 3.81 us -> 6.15 us  [over_x(): return lax.ppermute(value, 'dp', [(d, d ^ 2) for d in range(groups)])]
    ppermute x5 -> x6, starting transfers between devices: 6.09 us -> 7.35 us  [over_x(): return lax.ppermute(value, 'dp', [(d, d ^ 2) for d in range(groups)])]
    ppermute x3 -> x4, waiting for transfers between devices: 0.01 us -> 1.16 us  [over_core(): return lax.ppermute(value, 'dp', [(d, d ^ 1) for d in range(groups)])]
  transfers between devices with their start and end apart: 21 -> 23, of which waited for: 7 -> 9; matrix products, arithmetic and copies ran while one was open for 0% -> 0% of each run, Pallas kernels for 22% -> 22%
where the time goes in v5:
time: 93.8 us; the launch traced here: 93.5 us
  waiting for transfers between devices  40.9 us (44%)
  starting transfers between devices  24.4 us (26%)
  Pallas kernels  23.1 us (25%)
  local copies, waits for them, and re-layouts  3.73 us (4%)
    ppermute x6, waiting for transfers between devices, over_expert(): lax.ppermute(value, ('expert', 'dp'), [(e * groups + d, (e ^ bit) * group...  32.5 us
    pallas_call x4, Pallas kernels, products(): pl.pallas_call(functools.partial(products_kernel, cap, width, len(sent),...  10.1 us
    ppermute x6, starting transfers between devices, over_expert(): lax.ppermute(value, ('expert', 'dp'), [(e * groups + d, (e ^ bit) * group...  9.47 us
    ppermute x6, starting transfers between devices, over_x(): return lax.ppermute(value, 'dp', [(d, d ^ 2) for d in range(groups)])  7.35 us
    ppermute x7, starting transfers between devices, over_tensor(): return lax.ppermute(value, 'tensor', [(0, 1), (1, 0)])  6.49 us
    ppermute x6, waiting for transfers between devices, over_x(): return lax.ppermute(value, 'dp', [(d, d ^ 2) for d in range(groups)])  6.15 us
    pallas_call x2, Pallas kernels, last(): pl.pallas_call(functools.partial(last_kernel, cap, width), out_shape=jax....  4.86 us
    unnamed x16, local copies, waits for them, and re-layouts  3.73 us
  transfers between devices with their start and end apart: 23, of which 9 were waited for; matrix products, arithmetic and copies ran while one was open for 0% of the time, Pallas kernels for 22%

profile of v5, /device:TPU:0, one launch (start us, length us, event | category | flops | bytes accessed | tf_op | source)
XLA Modules:
  0.0 93.5 jit_solution(7145036869457136445)
XLA Ops:
  1.7 1.2 %copy-done.3 = bf16[2,32,7168]{2,1,0:T(8,128)(2,1)S(1)} copy-done((bf16[2,32,7168]{2,1,0:T(8,128)(2,1)S(1)}, bf16[2,32,7168]{2,1,0:T(8,128)(2,1)}, u32[]{:S(2)}) %copy-start.3) | copy-done | bytes 917528
  2.9 1.2 %copy-done.4 = bf16[2,32,7168]{2,1,0:T(8,128)(2,1)S(1)} copy-done((bf16[2,32,7168]{2,1,0:T(8,128)(2,1)S(1)}, bf16[2,32,7168]{2,1,0:T(8,128)(2,1)}, u32[]{:S(2)}) %copy-start.4) | copy-done | bytes 917528
  4.0 0.7 copy-done.5
  4.7 0.7 copy-done.6
  5.8 4.7 %collective-permute-start.1 = (bf16[64,3712]{1,0:T(8,128)(2,1)S(1)}, bf16[64,3712]{1,0:T(8,128)(2,1)S(1)}, u32[]{:S(2)}, u32[]{:S(2)}) collective-permute-start(bf16[64,3712]{1,0:T(8,128)(2,1)S(1)} %get-tuple-element.30), channel_id=1, source_target_pairs={{0,20},{2,22},{4,16},{6,18},{8,28},{10,30},{12,24},{14,26},{16,4},... | collective-permute-start | bytes 1425416 | tf_op jit(solution)/shard_map/ppermute | solution.py:510
  10.5 3.4 %pack_rows.1 = (bf16[48,3712]{1,0:T(8,128)(2,1)S(1)}, bf16[48,3584]{1,0:T(8,128)(2,1)S(1)}, bf16[96,3584]{1,0:T(8,128)(2,1)S(1)}, bf16[96,3712]{1,0:T(8,128)(2,1)S(1)}, bf16[3,64,1792]{2,1,0:T(8,128)(2,1)S(1)}) custom-call(s32[2,2,32]{2,1,0:T(2,128)S(1)} %bitcast.31, bf16[2,2,32]{2,1,0:T(2,128)(2,1)S(1)} %bitcast.33, bf16[2,32,7168]{2,1,0:T(8,128)(2,1)S(1)} %copy-done.3, ...), custom_call_target="tpu_custom_call" | custom-call | tf_op jit(solution)/shard_map/pack_rows/pallas_call | solution.py:245
  13.8 1.6 %collective-permute-start.13 = (bf16[3,64,1792]{2,1,0:T(8,128)(2,1)S(1)}, bf16[3,64,1792]{2,1,0:T(8,128)(2,1)S(1)}, u32[]{:S(2)}, u32[]{:S(2)}) collective-permute-start(bf16[3,64,1792]{2,1,0:T(8,128)(2,1)S(1)} %get-tuple-element.44), channel_id=1, source_target_pairs={{0,1},{1,0},{2,3},{3,2},{4,5},{5,4},{6,7},{7,6},{8,9},{9,8},{10,11... | collective-permute-start | bytes 2064392 | tf_op jit(solution)/shard_map/ppermute | solution.py:507
  16.0 2.5 %collective-permute-start.10 = (bf16[48,3584]{1,0:T(8,128)(2,1)S(1)}, bf16[48,3584]{1,0:T(8,128)(2,1)S(1)}, u32[]{:S(2)}, u32[]{:S(2)}) collective-permute-start(bf16[48,3584]{1,0:T(8,128)(2,1)S(1)} %get-tuple-element.41), channel_id=1, source_target_pairs={{0,12},{2,14},{4,8},{6,10},{8,4},{10,6},{12,0},{14,2},{16,28},{18,... | collective-permute-start | bytes 1032200 | tf_op jit(solution)/shard_map/ppermute | solution.py:510
  18.5 13.7 %collective-permute-done.1.raw = bf16[64,3712]{1,0:T(8,128)(2,1)S(1)} collective-permute-done((bf16[64,3712]{1,0:T(8,128)(2,1)S(1)}, bf16[64,3712]{1,0:T(8,128)(2,1)S(1)}, u32[]{:S(2)}, u32[]{:S(2)}) %collective-permute-start.1) | collective-permute-done | bytes 475168 | tf_op jit(solution)/shard_map/ppermute | solution.py:510
  32.9 2.9 %collective-permute-done.10.refs_0_ = bf16[48,3584]{1,0:T(8,128)(2,1)S(1)} collective-permute-done((bf16[48,3584]{1,0:T(8,128)(2,1)S(1)}, bf16[48,3584]{1,0:T(8,128)(2,1)S(1)}, u32[]{:S(2)}, u32[]{:S(2)}) %collective-permute-start.10) | collective-permute-done | bytes 344096 | tf_op jit(solution)/shard_map/ppermute | solution.py:510
  36.2 1.7 %collective-permute-start = (bf16[64,3712]{1,0:T(8,128)(2,1)S(1)}, bf16[64,3712]{1,0:T(8,128)(2,1)S(1)}, u32[]{:S(2)}, u32[]{:S(2)}) collective-permute-start(bf16[64,3712]{1,0:T(8,128)(2,1)S(1)} %get-tuple-element.28), channel_id=1, source_target_pairs={{0,16},{2,18},{4,20},{6,22},{8,24},{10,26},{12,28},{14,30},{16,0},... | collective-permute-start | bytes 1425416 | tf_op jit(solution)/shard_map/ppermute | solution.py:510
  38.9 10.6 %collective-permute-done.12.refs_2_ = bf16[48,3712]{1,0:T(8,128)(2,1)S(1)} collective-permute-done((bf16[48,3712]{1,0:T(8,128)(2,1)S(1)}, bf16[48,3712]{1,0:T(8,128)(2,1)S(1)}, u32[]{:S(2)}, u32[]{:S(2)}) %collective-permute-start.12) | collective-permute-done | bytes 356384 | tf_op jit(solution)/shard_map/ppermute | solution.py:510
  50.0 2.7 %partial_products.4 = (f32[48,1536]{1,0:T(8,128)S(1)}, f32[48,1536]{1,0:T(8,128)S(1)}, f32[48,128]{1,0:T(8,128)S(1)}) custom-call(bf16[96,3584]{1,0:T(8,128)(2,1)S(1)} %collective-permute-done.6.refs_0_, bf16[96,3712]{1,0:T(8,128)(2,1)S(1)} %get-tuple-element.35.refs_1_, bf16[1792,512]{1,0:T(8,128)(2,1)S(1)} %bitcast.17, bf16[1792,512]{1,0:T(8,128)(2,1)S(1)} %bitcast.24, ...), custom_call_target="tpu_custom_call" | custom-call | tf_op jit(solution)/shard_map/partial_products/pallas_call | solution.py:348
  52.8 1.3 %collective-permute-start.7 = (f32[48,1536]{1,0:T(8,128)S(1)}, f32[48,1536]{1,0:T(8,128)S(1)}, u32[]{:S(2)}, u32[]{:S(2)}) collective-permute-start(f32[48,1536]{1,0:T(8,128)S(1)} %get-tuple-element.36), channel_id=1, source_target_pairs={{0,4},{2,6},{4,0},{6,2},{1,5},{3,7},{5,1},{7,3},{8,12},{10,14},{12... | collective-permute-start | bytes 884744 | tf_op jit(solution)/shard_map/ppermute | solution.py:504
  54.0 4.6 %collective-permute-done.raw = bf16[64,3712]{1,0:T(8,128)(2,1)S(1)} collective-permute-done((bf16[64,3712]{1,0:T(8,128)(2,1)S(1)}, bf16[64,3712]{1,0:T(8,128)(2,1)S(1)}, u32[]{:S(2)}, u32[]{:S(2)}) %collective-permute-start) | collective-permute-done | bytes 475168 | tf_op jit(solution)/shard_map/ppermute | solution.py:510
  59.1 1.5 %collective-permute-start.9 = (bf16[48,3712]{1,0:T(8,128)(2,1)S(1)}, bf16[48,3712]{1,0:T(8,128)(2,1)S(1)}, u32[]{:S(2)}, u32[]{:S(2)}) collective-permute-start(bf16[48,3712]{1,0:T(8,128)(2,1)S(1)} %get-tuple-element.38.mine), channel_id=1, source_target_pairs={{0,1},{1,0},{2,3},{3,2},{4,5},{5,4},{6,7},{7,6},{8,9},{9,8},{10,11... | collective-permute-start | bytes 1069064 | tf_op jit(solution)/shard_map/ppermute | solution.py:507
  60.6 2.7 %partial_products.6 = (f32[48,1536]{1,0:T(8,128)S(1)}, f32[48,1536]{1,0:T(8,128)S(1)}, f32[48,128]{1,0:T(8,128)S(1)}) custom-call(bf16[48,3584]{1,0:T(8,128)(2,1)S(1)} %collective-permute-done.10.refs_0_, bf16[48,3584]{1,0:T(8,128)(2,1)S(1)} %collective-permute-done.11.refs_1_, bf16[48,3712]{1,0:T(8,128)(2,1)S(1)} %collective-permute-done.12.refs_2_, ...), custom_call_target="tpu_custom_call" | custom-call | tf_op jit(solution)/shard_map/partial_products/pallas_call | solution.py:348
  63.3 1.6 %collective-permute-start.15 = (f32[48,1536]{1,0:T(8,128)S(1)}, f32[48,1536]{1,0:T(8,128)S(1)}, u32[]{:S(2)}, u32[]{:S(2)}) collective-permute-start(f32[48,1536]{1,0:T(8,128)S(1)} %get-tuple-element.47), channel_id=1, source_target_pairs={{0,4},{2,6},{4,0},{6,2},{1,5},{3,7},{5,1},{7,3},{8,12},{10,14},{12... | collective-permute-start | bytes 884744 | tf_op jit(solution)/shard_map/ppermute | solution.py:504
  64.9 3.4 %kept_rows.1 = bf16[5,64,1792]{2,1,0:T(8,128)(2,1)} custom-call(s32[1,3]{1,0:T(1,128)S(1)} %copy-done.7, bf16[8,64,1792]{2,1,0:T(8,128)(2,1)S(1)} %bitcast.11, bf16[3,64,1792]{2,1,0:T(8,128)(2,1)S(1)} %collective-permute-done.13.came), custom_call_target="tpu_custom_call" | custom-call | tf_op jit(solution)/shard_map/kept_rows/pallas_call | solution.py:482
  68.9 2.4 %partial_products.5 = f32[48,1536]{1,0:T(8,128)S(1)} custom-call(bf16[48,3584]{1,0:T(8,128)(2,1)S(1)} %get-tuple-element.31.refs_0_, bf16[48,3584]{1,0:T(8,128)(2,1)S(1)} %collective-permute-done.2.refs_1_, bf16[1792,512]{1,0:T(8,128)(2,1)S(1)} %bitcast.19, bf16[1792,512]{1,0:T(8,128)(2,1)S(1)} %bitcast.26, bf16[512,1792]{1,0:T(8,128)(2,1)S(1)} %bitcast.12, ...), custom_call_target="tpu_custom_call" | custom-call | tf_op jit(solution)/shard_map/partial_products/pallas_call | solution.py:348
  71.3 1.4 %collective-permute-start.19 = (f32[48,1536]{1,0:T(8,128)S(1)}, f32[48,1536]{1,0:T(8,128)S(1)}, u32[]{:S(2)}, u32[]{:S(2)}) collective-permute-start(f32[48,1536]{1,0:T(8,128)S(1)} %partial_products.5), channel_id=1, source_target_pairs={{0,4},{2,6},{4,0},{6,2},{1,5},{3,7},{5,1},{7,3},{8,12},{10,14},{12... | collective-permute-start | bytes 884744 | tf_op jit(solution)/shard_map/ppermute | solution.py:504
  72.8 0.7 collective-permute-done.8.mine
  73.5 1.2 %collective-permute-start.16 = (bf16[48,3712]{1,0:T(8,128)(2,1)S(1)}, bf16[48,3712]{1,0:T(8,128)(2,1)S(1)}, u32[]{:S(2)}, u32[]{:S(2)}) collective-permute-start(bf16[48,3712]{1,0:T(8,128)(2,1)S(1)} %collective-permute-done.8.mine), channel_id=1, source_target_pairs={{0,1},{1,0},{2,3},{3,2},{4,5},{5,4},{6,7},{7,6},{8,9},{9,8},{10,11... | collective-permute-start | bytes 1069064 | tf_op jit(solution)/shard_map/ppermute | solution.py:507
  74.8 1.1 %collective-permute-done.18.refs_1_ = bf16[48,3584]{1,0:T(8,128)(2,1)S(1)} collective-permute-done((bf16[48,3584]{1,0:T(8,128)(2,1)S(1)}, bf16[48,3584]{1,0:T(8,128)(2,1)S(1)}, u32[]{:S(2)}, u32[]{:S(2)}) %collective-permute-start.18) | collective-permute-done | bytes 344096 | tf_op jit(solution)/shard_map/ppermute | solution.py:507
  75.9 2.3 %partial_products.7 = f32[48,1536]{1,0:T(8,128)S(1)} custom-call(bf16[48,3584]{1,0:T(8,128)(2,1)S(1)} %collective-permute-done.17.refs_0_, bf16[48,3584]{1,0:T(8,128)(2,1)S(1)} %collective-permute-done.18.refs_1_, bf16[1792,512]{1,0:T(8,128)(2,1)S(1)} %bitcast.20, bf16[1792,512]{1,0:T(8,128)(2,1)S(1)} %bitcast.27, bf16[512,1792]{1,0:T(8,128)(2,1)S(1)} %bitcast.13, ...), custom_call_target="tpu_custom_call" | custom-call | tf_op jit(solution)/shard_map/partial_products/pallas_call | solution.py:348
  78.2 1.2 %collective-permute-start.20 = (f32[48,1536]{1,0:T(8,128)S(1)}, f32[48,1536]{1,0:T(8,128)S(1)}, u32[]{:S(2)}, u32[]{:S(2)}) collective-permute-start(f32[48,1536]{1,0:T(8,128)S(1)} %partial_products.7), channel_id=1, source_target_pairs={{0,4},{2,6},{4,0},{6,2},{1,5},{3,7},{5,1},{7,3},{8,12},{10,14},{12... | collective-permute-start | bytes 884744 | tf_op jit(solution)/shard_map/ppermute | solution.py:504
  79.4 2.4 %last_products.2.refs_7_ = f32[2,1,512]{2,1,0:T(1,128)S(1)} custom-call(bf16[48,3712]{1,0:T(8,128)(2,1)S(1)} %get-tuple-element.38.mine, bf16[48,3712]{1,0:T(8,128)(2,1)S(1)} %collective-permute-done.9.other, bf16[1792,512]{1,0:T(8,128)(2,1)S(1)} %bitcast.21, bf16[1792,512]{1,0:T(8,128)(2,1)S(1)} %bitcast.28, bf16[512,1792]{1,0:T(8,128)(2,1)S(1)} %bitcast.14, ...), custom_call_target="tpu_custom_call" | custom-call | tf_op jit(solution)/shard_map/last_products/pallas_call | solution.py:421
  81.8 3.8 %collective-permute-done.20.refs_6_ = f32[48,1536]{1,0:T(8,128)S(1)} collective-permute-done((f32[48,1536]{1,0:T(8,128)S(1)}, f32[48,1536]{1,0:T(8,128)S(1)}, u32[]{:S(2)}, u32[]{:S(2)}) %collective-permute-start.20) | collective-permute-done | bytes 294944 | tf_op jit(solution)/shard_map/ppermute | solution.py:504
  85.6 2.5 %last_products.3 = f32[2,1,512]{2,1,0:T(1,128)S(1)} custom-call(bf16[48,3712]{1,0:T(8,128)(2,1)S(1)} %collective-permute-done.8.mine, bf16[48,3712]{1,0:T(8,128)(2,1)S(1)} %collective-permute-done.16.other, bf16[1792,512]{1,0:T(8,128)(2,1)S(1)} %bitcast.22, bf16[1792,512]{1,0:T(8,128)(2,1)S(1)} %bitcast.29, bf16[512,1792]{1,0:T(8,128)(2,1)S(1)} %bitcast.15, ...), custom_call_target="tpu_custom_call" | custom-call | tf_op jit(solution)/shard_map/last_products/pallas_call | solution.py:421
  88.2 1.2 %collective-permute-done.21 = f32[2,1,512]{2,1,0:T(1,128)S(1)} collective-permute-done((f32[2,1,512]{2,1,0:T(1,128)S(1)}, f32[2,1,512]{2,1,0:T(1,128)S(1)}, u32[]{:S(2)}, u32[]{:S(2)}) %collective-permute-start.21) | collective-permute-done | bytes 4128 | tf_op jit(solution)/shard_map/ppermute | solution.py:501
  89.3 1.3 %collective-permute-start.22 = (f32[2,1,512]{2,1,0:T(1,128)S(1)}, f32[2,1,512]{2,1,0:T(1,128)S(1)}, u32[]{:S(2)}, u32[]{:S(2)}) collective-permute-start(f32[2,1,512]{2,1,0:T(1,128)S(1)} %add.6), channel_id=1, source_target_pairs={{0,4},{2,6},{4,0},{6,2},{1,5},{3,7},{5,1},{7,3},{8,12},{10,14},{12... | collective-permute-start | bytes 12296 | tf_op jit(solution)/shard_map/ppermute | solution.py:504
  90.6 2.3 %collective-permute-done.22 = f32[2,1,512]{2,1,0:T(1,128)S(1)} collective-permute-done((f32[2,1,512]{2,1,0:T(1,128)S(1)}, f32[2,1,512]{2,1,0:T(1,128)S(1)}, u32[]{:S(2)}, u32[]{:S(2)}) %collective-permute-start.22) | collective-permute-done | bytes 4128 | tf_op jit(solution)/shard_map/ppermute | solution.py:504
  (44 shorter events, 6.6 us)
Async XLA Ops:
  0.6 9.8 %copy-start = (bf16[1,512,1792]{2,1,0:T(8,128)(2,1)S(1)}, bf16[1,512,1792]{2,1,0:T(8,128)(2,1)}, u32[]{:S(2)}) copy-start(bf16[1,512,1792]{2,1,0:T(8,128)(2,1)} %param.14) | copy-start | bytes 5505028
  0.6 14.8 %collective-permute-start.3 = (bf16[1792,512]{1,0:T(8,128)(2,1)}, bf16[1792,512]{1,0:T(8,128)(2,1)S(1)}, u32[]{:S(2)}, u32[]{:S(2)}) collective-permute-start(bf16[1792,512]{1,0:T(8,128)(2,1)} %bitcast.16), channel_id=1, source_target_pairs={{0,2},{2,0},{4,6},{6,4},{1,3},{3,1},{5,7},{7,5},{8,10},{10,8},{12,... | collective-permute-start | bytes 5505032 | tf_op jit(solution)/shard_map/ppermute | solution.py:501
  1.2 14.3 %collective-permute-start.4 = (bf16[1792,512]{1,0:T(8,128)(2,1)}, bf16[1792,512]{1,0:T(8,128)(2,1)S(1)}, u32[]{:S(2)}, u32[]{:S(2)}) collective-permute-start(bf16[1792,512]{1,0:T(8,128)(2,1)} %bitcast.23), channel_id=1, source_target_pairs={{0,2},{2,0},{4,6},{6,4},{1,3},{3,1},{5,7},{7,5},{8,10},{10,8},{12,... | collective-permute-start | bytes 5505032 | tf_op jit(solution)/shard_map/ppermute | solution.py:501
  1.2 14.2 %collective-permute-start.5 = (bf16[512,1792]{1,0:T(8,128)(2,1)}, bf16[512,1792]{1,0:T(8,128)(2,1)S(1)}, u32[]{:S(2)}, u32[]{:S(2)}) collective-permute-start(bf16[512,1792]{1,0:T(8,128)(2,1)} %bitcast.7), channel_id=1, source_target_pairs={{0,2},{2,0},{4,6},{6,4},{1,3},{3,1},{5,7},{7,5},{8,10},{10,8},{12,... | collective-permute-start | bytes 5505032 | tf_op jit(solution)/shard_map/ppermute | solution.py:501
  1.7 1.2 %copy-start.3 = (bf16[2,32,7168]{2,1,0:T(8,128)(2,1)S(1)}, bf16[2,32,7168]{2,1,0:T(8,128)(2,1)}, u32[]{:S(2)}) copy-start(bf16[2,32,7168]{2,1,0:T(8,128)(2,1)} %tokens.3) | copy-start | bytes 2752516
  2.9 1.2 %copy-start.4 = (bf16[2,32,7168]{2,1,0:T(8,128)(2,1)S(1)}, bf16[2,32,7168]{2,1,0:T(8,128)(2,1)}, u32[]{:S(2)}) copy-start(bf16[2,32,7168]{2,1,0:T(8,128)(2,1)} %cotangent.3) | copy-start | bytes 2752516
  4.0 0.7 copy-start.5
  4.7 0.7 copy-start.6
  5.4 5.1 %copy-start.7 = (s32[1,3]{1,0:T(1,128)S(1)}, s32[1,3]{1,0:T(1,128)}, u32[]{:S(2)}) copy-start(s32[1,3]{1,0:T(1,128)} %dropped.3) | copy-start | bytes 40
  5.8 26.5 %collective-permute-start.1 = (bf16[64,3712]{1,0:T(8,128)(2,1)S(1)}, bf16[64,3712]{1,0:T(8,128)(2,1)S(1)}, u32[]{:S(2)}, u32[]{:S(2)}) collective-permute-start(bf16[64,3712]{1,0:T(8,128)(2,1)S(1)} %get-tuple-element.30), channel_id=1, source_target_pairs={{0,20},{2,22},{4,16},{6,18},{8,28},{10,30},{12,24},{14,26},{16,4},... | collective-permute-start | bytes 1425416 | tf_op jit(solution)/shard_map/ppermute | solution.py:510
  10.5 39.6 %copy-start.1 = (bf16[1,1792,512]{2,1,0:T(8,128)(2,1)S(1)}, bf16[1,1792,512]{2,1,0:T(8,128)(2,1)}, u32[]{:S(2)}) copy-start(bf16[1,1792,512]{2,1,0:T(8,128)(2,1)} %param.12) | copy-start | bytes 5505028
  10.5 39.6 %copy-start.2 = (bf16[1,1792,512]{2,1,0:T(8,128)(2,1)S(1)}, bf16[1,1792,512]{2,1,0:T(8,128)(2,1)}, u32[]{:S(2)}) copy-start(bf16[1,1792,512]{2,1,0:T(8,128)(2,1)} %param.13) | copy-start | bytes 5505028
  13.8 24.5 %collective-permute-start.13 = (bf16[3,64,1792]{2,1,0:T(8,128)(2,1)S(1)}, bf16[3,64,1792]{2,1,0:T(8,128)(2,1)S(1)}, u32[]{:S(2)}, u32[]{:S(2)}) collective-permute-start(bf16[3,64,1792]{2,1,0:T(8,128)(2,1)S(1)} %get-tuple-element.44), channel_id=1, source_target_pairs={{0,1},{1,0},{2,3},{3,2},{4,5},{5,4},{6,7},{7,6},{8,9},{9,8},{10,11... | collective-permute-start | bytes 2064392 | tf_op jit(solution)/shard_map/ppermute | solution.py:507
  15.4 34.6 %collective-permute-start.6 = (bf16[96,3584]{1,0:T(8,128)(2,1)S(1)}, bf16[96,3584]{1,0:T(8,128)(2,1)S(1)}, u32[]{:S(2)}, u32[]{:S(2)}) collective-permute-start(bf16[96,3584]{1,0:T(8,128)(2,1)S(1)} %get-tuple-element.34), channel_id=1, source_target_pairs={{0,4},{2,6},{4,0},{6,2},{1,5},{3,7},{5,1},{7,3},{8,12},{10,14},{12... | collective-permute-start | bytes 2064392 | tf_op jit(solution)/shard_map/ppermute | solution.py:504
  16.0 19.7 %collective-permute-start.10 = (bf16[48,3584]{1,0:T(8,128)(2,1)S(1)}, bf16[48,3584]{1,0:T(8,128)(2,1)S(1)}, u32[]{:S(2)}, u32[]{:S(2)}) collective-permute-start(bf16[48,3584]{1,0:T(8,128)(2,1)S(1)} %get-tuple-element.41), channel_id=1, source_target_pairs={{0,12},{2,14},{4,8},{6,10},{8,4},{10,6},{12,0},{14,2},{16,28},{18,... | collective-permute-start | bytes 1032200 | tf_op jit(solution)/shard_map/ppermute | solution.py:510
  32.3 17.2 %collective-permute-start.12 = (bf16[48,3712]{1,0:T(8,128)(2,1)S(1)}, bf16[48,3712]{1,0:T(8,128)(2,1)S(1)}, u32[]{:S(2)}, u32[]{:S(2)}) collective-permute-start(bf16[48,3712]{1,0:T(8,128)(2,1)S(1)} %get-tuple-element.43), channel_id=1, source_target_pairs={{0,8},{2,10},{4,12},{6,14},{8,0},{10,2},{12,4},{14,6},{16,24},{18,... | collective-permute-start | bytes 1069064 | tf_op jit(solution)/shard_map/ppermute | solution.py:510
  35.7 18.3 %collective-permute-start.11 = (bf16[48,3584]{1,0:T(8,128)(2,1)S(1)}, bf16[48,3584]{1,0:T(8,128)(2,1)S(1)}, u32[]{:S(2)}, u32[]{:S(2)}) collective-permute-start(bf16[48,3584]{1,0:T(8,128)(2,1)S(1)} %collective-permute-done.10.refs_0_), channel_id=1, source_target_pairs={{0,1},{1,0},{2,3},{3,2},{4,5},{5,4},{6,7},{7,6},{8,9},{9,8},{10,11... | collective-permute-start | bytes 1032200 | tf_op jit(solution)/shard_map/ppermute | solution.py:507
  36.2 22.4 %collective-permute-start = (bf16[64,3712]{1,0:T(8,128)(2,1)S(1)}, bf16[64,3712]{1,0:T(8,128)(2,1)S(1)}, u32[]{:S(2)}, u32[]{:S(2)}) collective-permute-start(bf16[64,3712]{1,0:T(8,128)(2,1)S(1)} %get-tuple-element.28), channel_id=1, source_target_pairs={{0,16},{2,18},{4,20},{6,22},{8,24},{10,26},{12,28},{14,30},{16,0},... | collective-permute-start | bytes 1425416 | tf_op jit(solution)/shard_map/ppermute | solution.py:510
  38.3 22.3 %collective-permute-start.2 = (bf16[48,3584]{1,0:T(8,128)(2,1)S(1)}, bf16[48,3584]{1,0:T(8,128)(2,1)S(1)}, u32[]{:S(2)}, u32[]{:S(2)}) collective-permute-start(bf16[48,3584]{1,0:T(8,128)(2,1)S(1)} %get-tuple-element.31.refs_0_), channel_id=1, source_target_pairs={{0,1},{1,0},{2,3},{3,2},{4,5},{5,4},{6,7},{7,6},{8,9},{9,8},{10,11... | collective-permute-start | bytes 1032200 | tf_op jit(solution)/shard_map/ppermute | solution.py:507
  49.5 11.2 %collective-permute-start.14 = (bf16[48,3712]{1,0:T(8,128)(2,1)S(1)}, bf16[48,3712]{1,0:T(8,128)(2,1)S(1)}, u32[]{:S(2)}, u32[]{:S(2)}) collective-permute-start(bf16[48,3712]{1,0:T(8,128)(2,1)S(1)} %collective-permute-done.12.refs_2_), channel_id=1, source_target_pairs={{0,1},{1,0},{2,3},{3,2},{4,5},{5,4},{6,7},{7,6},{8,9},{9,8},{10,11... | collective-permute-start | bytes 1069064 | tf_op jit(solution)/shard_map/ppermute | solution.py:507
  52.8 7.8 %collective-permute-start.7 = (f32[48,1536]{1,0:T(8,128)S(1)}, f32[48,1536]{1,0:T(8,128)S(1)}, u32[]{:S(2)}, u32[]{:S(2)}) collective-permute-start(f32[48,1536]{1,0:T(8,128)S(1)} %get-tuple-element.36), channel_id=1, source_target_pairs={{0,4},{2,6},{4,0},{6,2},{1,5},{3,7},{5,1},{7,3},{8,12},{10,14},{12... | collective-permute-start | bytes 884744 | tf_op jit(solution)/shard_map/ppermute | solution.py:504
  54.0 14.3 %collective-permute-start.17 = (bf16[48,3584]{1,0:T(8,128)(2,1)S(1)}, bf16[48,3584]{1,0:T(8,128)(2,1)S(1)}, u32[]{:S(2)}, u32[]{:S(2)}) collective-permute-start(bf16[48,3584]{1,0:T(8,128)(2,1)S(1)} %get-tuple-element.51), channel_id=1, source_target_pairs={{0,8},{2,10},{4,12},{6,14},{8,0},{10,2},{12,4},{14,6},{16,24},{18,... | collective-permute-start | bytes 1032200 | tf_op jit(solution)/shard_map/ppermute | solution.py:510
  59.1 13.7 %collective-permute-start.9 = (bf16[48,3712]{1,0:T(8,128)(2,1)S(1)}, bf16[48,3712]{1,0:T(8,128)(2,1)S(1)}, u32[]{:S(2)}, u32[]{:S(2)}) collective-permute-start(bf16[48,3712]{1,0:T(8,128)(2,1)S(1)} %get-tuple-element.38.mine), channel_id=1, source_target_pairs={{0,1},{1,0},{2,3},{3,2},{4,5},{5,4},{6,7},{7,6},{8,9},{9,8},{10,11... | collective-permute-start | bytes 1069064 | tf_op jit(solution)/shard_map/ppermute | solution.py:507
  60.6 12.9 %collective-permute-start.8 = (bf16[48,3712]{1,0:T(8,128)(2,1)S(1)}, bf16[48,3712]{1,0:T(8,128)(2,1)S(1)}, u32[]{:S(2)}, u32[]{:S(2)}) collective-permute-start(bf16[48,3712]{1,0:T(8,128)(2,1)S(1)} %get-tuple-element.37), channel_id=1, source_target_pairs={{0,8},{2,10},{4,12},{6,14},{8,0},{10,2},{12,4},{14,6},{16,24},{18,... | collective-permute-start | bytes 1069064 | tf_op jit(solution)/shard_map/ppermute | solution.py:510
  63.3 9.4 %collective-permute-start.15 = (f32[48,1536]{1,0:T(8,128)S(1)}, f32[48,1536]{1,0:T(8,128)S(1)}, u32[]{:S(2)}, u32[]{:S(2)}) collective-permute-start(f32[48,1536]{1,0:T(8,128)S(1)} %get-tuple-element.47), channel_id=1, source_target_pairs={{0,4},{2,6},{4,0},{6,2},{1,5},{3,7},{5,1},{7,3},{8,12},{10,14},{12... | collective-permute-start | bytes 884744 | tf_op jit(solution)/shard_map/ppermute | solution.py:504
  68.3 7.5 %collective-permute-start.18 = (bf16[48,3584]{1,0:T(8,128)(2,1)S(1)}, bf16[48,3584]{1,0:T(8,128)(2,1)S(1)}, u32[]{:S(2)}, u32[]{:S(2)}) collective-permute-start(bf16[48,3584]{1,0:T(8,128)(2,1)S(1)} %collective-permute-done.17.refs_0_), channel_id=1, source_target_pairs={{0,1},{1,0},{2,3},{3,2},{4,5},{5,4},{6,7},{7,6},{8,9},{9,8},{10,11... | collective-permute-start | bytes 1032200 | tf_op jit(solution)/shard_map/ppermute | solution.py:507
  71.3 6.9 %collective-permute-start.19 = (f32[48,1536]{1,0:T(8,128)S(1)}, f32[48,1536]{1,0:T(8,128)S(1)}, u32[]{:S(2)}, u32[]{:S(2)}) collective-permute-start(f32[48,1536]{1,0:T(8,128)S(1)} %partial_products.5), channel_id=1, source_target_pairs={{0,4},{2,6},{4,0},{6,2},{1,5},{3,7},{5,1},{7,3},{8,12},{10,14},{12... | collective-permute-start | bytes 884744 | tf_op jit(solution)/shard_map/ppermute | solution.py:504
  73.5 12.0 %collective-permute-start.16 = (bf16[48,3712]{1,0:T(8,128)(2,1)S(1)}, bf16[48,3712]{1,0:T(8,128)(2,1)S(1)}, u32[]{:S(2)}, u32[]{:S(2)}) collective-permute-start(bf16[48,3712]{1,0:T(8,128)(2,1)S(1)} %collective-permute-done.8.mine), channel_id=1, source_target_pairs={{0,1},{1,0},{2,3},{3,2},{4,5},{5,4},{6,7},{7,6},{8,9},{9,8},{10,11... | collective-permute-start | bytes 1069064 | tf_op jit(solution)/shard_map/ppermute | solution.py:507
  78.2 7.4 %collective-permute-start.20 = (f32[48,1536]{1,0:T(8,128)S(1)}, f32[48,1536]{1,0:T(8,128)S(1)}, u32[]{:S(2)}, u32[]{:S(2)}) collective-permute-start(f32[48,1536]{1,0:T(8,128)S(1)} %partial_products.7), channel_id=1, source_target_pairs={{0,4},{2,6},{4,0},{6,2},{1,5},{3,7},{5,1},{7,3},{8,12},{10,14},{12... | collective-permute-start | bytes 884744 | tf_op jit(solution)/shard_map/ppermute | solution.py:504
  88.1 1.2 %collective-permute-start.21 = (f32[2,1,512]{2,1,0:T(1,128)S(1)}, f32[2,1,512]{2,1,0:T(1,128)S(1)}, u32[]{:S(2)}, u32[]{:S(2)}) collective-permute-start(f32[2,1,512]{2,1,0:T(1,128)S(1)} %last_products.3), channel_id=1, source_target_pairs={{0,2},{2,0},{4,6},{6,4},{1,3},{3,1},{5,7},{7,5},{8,10},{10,8},{12,... | collective-permute-start | bytes 12296 | tf_op jit(solution)/shard_map/ppermute | solution.py:501
  89.3 3.6 %collective-permute-start.22 = (f32[2,1,512]{2,1,0:T(1,128)S(1)}, f32[2,1,512]{2,1,0:T(1,128)S(1)}, u32[]{:S(2)}, u32[]{:S(2)}) collective-permute-start(f32[2,1,512]{2,1,0:T(1,128)S(1)} %add.6), channel_id=1, source_target_pairs={{0,4},{2,6},{4,0},{6,2},{1,5},{3,7},{5,1},{7,3},{8,12},{10,14},{12... | collective-permute-start | bytes 12296 | tf_op jit(solution)/shard_map/ppermute | solution.py:504

commit v6 on v5

--- a/solution.py
+++ b/solution.py
@@ -24,7 +24,7 @@
     "n": ("w0", "w1", "w2",),
     "p10": ("d",),
     "p30": ("p20", "s2", "t",),
-    "p31": ("k",),
+    "x0": ("k",),
     "x3": ("x2",),
 }
 SMALL = pl.CostEstimate(flops=0, bytes_accessed=0, transcendentals=0)

time: 93.8 us -> 94.3 us (level)
    ppermute x6, waiting for transfers between devices: 6.15 us -> 7.62 us  [over_x(): return lax.ppermute(value, 'dp', [(d, d ^ 2) for d in range(groups)])]
    ppermute x6, waiting for transfers between devices: 32.5 us -> 31.2 us  [over_expert(): lax.ppermute(value, ('expert', 'dp'), [(e * groups + d, (e ^ bit) * group...]
  transfers between devices with their start and end apart: 23 -> 23, of which waited for: 9 -> 10; matrix products, arithmetic and copies ran while one was open for 0% -> 0% of each run, Pallas kernels for 22% -> 22%
where the time goes in v6:
time: 94.3 us; the launch traced here: 94.1 us
  waiting for transfers between devices  41.2 us (44%)
  starting transfers between devices  24.7 us (26%)
  Pallas kernels  23 us (24%)
  local copies, waits for them, and re-layouts  3.74 us (4%)
    ppermute x6, waiting for transfers between devices, over_expert(): lax.ppermute(value, ('expert', 'dp'), [(e * groups + d, (e ^ bit) * group...  31.2 us
    pallas_call x4, Pallas kernels, products(): pl.pallas_call(functools.partial(products_kernel, cap, width, len(sent),...  10 us
    ppermute x6, starting transfers between devices, over_expert(): lax.ppermute(value, ('expert', 'dp'), [(e * groups + d, (e ^ bit) * group...  9.48 us
    ppermute x6, waiting for transfers between devices, over_x(): return lax.ppermute(value, 'dp', [(d, d ^ 2) for d in range(groups)])  7.62 us
    ppermute x7, starting transfers between devices, over_tensor(): return lax.ppermute(value, 'tensor', [(0, 1), (1, 0)])  7.34 us
    ppermute x6, starting transfers between devices, over_x(): return lax.ppermute(value, 'dp', [(d, d ^ 2) for d in range(groups)])  6.79 us
    pallas_call x2, Pallas kernels, last(): pl.pallas_call(functools.partial(last_kernel, cap, width), out_shape=jax....  4.82 us
    unnamed x16, local copies, waits for them, and re-layouts  3.74 us
  transfers between devices with their start and end apart: 23, of which 10 were waited for; matrix products, arithmetic and copies ran while one was open for 0% of the time, Pallas kernels for 22%

profile of v6, /device:TPU:0, one launch (start us, length us, event | category | flops | bytes accessed | tf_op | source)
XLA Modules:
  0.0 94.1 jit_solution(17202403963499519649)
XLA Ops:
  1.7 1.2 %copy-done.3 = bf16[2,32,7168]{2,1,0:T(8,128)(2,1)S(1)} copy-done((bf16[2,32,7168]{2,1,0:T(8,128)(2,1)S(1)}, bf16[2,32,7168]{2,1,0:T(8,128)(2,1)}, u32[]{:S(2)}) %copy-start.3) | copy-done | bytes 917528
  2.9 1.2 %copy-done.4 = bf16[2,32,7168]{2,1,0:T(8,128)(2,1)S(1)} copy-done((bf16[2,32,7168]{2,1,0:T(8,128)(2,1)S(1)}, bf16[2,32,7168]{2,1,0:T(8,128)(2,1)}, u32[]{:S(2)}) %copy-start.4) | copy-done | bytes 917528
  4.0 0.7 copy-done.5
  5.8 4.7 %collective-permute-start.1 = (bf16[64,3712]{1,0:T(8,128)(2,1)S(1)}, bf16[64,3712]{1,0:T(8,128)(2,1)S(1)}, u32[]{:S(2)}, u32[]{:S(2)}) collective-permute-start(bf16[64,3712]{1,0:T(8,128)(2,1)S(1)} %get-tuple-element.30), channel_id=1, source_target_pairs={{0,20},{2,22},{4,16},{6,18},{8,28},{10,30},{12,24},{14,26},{16,4},... | collective-permute-start | bytes 1425416 | tf_op jit(solution)/shard_map/ppermute | solution.py:510
  10.5 3.4 %pack_rows.1 = (bf16[48,3712]{1,0:T(8,128)(2,1)S(1)}, bf16[48,3584]{1,0:T(8,128)(2,1)S(1)}, bf16[96,3584]{1,0:T(8,128)(2,1)S(1)}, bf16[96,3712]{1,0:T(8,128)(2,1)S(1)}, bf16[3,64,1792]{2,1,0:T(8,128)(2,1)S(1)}) custom-call(s32[2,2,32]{2,1,0:T(2,128)S(1)} %bitcast.31, bf16[2,2,32]{2,1,0:T(2,128)(2,1)S(1)} %bitcast.33, bf16[2,32,7168]{2,1,0:T(8,128)(2,1)S(1)} %copy-done.3, ...), custom_call_target="tpu_custom_call" | custom-call | tf_op jit(solution)/shard_map/pack_rows/pallas_call | solution.py:245
  13.8 1.6 %collective-permute-start.7 = (bf16[3,64,1792]{2,1,0:T(8,128)(2,1)S(1)}, bf16[3,64,1792]{2,1,0:T(8,128)(2,1)S(1)}, u32[]{:S(2)}, u32[]{:S(2)}) collective-permute-start(bf16[3,64,1792]{2,1,0:T(8,128)(2,1)S(1)} %get-tuple-element.37), channel_id=1, source_target_pairs={{0,1},{1,0},{2,3},{3,2},{4,5},{5,4},{6,7},{7,6},{8,9},{9,8},{10,11... | collective-permute-start | bytes 2064392 | tf_op jit(solution)/shard_map/ppermute | solution.py:507
  16.0 2.5 %collective-permute-start.11 = (bf16[48,3584]{1,0:T(8,128)(2,1)S(1)}, bf16[48,3584]{1,0:T(8,128)(2,1)S(1)}, u32[]{:S(2)}, u32[]{:S(2)}) collective-permute-start(bf16[48,3584]{1,0:T(8,128)(2,1)S(1)} %get-tuple-element.43), channel_id=1, source_target_pairs={{0,12},{2,14},{4,8},{6,10},{8,4},{10,6},{12,0},{14,2},{16,28},{18,... | collective-permute-start | bytes 1032200 | tf_op jit(solution)/shard_map/ppermute | solution.py:510
  18.5 13.7 %collective-permute-done.1.raw = bf16[64,3712]{1,0:T(8,128)(2,1)S(1)} collective-permute-done((bf16[64,3712]{1,0:T(8,128)(2,1)S(1)}, bf16[64,3712]{1,0:T(8,128)(2,1)S(1)}, u32[]{:S(2)}, u32[]{:S(2)}) %collective-permute-start.1) | collective-permute-done | bytes 475168 | tf_op jit(solution)/shard_map/ppermute | solution.py:510
  32.9 2.8 %collective-permute-done.11.refs_0_ = bf16[48,3584]{1,0:T(8,128)(2,1)S(1)} collective-permute-done((bf16[48,3584]{1,0:T(8,128)(2,1)S(1)}, bf16[48,3584]{1,0:T(8,128)(2,1)S(1)}, u32[]{:S(2)}, u32[]{:S(2)}) %collective-permute-start.11) | collective-permute-done | bytes 344096 | tf_op jit(solution)/shard_map/ppermute | solution.py:510
  36.2 1.7 %collective-permute-start = (bf16[64,3712]{1,0:T(8,128)(2,1)S(1)}, bf16[64,3712]{1,0:T(8,128)(2,1)S(1)}, u32[]{:S(2)}, u32[]{:S(2)}) collective-permute-start(bf16[64,3712]{1,0:T(8,128)(2,1)S(1)} %get-tuple-element.28), channel_id=1, source_target_pairs={{0,16},{2,18},{4,20},{6,22},{8,24},{10,26},{12,28},{14,30},{16,0},... | collective-permute-start | bytes 1425416 | tf_op jit(solution)/shard_map/ppermute | solution.py:510
  38.9 3.4 %kept_rows.1 = bf16[5,64,1792]{2,1,0:T(8,128)(2,1)} custom-call(s32[1,3]{1,0:T(1,128)S(1)} %copy-done.7, bf16[8,64,1792]{2,1,0:T(8,128)(2,1)S(1)} %bitcast.9, bf16[3,64,1792]{2,1,0:T(8,128)(2,1)S(1)} %collective-permute-done.7.came), custom_call_target="tpu_custom_call" | custom-call | tf_op jit(solution)/shard_map/kept_rows/pallas_call | solution.py:482
  42.3 7.1 %collective-permute-done.13.refs_2_ = bf16[48,3712]{1,0:T(8,128)(2,1)S(1)} collective-permute-done((bf16[48,3712]{1,0:T(8,128)(2,1)S(1)}, bf16[48,3712]{1,0:T(8,128)(2,1)S(1)}, u32[]{:S(2)}, u32[]{:S(2)}) %collective-permute-start.13) | collective-permute-done | bytes 356384 | tf_op jit(solution)/shard_map/ppermute | solution.py:510
  50.0 2.7 %partial_products.4 = (f32[48,1536]{1,0:T(8,128)S(1)}, f32[48,1536]{1,0:T(8,128)S(1)}, f32[48,128]{1,0:T(8,128)S(1)}) custom-call(bf16[96,3584]{1,0:T(8,128)(2,1)S(1)} %collective-permute-done.6.refs_0_, bf16[96,3712]{1,0:T(8,128)(2,1)S(1)} %get-tuple-element.35.refs_1_, bf16[1792,512]{1,0:T(8,128)(2,1)S(1)} %bitcast.17, bf16[1792,512]{1,0:T(8,128)(2,1)S(1)} %bitcast.24, ...), custom_call_target="tpu_custom_call" | custom-call | tf_op jit(solution)/shard_map/partial_products/pallas_call | solution.py:348
  52.8 1.3 %collective-permute-start.8 = (f32[48,1536]{1,0:T(8,128)S(1)}, f32[48,1536]{1,0:T(8,128)S(1)}, u32[]{:S(2)}, u32[]{:S(2)}) collective-permute-start(f32[48,1536]{1,0:T(8,128)S(1)} %get-tuple-element.38), channel_id=1, source_target_pairs={{0,4},{2,6},{4,0},{6,2},{1,5},{3,7},{5,1},{7,3},{8,12},{10,14},{12... | collective-permute-start | bytes 884744 | tf_op jit(solution)/shard_map/ppermute | solution.py:504
  54.0 4.6 %collective-permute-done.raw = bf16[64,3712]{1,0:T(8,128)(2,1)S(1)} collective-permute-done((bf16[64,3712]{1,0:T(8,128)(2,1)S(1)}, bf16[64,3712]{1,0:T(8,128)(2,1)S(1)}, u32[]{:S(2)}, u32[]{:S(2)}) %collective-permute-start) | collective-permute-done | bytes 475168 | tf_op jit(solution)/shard_map/ppermute | solution.py:510
  59.1 1.5 %collective-permute-start.10 = (bf16[48,3712]{1,0:T(8,128)(2,1)S(1)}, bf16[48,3712]{1,0:T(8,128)(2,1)S(1)}, u32[]{:S(2)}, u32[]{:S(2)}) collective-permute-start(bf16[48,3712]{1,0:T(8,128)(2,1)S(1)} %get-tuple-element.40.mine), channel_id=1, source_target_pairs={{0,1},{1,0},{2,3},{3,2},{4,5},{5,4},{6,7},{7,6},{8,9},{9,8},{10,11... | collective-permute-start | bytes 1069064 | tf_op jit(solution)/shard_map/ppermute | solution.py:507
  60.6 2.7 %partial_products.6 = (f32[48,1536]{1,0:T(8,128)S(1)}, f32[48,1536]{1,0:T(8,128)S(1)}, f32[48,128]{1,0:T(8,128)S(1)}) custom-call(bf16[48,3584]{1,0:T(8,128)(2,1)S(1)} %collective-permute-done.11.refs_0_, bf16[48,3584]{1,0:T(8,128)(2,1)S(1)} %collective-permute-done.12.refs_1_, bf16[48,3712]{1,0:T(8,128)(2,1)S(1)} %collective-permute-done.13.refs_2_, ...), custom_call_target="tpu_custom_call" | custom-call | tf_op jit(solution)/shard_map/partial_products/pallas_call | solution.py:348
  63.3 1.7 %collective-permute-start.15 = (f32[48,1536]{1,0:T(8,128)S(1)}, f32[48,1536]{1,0:T(8,128)S(1)}, u32[]{:S(2)}, u32[]{:S(2)}) collective-permute-start(f32[48,1536]{1,0:T(8,128)S(1)} %get-tuple-element.48), channel_id=1, source_target_pairs={{0,4},{2,6},{4,0},{6,2},{1,5},{3,7},{5,1},{7,3},{8,12},{10,14},{12... | collective-permute-start | bytes 884744 | tf_op jit(solution)/shard_map/ppermute | solution.py:504
  65.0 1.0 %collective-permute-done.17.refs_0_ = bf16[48,3584]{1,0:T(8,128)(2,1)S(1)} collective-permute-done((bf16[48,3584]{1,0:T(8,128)(2,1)S(1)}, bf16[48,3584]{1,0:T(8,128)(2,1)S(1)}, u32[]{:S(2)}, u32[]{:S(2)}) %collective-permute-start.17) | collective-permute-done | bytes 344096 | tf_op jit(solution)/shard_map/ppermute | solution.py:510
  66.0 1.4 %collective-permute-start.18 = (bf16[48,3584]{1,0:T(8,128)(2,1)S(1)}, bf16[48,3584]{1,0:T(8,128)(2,1)S(1)}, u32[]{:S(2)}, u32[]{:S(2)}) collective-permute-start(bf16[48,3584]{1,0:T(8,128)(2,1)S(1)} %collective-permute-done.17.refs_0_), channel_id=1, source_target_pairs={{0,1},{1,0},{2,3},{3,2},{4,5},{5,4},{6,7},{7,6},{8,9},{9,8},{10,11... | collective-permute-start | bytes 1032200 | tf_op jit(solution)/shard_map/ppermute | solution.py:507
  67.4 2.3 %partial_products.5 = f32[48,1536]{1,0:T(8,128)S(1)} custom-call(bf16[48,3584]{1,0:T(8,128)(2,1)S(1)} %get-tuple-element.31.refs_0_, bf16[48,3584]{1,0:T(8,128)(2,1)S(1)} %collective-permute-done.2.refs_1_, bf16[1792,512]{1,0:T(8,128)(2,1)S(1)} %bitcast.19, bf16[1792,512]{1,0:T(8,128)(2,1)S(1)} %bitcast.26, bf16[512,1792]{1,0:T(8,128)(2,1)S(1)} %bitcast.12, ...), custom_call_target="tpu_custom_call" | custom-call | tf_op jit(solution)/shard_map/partial_products/pallas_call | solution.py:348
  69.8 1.7 %collective-permute-start.19 = (f32[48,1536]{1,0:T(8,128)S(1)}, f32[48,1536]{1,0:T(8,128)S(1)}, u32[]{:S(2)}, u32[]{:S(2)}) collective-permute-start(f32[48,1536]{1,0:T(8,128)S(1)} %partial_products.5), channel_id=1, source_target_pairs={{0,4},{2,6},{4,0},{6,2},{1,5},{3,7},{5,1},{7,3},{8,12},{10,14},{12... | collective-permute-start | bytes 884744 | tf_op jit(solution)/shard_map/ppermute | solution.py:504
  71.6 1.9 %collective-permute-done.9.mine = bf16[48,3712]{1,0:T(8,128)(2,1)S(1)} collective-permute-done((bf16[48,3712]{1,0:T(8,128)(2,1)S(1)}, bf16[48,3712]{1,0:T(8,128)(2,1)S(1)}, u32[]{:S(2)}, u32[]{:S(2)}) %collective-permute-start.9) | collective-permute-done | bytes 356384 | tf_op jit(solution)/shard_map/ppermute | solution.py:510
  73.5 1.2 %collective-permute-start.16 = (bf16[48,3712]{1,0:T(8,128)(2,1)S(1)}, bf16[48,3712]{1,0:T(8,128)(2,1)S(1)}, u32[]{:S(2)}, u32[]{:S(2)}) collective-permute-start(bf16[48,3712]{1,0:T(8,128)(2,1)S(1)} %collective-permute-done.9.mine), channel_id=1, source_target_pairs={{0,1},{1,0},{2,3},{3,2},{4,5},{5,4},{6,7},{7,6},{8,9},{9,8},{10,11... | collective-permute-start | bytes 1069064 | tf_op jit(solution)/shard_map/ppermute | solution.py:507
  74.7 1.1 %collective-permute-done.18.refs_1_ = bf16[48,3584]{1,0:T(8,128)(2,1)S(1)} collective-permute-done((bf16[48,3584]{1,0:T(8,128)(2,1)S(1)}, bf16[48,3584]{1,0:T(8,128)(2,1)S(1)}, u32[]{:S(2)}, u32[]{:S(2)}) %collective-permute-start.18) | collective-permute-done | bytes 344096 | tf_op jit(solution)/shard_map/ppermute | solution.py:507
  75.9 2.3 %partial_products.7 = f32[48,1536]{1,0:T(8,128)S(1)} custom-call(bf16[48,3584]{1,0:T(8,128)(2,1)S(1)} %collective-permute-done.17.refs_0_, bf16[48,3584]{1,0:T(8,128)(2,1)S(1)} %collective-permute-done.18.refs_1_, bf16[1792,512]{1,0:T(8,128)(2,1)S(1)} %bitcast.20, bf16[1792,512]{1,0:T(8,128)(2,1)S(1)} %bitcast.27, bf16[512,1792]{1,0:T(8,128)(2,1)S(1)} %bitcast.13, ...), custom_call_target="tpu_custom_call" | custom-call | tf_op jit(solution)/shard_map/partial_products/pallas_call | solution.py:348
  78.2 1.0 %collective-permute-start.20 = (f32[48,1536]{1,0:T(8,128)S(1)}, f32[48,1536]{1,0:T(8,128)S(1)}, u32[]{:S(2)}, u32[]{:S(2)}) collective-permute-start(f32[48,1536]{1,0:T(8,128)S(1)} %partial_products.7), channel_id=1, source_target_pairs={{0,4},{2,6},{4,0},{6,2},{1,5},{3,7},{5,1},{7,3},{8,12},{10,14},{12... | collective-permute-start | bytes 884744 | tf_op jit(solution)/shard_map/ppermute | solution.py:504
  79.2 2.5 %last_products.2.refs_7_ = f32[2,1,512]{2,1,0:T(1,128)S(1)} custom-call(bf16[48,3712]{1,0:T(8,128)(2,1)S(1)} %get-tuple-element.40.mine, bf16[48,3712]{1,0:T(8,128)(2,1)S(1)} %collective-permute-done.10.other, bf16[1792,512]{1,0:T(8,128)(2,1)S(1)} %bitcast.21, bf16[1792,512]{1,0:T(8,128)(2,1)S(1)} %bitcast.28, bf16[512,1792]{1,0:T(8,128)(2,1)S(1)} %bitcast.14, ...), custom_call_target="tpu_custom_call" | custom-call | tf_op jit(solution)/shard_map/last_products/pallas_call | solution.py:421
  81.7 4.6 %collective-permute-done.20.refs_6_ = f32[48,1536]{1,0:T(8,128)S(1)} collective-permute-done((f32[48,1536]{1,0:T(8,128)S(1)}, f32[48,1536]{1,0:T(8,128)S(1)}, u32[]{:S(2)}, u32[]{:S(2)}) %collective-permute-start.20) | collective-permute-done | bytes 294944 | tf_op jit(solution)/shard_map/ppermute | solution.py:504
  86.2 2.3 %last_products.3 = f32[2,1,512]{2,1,0:T(1,128)S(1)} custom-call(bf16[48,3712]{1,0:T(8,128)(2,1)S(1)} %collective-permute-done.9.mine, bf16[48,3712]{1,0:T(8,128)(2,1)S(1)} %collective-permute-done.16.other, bf16[1792,512]{1,0:T(8,128)(2,1)S(1)} %bitcast.22, bf16[1792,512]{1,0:T(8,128)(2,1)S(1)} %bitcast.29, bf16[512,1792]{1,0:T(8,128)(2,1)S(1)} %bitcast.15, ...), custom_call_target="tpu_custom_call" | custom-call | tf_op jit(solution)/shard_map/last_products/pallas_call | solution.py:421
  88.7 1.2 %collective-permute-done.21 = f32[2,1,512]{2,1,0:T(1,128)S(1)} collective-permute-done((f32[2,1,512]{2,1,0:T(1,128)S(1)}, f32[2,1,512]{2,1,0:T(1,128)S(1)}, u32[]{:S(2)}, u32[]{:S(2)}) %collective-permute-start.21) | collective-permute-done | bytes 4128 | tf_op jit(solution)/shard_map/ppermute | solution.py:501
  90.4 3.0 %collective-permute-done.22 = f32[2,1,512]{2,1,0:T(1,128)S(1)} collective-permute-done((f32[2,1,512]{2,1,0:T(1,128)S(1)}, f32[2,1,512]{2,1,0:T(1,128)S(1)}, u32[]{:S(2)}, u32[]{:S(2)}) %collective-permute-start.22) | collective-permute-done | bytes 4128 | tf_op jit(solution)/shard_map/ppermute | solution.py:504
  (44 shorter events, 7.3 us)
Async XLA Ops:
  0.6 9.8 %copy-start = (bf16[1,512,1792]{2,1,0:T(8,128)(2,1)S(1)}, bf16[1,512,1792]{2,1,0:T(8,128)(2,1)}, u32[]{:S(2)}) copy-start(bf16[1,512,1792]{2,1,0:T(8,128)(2,1)} %param.14) | copy-start | bytes 5505028
  0.6 14.8 %collective-permute-start.3 = (bf16[1792,512]{1,0:T(8,128)(2,1)}, bf16[1792,512]{1,0:T(8,128)(2,1)S(1)}, u32[]{:S(2)}, u32[]{:S(2)}) collective-permute-start(bf16[1792,512]{1,0:T(8,128)(2,1)} %bitcast.16), channel_id=1, source_target_pairs={{0,2},{2,0},{4,6},{6,4},{1,3},{3,1},{5,7},{7,5},{8,10},{10,8},{12,... | collective-permute-start | bytes 5505032 | tf_op jit(solution)/shard_map/ppermute | solution.py:501
  1.2 14.3 %collective-permute-start.4 = (bf16[1792,512]{1,0:T(8,128)(2,1)}, bf16[1792,512]{1,0:T(8,128)(2,1)S(1)}, u32[]{:S(2)}, u32[]{:S(2)}) collective-permute-start(bf16[1792,512]{1,0:T(8,128)(2,1)} %bitcast.23), channel_id=1, source_target_pairs={{0,2},{2,0},{4,6},{6,4},{1,3},{3,1},{5,7},{7,5},{8,10},{10,8},{12,... | collective-permute-start | bytes 5505032 | tf_op jit(solution)/shard_map/ppermute | solution.py:501
  1.2 14.2 %collective-permute-start.5 = (bf16[512,1792]{1,0:T(8,128)(2,1)}, bf16[512,1792]{1,0:T(8,128)(2,1)S(1)}, u32[]{:S(2)}, u32[]{:S(2)}) collective-permute-start(bf16[512,1792]{1,0:T(8,128)(2,1)} %bitcast.7), channel_id=1, source_target_pairs={{0,2},{2,0},{4,6},{6,4},{1,3},{3,1},{5,7},{7,5},{8,10},{10,8},{12,... | collective-permute-start | bytes 5505032 | tf_op jit(solution)/shard_map/ppermute | solution.py:501
  1.7 1.2 %copy-start.3 = (bf16[2,32,7168]{2,1,0:T(8,128)(2,1)S(1)}, bf16[2,32,7168]{2,1,0:T(8,128)(2,1)}, u32[]{:S(2)}) copy-start(bf16[2,32,7168]{2,1,0:T(8,128)(2,1)} %tokens.3) | copy-start | bytes 2752516
  2.9 1.2 %copy-start.4 = (bf16[2,32,7168]{2,1,0:T(8,128)(2,1)S(1)}, bf16[2,32,7168]{2,1,0:T(8,128)(2,1)}, u32[]{:S(2)}) copy-start(bf16[2,32,7168]{2,1,0:T(8,128)(2,1)} %cotangent.3) | copy-start | bytes 2752516
  4.0 0.7 copy-start.5
  4.7 0.7 copy-start.6
  5.4 5.1 %copy-start.7 = (s32[1,3]{1,0:T(1,128)S(1)}, s32[1,3]{1,0:T(1,128)}, u32[]{:S(2)}) copy-start(s32[1,3]{1,0:T(1,128)} %dropped.3) | copy-start | bytes 40
  5.8 26.5 %collective-permute-start.1 = (bf16[64,3712]{1,0:T(8,128)(2,1)S(1)}, bf16[64,3712]{1,0:T(8,128)(2,1)S(1)}, u32[]{:S(2)}, u32[]{:S(2)}) collective-permute-start(bf16[64,3712]{1,0:T(8,128)(2,1)S(1)} %get-tuple-element.30), channel_id=1, source_target_pairs={{0,20},{2,22},{4,16},{6,18},{8,28},{10,30},{12,24},{14,26},{16,4},... | collective-permute-start | bytes 1425416 | tf_op jit(solution)/shard_map/ppermute | solution.py:510
  13.8 24.5 %collective-permute-start.7 = (bf16[3,64,1792]{2,1,0:T(8,128)(2,1)S(1)}, bf16[3,64,1792]{2,1,0:T(8,128)(2,1)S(1)}, u32[]{:S(2)}, u32[]{:S(2)}) collective-permute-start(bf16[3,64,1792]{2,1,0:T(8,128)(2,1)S(1)} %get-tuple-element.37), channel_id=1, source_target_pairs={{0,1},{1,0},{2,3},{3,2},{4,5},{5,4},{6,7},{7,6},{8,9},{9,8},{10,11... | collective-permute-start | bytes 2064392 | tf_op jit(solution)/shard_map/ppermute | solution.py:507
  15.4 34.6 %collective-permute-start.6 = (bf16[96,3584]{1,0:T(8,128)(2,1)S(1)}, bf16[96,3584]{1,0:T(8,128)(2,1)S(1)}, u32[]{:S(2)}, u32[]{:S(2)}) collective-permute-start(bf16[96,3584]{1,0:T(8,128)(2,1)S(1)} %get-tuple-element.34), channel_id=1, source_target_pairs={{0,4},{2,6},{4,0},{6,2},{1,5},{3,7},{5,1},{7,3},{8,12},{10,14},{12... | collective-permute-start | bytes 2064392 | tf_op jit(solution)/shard_map/ppermute | solution.py:504
  16.0 19.7 %collective-permute-start.11 = (bf16[48,3584]{1,0:T(8,128)(2,1)S(1)}, bf16[48,3584]{1,0:T(8,128)(2,1)S(1)}, u32[]{:S(2)}, u32[]{:S(2)}) collective-permute-start(bf16[48,3584]{1,0:T(8,128)(2,1)S(1)} %get-tuple-element.43), channel_id=1, source_target_pairs={{0,12},{2,14},{4,8},{6,10},{8,4},{10,6},{12,0},{14,2},{16,28},{18,... | collective-permute-start | bytes 1032200 | tf_op jit(solution)/shard_map/ppermute | solution.py:510
  32.3 17.2 %collective-permute-start.13 = (bf16[48,3712]{1,0:T(8,128)(2,1)S(1)}, bf16[48,3712]{1,0:T(8,128)(2,1)S(1)}, u32[]{:S(2)}, u32[]{:S(2)}) collective-permute-start(bf16[48,3712]{1,0:T(8,128)(2,1)S(1)} %get-tuple-element.45), channel_id=1, source_target_pairs={{0,8},{2,10},{4,12},{6,14},{8,0},{10,2},{12,4},{14,6},{16,24},{18,... | collective-permute-start | bytes 1069064 | tf_op jit(solution)/shard_map/ppermute | solution.py:510
  35.7 18.3 %collective-permute-start.12 = (bf16[48,3584]{1,0:T(8,128)(2,1)S(1)}, bf16[48,3584]{1,0:T(8,128)(2,1)S(1)}, u32[]{:S(2)}, u32[]{:S(2)}) collective-permute-start(bf16[48,3584]{1,0:T(8,128)(2,1)S(1)} %collective-permute-done.11.refs_0_), channel_id=1, source_target_pairs={{0,1},{1,0},{2,3},{3,2},{4,5},{5,4},{6,7},{7,6},{8,9},{9,8},{10,11... | collective-permute-start | bytes 1032200 | tf_op jit(solution)/shard_map/ppermute | solution.py:507
  36.2 22.4 %collective-permute-start = (bf16[64,3712]{1,0:T(8,128)(2,1)S(1)}, bf16[64,3712]{1,0:T(8,128)(2,1)S(1)}, u32[]{:S(2)}, u32[]{:S(2)}) collective-permute-start(bf16[64,3712]{1,0:T(8,128)(2,1)S(1)} %get-tuple-element.28), channel_id=1, source_target_pairs={{0,16},{2,18},{4,20},{6,22},{8,24},{10,26},{12,28},{14,30},{16,0},... | collective-permute-start | bytes 1425416 | tf_op jit(solution)/shard_map/ppermute | solution.py:510
  38.3 11.7 %copy-start.1 = (bf16[1,1792,512]{2,1,0:T(8,128)(2,1)S(1)}, bf16[1,1792,512]{2,1,0:T(8,128)(2,1)}, u32[]{:S(2)}) copy-start(bf16[1,1792,512]{2,1,0:T(8,128)(2,1)} %param.12) | copy-start | bytes 5505028
  38.3 11.7 %copy-start.2 = (bf16[1,1792,512]{2,1,0:T(8,128)(2,1)S(1)}, bf16[1,1792,512]{2,1,0:T(8,128)(2,1)}, u32[]{:S(2)}) copy-start(bf16[1,1792,512]{2,1,0:T(8,128)(2,1)} %param.13) | copy-start | bytes 5505028
  38.3 22.2 %collective-permute-start.2 = (bf16[48,3584]{1,0:T(8,128)(2,1)S(1)}, bf16[48,3584]{1,0:T(8,128)(2,1)S(1)}, u32[]{:S(2)}, u32[]{:S(2)}) collective-permute-start(bf16[48,3584]{1,0:T(8,128)(2,1)S(1)} %get-tuple-element.31.refs_0_), channel_id=1, source_target_pairs={{0,1},{1,0},{2,3},{3,2},{4,5},{5,4},{6,7},{7,6},{8,9},{9,8},{10,11... | collective-permute-start | bytes 1032200 | tf_op jit(solution)/shard_map/ppermute | solution.py:507
  49.4 11.1 %collective-permute-start.14 = (bf16[48,3712]{1,0:T(8,128)(2,1)S(1)}, bf16[48,3712]{1,0:T(8,128)(2,1)S(1)}, u32[]{:S(2)}, u32[]{:S(2)}) collective-permute-start(bf16[48,3712]{1,0:T(8,128)(2,1)S(1)} %collective-permute-done.13.refs_2_), channel_id=1, source_target_pairs={{0,1},{1,0},{2,3},{3,2},{4,5},{5,4},{6,7},{7,6},{8,9},{9,8},{10,11... | collective-permute-start | bytes 1069064 | tf_op jit(solution)/shard_map/ppermute | solution.py:507
  52.8 7.8 %collective-permute-start.8 = (f32[48,1536]{1,0:T(8,128)S(1)}, f32[48,1536]{1,0:T(8,128)S(1)}, u32[]{:S(2)}, u32[]{:S(2)}) collective-permute-start(f32[48,1536]{1,0:T(8,128)S(1)} %get-tuple-element.38), channel_id=1, source_target_pairs={{0,4},{2,6},{4,0},{6,2},{1,5},{3,7},{5,1},{7,3},{8,12},{10,14},{12... | collective-permute-start | bytes 884744 | tf_op jit(solution)/shard_map/ppermute | solution.py:504
  54.0 12.0 %collective-permute-start.17 = (bf16[48,3584]{1,0:T(8,128)(2,1)S(1)}, bf16[48,3584]{1,0:T(8,128)(2,1)S(1)}, u32[]{:S(2)}, u32[]{:S(2)}) collective-permute-start(bf16[48,3584]{1,0:T(8,128)(2,1)S(1)} %get-tuple-element.52), channel_id=1, source_target_pairs={{0,8},{2,10},{4,12},{6,14},{8,0},{10,2},{12,4},{14,6},{16,24},{18,... | collective-permute-start | bytes 1032200 | tf_op jit(solution)/shard_map/ppermute | solution.py:510
  59.1 12.5 %collective-permute-start.10 = (bf16[48,3712]{1,0:T(8,128)(2,1)S(1)}, bf16[48,3712]{1,0:T(8,128)(2,1)S(1)}, u32[]{:S(2)}, u32[]{:S(2)}) collective-permute-start(bf16[48,3712]{1,0:T(8,128)(2,1)S(1)} %get-tuple-element.40.mine), channel_id=1, source_target_pairs={{0,1},{1,0},{2,3},{3,2},{4,5},{5,4},{6,7},{7,6},{8,9},{9,8},{10,11... | collective-permute-start | bytes 1069064 | tf_op jit(solution)/shard_map/ppermute | solution.py:507
  60.6 12.9 %collective-permute-start.9 = (bf16[48,3712]{1,0:T(8,128)(2,1)S(1)}, bf16[48,3712]{1,0:T(8,128)(2,1)S(1)}, u32[]{:S(2)}, u32[]{:S(2)}) collective-permute-start(bf16[48,3712]{1,0:T(8,128)(2,1)S(1)} %get-tuple-element.39), channel_id=1, source_target_pairs={{0,8},{2,10},{4,12},{6,14},{8,0},{10,2},{12,4},{14,6},{16,24},{18,... | collective-permute-start | bytes 1069064 | tf_op jit(solution)/shard_map/ppermute | solution.py:510
  63.3 8.2 %collective-permute-start.15 = (f32[48,1536]{1,0:T(8,128)S(1)}, f32[48,1536]{1,0:T(8,128)S(1)}, u32[]{:S(2)}, u32[]{:S(2)}) collective-permute-start(f32[48,1536]{1,0:T(8,128)S(1)} %get-tuple-element.48), channel_id=1, source_target_pairs={{0,4},{2,6},{4,0},{6,2},{1,5},{3,7},{5,1},{7,3},{8,12},{10,14},{12... | collective-permute-start | bytes 884744 | tf_op jit(solution)/shard_map/ppermute | solution.py:504
  66.0 9.9 %collective-permute-start.18 = (bf16[48,3584]{1,0:T(8,128)(2,1)S(1)}, bf16[48,3584]{1,0:T(8,128)(2,1)S(1)}, u32[]{:S(2)}, u32[]{:S(2)}) collective-permute-start(bf16[48,3584]{1,0:T(8,128)(2,1)S(1)} %collective-permute-done.17.refs_0_), channel_id=1, source_target_pairs={{0,1},{1,0},{2,3},{3,2},{4,5},{5,4},{6,7},{7,6},{8,9},{9,8},{10,11... | collective-permute-start | bytes 1032200 | tf_op jit(solution)/shard_map/ppermute | solution.py:507
  69.8 8.4 %collective-permute-start.19 = (f32[48,1536]{1,0:T(8,128)S(1)}, f32[48,1536]{1,0:T(8,128)S(1)}, u32[]{:S(2)}, u32[]{:S(2)}) collective-permute-start(f32[48,1536]{1,0:T(8,128)S(1)} %partial_products.5), channel_id=1, source_target_pairs={{0,4},{2,6},{4,0},{6,2},{1,5},{3,7},{5,1},{7,3},{8,12},{10,14},{12... | collective-permute-start | bytes 884744 | tf_op jit(solution)/shard_map/ppermute | solution.py:504
  73.5 12.7 %collective-permute-start.16 = (bf16[48,3712]{1,0:T(8,128)(2,1)S(1)}, bf16[48,3712]{1,0:T(8,128)(2,1)S(1)}, u32[]{:S(2)}, u32[]{:S(2)}) collective-permute-start(bf16[48,3712]{1,0:T(8,128)(2,1)S(1)} %collective-permute-done.9.mine), channel_id=1, source_target_pairs={{0,1},{1,0},{2,3},{3,2},{4,5},{5,4},{6,7},{7,6},{8,9},{9,8},{10,11... | collective-permute-start | bytes 1069064 | tf_op jit(solution)/shard_map/ppermute | solution.py:507
  78.2 8.0 %collective-permute-start.20 = (f32[48,1536]{1,0:T(8,128)S(1)}, f32[48,1536]{1,0:T(8,128)S(1)}, u32[]{:S(2)}, u32[]{:S(2)}) collective-permute-start(f32[48,1536]{1,0:T(8,128)S(1)} %partial_products.7), channel_id=1, source_target_pairs={{0,4},{2,6},{4,0},{6,2},{1,5},{3,7},{5,1},{7,3},{8,12},{10,14},{12... | collective-permute-start | bytes 884744 | tf_op jit(solution)/shard_map/ppermute | solution.py:504
  88.6 1.2 %collective-permute-start.21 = (f32[2,1,512]{2,1,0:T(1,128)S(1)}, f32[2,1,512]{2,1,0:T(1,128)S(1)}, u32[]{:S(2)}, u32[]{:S(2)}) collective-permute-start(f32[2,1,512]{2,1,0:T(1,128)S(1)} %last_products.3), channel_id=1, source_target_pairs={{0,2},{2,0},{4,6},{6,4},{1,3},{3,1},{5,7},{7,5},{8,10},{10,8},{12,... | collective-permute-start | bytes 12296 | tf_op jit(solution)/shard_map/ppermute | solution.py:501
  89.8 3.6 %collective-permute-start.22 = (f32[2,1,512]{2,1,0:T(1,128)S(1)}, f32[2,1,512]{2,1,0:T(1,128)S(1)}, u32[]{:S(2)}, u32[]{:S(2)}) collective-permute-start(f32[2,1,512]{2,1,0:T(1,128)S(1)} %add.6), channel_id=1, source_target_pairs={{0,4},{2,6},{4,0},{6,2},{1,5},{3,7},{5,1},{7,3},{8,12},{10,14},{12... | collective-permute-start | bytes 12296 | tf_op jit(solution)/shard_map/ppermute | solution.py:504
